TPU v7x, 32 devices: a whole 2x2x4 slice. The times are simulated.
32 devices in a mesh: fsdp: 32 (over z, y, x, core).
Axes of the slice: x: 2, y: 2, z: 4, core: 2. Of those that a mesh axis runs over, the one named last changes fastest.
Arguments:
- tokens: bfloat16 [32768, 1024], P('fsdp'), may hold values from -6 to 6
- image_ids: int32 [32768], P('fsdp'), may hold values from 0 to 57, as said below
- cotangent: bfloat16 [32768, 1024], P('fsdp'), may hold values from -6 to 6
- norm1_gain: bfloat16 [1024], P('fsdp'), may hold values from 0.099609375 to 1.8984375
- norm1_shift: bfloat16 [1024], P('fsdp'), may hold values from -1.5 to 1.5
- qkv_weight: bfloat16 [1024, 3072], P('fsdp'), may hold values from -0.1875 to 0.1875
- query_bias: bfloat16 [1024], P('fsdp'), may hold values from -2.5 to 2.5
- value_bias: bfloat16 [1024], P('fsdp'), may hold values from -1 to 1
- out_weight: bfloat16 [1024, 1024], P('fsdp'), may hold values from -1.5 to 1.5
- out_bias: bfloat16 [1024], P('fsdp'), may hold values from -1 to 1
- norm2_gain: bfloat16 [1024], P('fsdp'), may hold values from 0.099609375 to 1.8984375
- norm2_shift: bfloat16 [1024], P('fsdp'), may hold values from -1.5 to 1.5
- up_weight: bfloat16 [1024, 4096], P('fsdp'), may hold values from -0.1875 to 0.1875
- up_bias: bfloat16 [4096], P('fsdp'), may hold values from -2.5 to 2.5
- down_weight: bfloat16 [4096, 1024], P('fsdp'), may hold values from -0.1875 to 0.1875
- down_bias: bfloat16 [1024], P('fsdp'), may hold values from -1 to 1
Outputs:
- layer_out: bfloat16 [32768, 1024], P('fsdp')
- grad_tokens: float32 [32768, 1024], P('fsdp')
- grad_norm1_gain: float32 [1024], P('fsdp')
- grad_norm1_shift: float32 [1024], P('fsdp')
- grad_qkv_weight: float32 [1024, 3072], P('fsdp')
- grad_query_bias: float32 [1024], P('fsdp')
- grad_value_bias: float32 [1024], P('fsdp')
- grad_out_weight: float32 [1024, 1024], P('fsdp')
- grad_out_bias: float32 [1024], P('fsdp')
- grad_norm2_gain: float32 [1024], P('fsdp')
- grad_norm2_shift: float32 [1024], P('fsdp')
- grad_up_weight: float32 [1024, 4096], P('fsdp')
- grad_up_bias: float32 [4096], P('fsdp')
- grad_down_weight: float32 [4096, 1024], P('fsdp')
- grad_down_bias: float32 [1024], P('fsdp')
Inputs may be any that keep to these rules, and one draw needn't show every extreme that they name: `image_ids`: image numbers never fall along the tokens and rise by one from image to image; every image has 577 tokens except the first and the last, which have 1 to 577.
All inputs are finite; a program needn't handle non-finite values.
Results may differ from a plain program's by a relative error of at most 0.013.
Values may be sent and summed in bfloat16 or wider, within the bound.
A program may use at most 256 MiB of HBM per device.

v0:
```python
import math

import jax
import jax.numpy as jnp
from jax import lax
from jax.sharding import PartitionSpec as P

HDIM = 64
IMG = 577


EPS = 1e-06


def extended(block, sides, width):
    for axis, dim in sides:
        count = lax.axis_size(axis)
        forward = [(i, i + 1) for i in range(count - 1)]
        backward = [(target, source) for source, target in forward]
        low = lax.ppermute(
            lax.slice_in_dim(block, block.shape[dim] - width, None, axis=dim), axis, forward
        )
        high = lax.ppermute(lax.slice_in_dim(block, 0, width, axis=dim), axis, backward)
        block = jnp.concatenate([low, block, high], axis=dim)
    return block


def from_behind(value, axis, by):
    peers = lax.axis_size(axis)
    pairs = [(i, i + by) for i in range(peers) if 0 <= i + by < peers]
    return lax.ppermute(value, axis, pairs)


def normalize(inputs, gain, shift):
    center = inputs - jnp.mean(inputs, axis=1, keepdims=True)
    inv_std = lax.rsqrt(jnp.mean(center * center, axis=1, keepdims=True) + EPS)
    scaled = center * inv_std
    return (scaled * gain + shift, scaled, inv_std)


def normalize_back(upstream, scaled, inv_std, gain):
    through = upstream * gain
    inner = (
        through
        - jnp.mean(through, axis=1, keepdims=True)
        - scaled * jnp.mean(through * scaled, axis=1, keepdims=True)
    )
    return (inv_std * inner, jnp.sum(upstream * scaled, axis=0), jnp.sum(upstream, axis=0))


def local(
    tokens,
    image_ids,
    cotangent,
    norm1_gain,
    norm1_shift,
    qkv_weight,
    query_bias,
    value_bias,
    out_weight,
    out_bias,
    norm2_gain,
    norm2_shift,
    up_weight,
    up_bias,
    down_weight,
    down_bias,
):
    tok_rows, model_width = tokens.shape
    head_count = model_width // HDIM
    pair_cols = 2 * HDIM
    pair_count = head_count // 2
    block_rows = min(512, tok_rows)
    block_count = tok_rows // block_rows
    piece_count = block_count * pair_count
    rim_rows = IMG - 1
    window_rows = block_rows + 2 * rim_rows
    score_scale = 1.0 / math.sqrt(HDIM)
    params = (
        lax.all_gather(norm1_gain, "fsdp", axis=0, tiled=True),
        lax.all_gather(norm1_shift, "fsdp", axis=0, tiled=True),
        lax.all_gather(qkv_weight, "fsdp", axis=0, tiled=True),
        lax.all_gather(query_bias, "fsdp", axis=0, tiled=True),
        lax.all_gather(value_bias, "fsdp", axis=0, tiled=True),
        lax.all_gather(out_weight, "fsdp", axis=0, tiled=True),
        lax.all_gather(out_bias, "fsdp", axis=0, tiled=True),
        lax.all_gather(norm2_gain, "fsdp", axis=0, tiled=True),
        lax.all_gather(norm2_shift, "fsdp", axis=0, tiled=True),
        lax.all_gather(up_weight, "fsdp", axis=0, tiled=True),
        lax.all_gather(up_bias, "fsdp", axis=0, tiled=True),
        lax.all_gather(down_weight, "fsdp", axis=0, tiled=True),
        lax.all_gather(down_bias, "fsdp", axis=0, tiled=True),
    )
    inputs = tokens.astype(jnp.float32)
    normed, scaled_one, inv_one = normalize(
        inputs, params[0].astype(jnp.float32), params[1].astype(jnp.float32)
    )
    normed_low = normed.astype(jnp.bfloat16)
    bias_row = jnp.concatenate(
        [
            params[3].astype(jnp.float32),
            jnp.zeros((model_width,), jnp.float32),
            params[4].astype(jnp.float32),
        ]
    )
    projected = (
        jnp.dot(normed_low, params[2], preferred_element_type=jnp.float32) + bias_row
    ).astype(jnp.bfloat16)
    queries = projected[:, :model_width]
    key_value = projected[:, model_width:]
    tags = (image_ids % 128 + 1).astype(jnp.bfloat16)
    near_pairs, near_tags = (
        extended(key_value, (("fsdp", 0),), rim_rows),
        extended(tags, (("fsdp", 0),), rim_rows),
    )

    def piece_inputs(piece_idx):
        row_start = piece_idx // pair_count * block_rows
        col_start = piece_idx % pair_count * pair_cols
        query_block = lax.dynamic_slice(
            queries, (row_start, col_start), (block_rows, pair_cols)
        ).reshape(block_rows, 2, HDIM)
        key_block = lax.dynamic_slice(
            near_pairs, (row_start, col_start), (window_rows, pair_cols)
        ).reshape(window_rows, 2, HDIM)
        value_block = lax.dynamic_slice(
            near_pairs, (row_start, model_width + col_start), (window_rows, pair_cols)
        ).reshape(window_rows, 2, HDIM)
        own_tags = lax.dynamic_slice_in_dim(tags, row_start, block_rows, 0)
        window_tags = lax.dynamic_slice_in_dim(near_tags, row_start, window_rows, 0)
        same_image = own_tags[:, None] == window_tags[None, :]
        logits = (
            jnp.einsum("qhd,khd->hqk", query_block, key_block, preferred_element_type=jnp.float32)
            * score_scale
        )
        logits = jnp.where(same_image[None], logits, -1e30)
        return (row_start, col_start, query_block, key_block, value_block, logits)

    def attend_piece(piece_idx):
        row_start, col_start, query_block, key_block, value_block, logits = piece_inputs(piece_idx)
        row_max = jnp.max(logits, axis=2, keepdims=True)
        exp_terms = jnp.exp(logits - row_max)
        row_total = jnp.sum(exp_terms, axis=2, keepdims=True)
        prob_block = (exp_terms / row_total).astype(jnp.bfloat16)
        mixed_piece = jnp.einsum(
            "hqk,khd->qhd", prob_block, value_block, preferred_element_type=jnp.float32
        )
        return (mixed_piece.reshape(block_rows, pair_cols), (row_max + jnp.log(row_total))[:, :, 0])

    def assemble(pieces):
        return (
            pieces.reshape(block_count, pair_count, block_rows, pair_cols)
            .transpose(0, 2, 1, 3)
            .reshape(tok_rows, model_width)
        )

    mixed_pieces, log_totals = lax.map(attend_piece, jnp.arange(piece_count, dtype=jnp.int32))
    mixed_low = assemble(mixed_pieces).astype(jnp.bfloat16)
    branch = jnp.dot(mixed_low, params[5], preferred_element_type=jnp.float32) + params[6].astype(
        jnp.float32
    )
    resid = inputs + branch
    normed_two, scaled_two, inv_two = normalize(
        resid, params[7].astype(jnp.float32), params[8].astype(jnp.float32)
    )
    normed_two_low = normed_two.astype(jnp.bfloat16)
    upward = jnp.dot(normed_two_low, params[9], preferred_element_type=jnp.float32) + params[
        10
    ].astype(jnp.float32)
    activated_low = jax.nn.gelu(upward, approximate=False).astype(jnp.bfloat16)
    down_out = jnp.dot(activated_low, params[11], preferred_element_type=jnp.float32) + params[
        12
    ].astype(jnp.float32)
    layer_out = (resid + down_out).astype(jnp.bfloat16)
    back_gain_one, back_qkv, back_out, back_gain_two, back_up, back_down = (
        lax.all_gather(norm1_gain, "fsdp", axis=0, tiled=True),
        lax.all_gather(qkv_weight, "fsdp", axis=0, tiled=True),
        lax.all_gather(out_weight, "fsdp", axis=0, tiled=True),
        lax.all_gather(norm2_gain, "fsdp", axis=0, tiled=True),
        lax.all_gather(up_weight, "fsdp", axis=0, tiled=True),
        lax.all_gather(down_weight, "fsdp", axis=0, tiled=True),
    )
    upstream_out = cotangent.astype(jnp.float32)
    grad_down = jnp.einsum(
        "tf,td->fd", activated_low, cotangent, preferred_element_type=jnp.float32
    )
    grad_down_b = jnp.sum(upstream_out, axis=0)
    dactive = jnp.einsum("td,fd->tf", cotangent, back_down, preferred_element_type=jnp.float32)
    normal_cdf = 0.5 * (1.0 + jax.scipy.special.erf(upward * (1.0 / math.sqrt(2.0))))
    normal_pdf = jnp.exp(-0.5 * upward * upward) * (1.0 / math.sqrt(2.0 * math.pi))
    dupward_low = (dactive * (normal_cdf + upward * normal_pdf)).astype(jnp.bfloat16)
    grad_up = jnp.einsum(
        "td,tf->df", normed_two_low, dupward_low, preferred_element_type=jnp.float32
    )
    grad_up_b = jnp.sum(dupward_low.astype(jnp.float32), axis=0)
    dnormed_two = jnp.einsum("tf,df->td", dupward_low, back_up, preferred_element_type=jnp.float32)
    dresid_norm, grad_gain_two, grad_shift_two = normalize_back(
        dnormed_two, scaled_two, inv_two, back_gain_two.astype(jnp.float32)
    )
    dresid = upstream_out + dresid_norm
    dbranch_low = dresid.astype(jnp.bfloat16)
    grad_out = jnp.einsum("td,te->de", mixed_low, dbranch_low, preferred_element_type=jnp.float32)
    grad_out_b = jnp.sum(dbranch_low.astype(jnp.float32), axis=0)
    dmixed_low = jnp.einsum(
        "te,de->td", dbranch_low, back_out, preferred_element_type=jnp.float32
    ).astype(jnp.bfloat16)

    def back_piece(running, piece_idx):
        dkey_ext, dvalue_ext = running
        row_start, col_start, query_block, key_block, value_block, logits = piece_inputs(piece_idx)
        prob_block = jnp.exp(logits - log_totals[piece_idx][:, :, None])
        upstream = lax.dynamic_slice(
            dmixed_low, (row_start, col_start), (block_rows, pair_cols)
        ).reshape(block_rows, 2, HDIM)
        dprobs = jnp.einsum(
            "qhd,khd->hqk", upstream, value_block, preferred_element_type=jnp.float32
        )
        row_dot = jnp.sum(prob_block * dprobs, axis=2, keepdims=True)
        dlogits_low = (prob_block * (dprobs - row_dot)).astype(jnp.bfloat16)
        dquery = (
            jnp.einsum("hqk,khd->qhd", dlogits_low, key_block, preferred_element_type=jnp.float32)
            * score_scale
        )
        dkey = (
            jnp.einsum("hqk,qhd->khd", dlogits_low, query_block, preferred_element_type=jnp.float32)
            * score_scale
        )
        dvalue = jnp.einsum(
            "hqk,qhd->khd",
            prob_block.astype(jnp.bfloat16),
            upstream,
            preferred_element_type=jnp.float32,
        )
        key_old = lax.dynamic_slice(dkey_ext, (row_start, col_start), (window_rows, pair_cols))
        dkey_ext = lax.dynamic_update_slice(
            dkey_ext, key_old + dkey.reshape(window_rows, pair_cols), (row_start, col_start)
        )
        value_old = lax.dynamic_slice(dvalue_ext, (row_start, col_start), (window_rows, pair_cols))
        dvalue_ext = lax.dynamic_update_slice(
            dvalue_ext, value_old + dvalue.reshape(window_rows, pair_cols), (row_start, col_start)
        )
        return ((dkey_ext, dvalue_ext), dquery.reshape(block_rows, pair_cols))

    ext_rows = tok_rows + 2 * rim_rows
    zero_ext = jnp.zeros((ext_rows, model_width), jnp.float32)
    (dkey_ext, dvalue_ext), dquery_pieces = lax.scan(
        back_piece, (zero_ext, zero_ext), jnp.arange(piece_count, dtype=jnp.int32)
    )
    lower_rim = jnp.concatenate([dkey_ext[:rim_rows], dvalue_ext[:rim_rows]], axis=1)
    upper_rim = jnp.concatenate(
        [dkey_ext[rim_rows + tok_rows :], dvalue_ext[rim_rows + tok_rows :]], axis=1
    )
    from_after = from_behind(lower_rim.astype(jnp.bfloat16), "fsdp", -1).astype(lower_rim.dtype)
    from_before = from_behind(upper_rim.astype(jnp.bfloat16), "fsdp", 1).astype(upper_rim.dtype)
    own_grads = jnp.concatenate(
        [dkey_ext[rim_rows : rim_rows + tok_rows], dvalue_ext[rim_rows : rim_rows + tok_rows]],
        axis=1,
    )
    own_grads = own_grads.at[:rim_rows].add(from_before).at[tok_rows - rim_rows :].add(from_after)
    dkv_low = own_grads.astype(jnp.bfloat16)
    dquery_low = assemble(dquery_pieces).astype(jnp.bfloat16)
    dproj_low = jnp.concatenate([dquery_low, dkv_low], axis=1)
    grad_qkv = jnp.einsum("td,te->de", normed_low, dproj_low, preferred_element_type=jnp.float32)
    grad_query_b = jnp.sum(dquery_low.astype(jnp.float32), axis=0)
    grad_value_b = jnp.sum(dkv_low[:, model_width:].astype(jnp.float32), axis=0)
    dnormed = jnp.einsum("te,de->td", dproj_low, back_qkv, preferred_element_type=jnp.float32)
    dinput_norm, grad_gain_one, grad_shift_one = normalize_back(
        dnormed, scaled_one, inv_one, back_gain_one.astype(jnp.float32)
    )
    grad_tokens = dresid + dinput_norm
    owned = (
        lax.psum_scatter(grad_gain_one, "fsdp", scatter_dimension=0, tiled=True),
        lax.psum_scatter(grad_shift_one, "fsdp", scatter_dimension=0, tiled=True),
        lax.psum_scatter(grad_qkv, "fsdp", scatter_dimension=0, tiled=True),
        lax.psum_scatter(grad_query_b, "fsdp", scatter_dimension=0, tiled=True),
        lax.psum_scatter(grad_value_b, "fsdp", scatter_dimension=0, tiled=True),
        lax.psum_scatter(grad_out, "fsdp", scatter_dimension=0, tiled=True),
        lax.psum_scatter(grad_out_b, "fsdp", scatter_dimension=0, tiled=True),
        lax.psum_scatter(grad_gain_two, "fsdp", scatter_dimension=0, tiled=True),
        lax.psum_scatter(grad_shift_two, "fsdp", scatter_dimension=0, tiled=True),
        lax.psum_scatter(grad_up, "fsdp", scatter_dimension=0, tiled=True),
        lax.psum_scatter(grad_up_b, "fsdp", scatter_dimension=0, tiled=True),
        lax.psum_scatter(grad_down, "fsdp", scatter_dimension=0, tiled=True),
        lax.psum_scatter(grad_down_b, "fsdp", scatter_dimension=0, tiled=True),
    )
    return (
        layer_out,
        grad_tokens,
        owned[0],
        owned[1],
        owned[2],
        owned[3],
        owned[4],
        owned[5],
        owned[6],
        owned[7],
        owned[8],
        owned[9],
        owned[10],
        owned[11],
        owned[12],
    )


def solution(mesh):
    placed = (
        P("fsdp", None),
        P("fsdp"),
        P("fsdp", None),
        P("fsdp"),
        P("fsdp"),
        P("fsdp", None),
        P("fsdp"),
        P("fsdp"),
        P("fsdp", None),
        P("fsdp"),
        P("fsdp"),
        P("fsdp"),
        P("fsdp", None),
        P("fsdp"),
        P("fsdp", None),
        P("fsdp"),
    )
    return jax.shard_map(
        local,
        mesh=mesh,
        in_specs=placed,
        out_specs=(
            P("fsdp", None),
            P("fsdp", None),
            P("fsdp"),
            P("fsdp"),
            P("fsdp", None),
            P("fsdp"),
            P("fsdp"),
            P("fsdp", None),
            P("fsdp"),
            P("fsdp"),
            P("fsdp"),
            P("fsdp", None),
            P("fsdp"),
            P("fsdp", None),
            P("fsdp"),
        ),
        check_vma=False,
    )
```

profile of v0, /device:TPU:0, one launch (start us, length us, event | category | flops | bytes accessed | tf_op | source)
XLA Modules:
  0.0 2121.3 jit_solution(2547552513867533343)
XLA Ops:
  16.2 42.5 %all-reduce.18 = (bf16[1024]{0:T(1024)(128)(2,1)S(1)}, bf16[1024]{0:T(1024)(128)(2,1)S(1)}, bf16[1024]{0:T(1024)(128)(2,1)S(1)}, bf16[1024]{0:T(1024)(128)(2,1)S...) all-reduce(bf16[1024]{0:T(1024)(128)(2,1)S(1)} %dynamic-update-slic, ...), channel_id=1, replica_groups=mesh['fsdp'=32] {'fsdp'}, use_global_device_ids=true, to_apply=%add.4 | all-reduce | flops 8192 | bytes 32768
  62.9 20.3 all-gather.6.cloned.1.call-done
  83.2 10.3 add_convert_fusion
  107.1 82.9 %all-gather = bf16[32,1,128]{2,1,0:T(2,128)(2,1)S(1)} all-gather(bf16[1,1,128]{2,1,0:T(2,128)(2,1)S(1)} %bitcast.156), channel_id=1, replica_groups=mesh['fsdp'=32] {'fsdp'}, dimensions={0}, use_global_device_ids=true | all-gather | bytes 8448 | tf_op jit(solution)/shard_map/all_gather | solution.py:90
  206.0 7.4 pad_maximum_fusion.1
  213.5 11.8 copy.83
  226.8 241.4 %while.32 = (s32[]{:T(128)}, bf16[16,512,128]{1,2,0:T(8,128)(2,1)}, f32[16,2,512]{2,1,0:T(2,128)}, s32[16]{0:T(128)S(1)}, bf16[2176,2048]{0,1:T(8,128)(2,1)}, /*...) while((s32[]{:T(128)}, bf16[16,512,128]{1,2,0:T(8,128)(2,1)}, ...), condition=%wide.region_5.6_spmd, body=%wide.region_2.5_spmd.sunk | while | flops 457505824 | bytes 27244868 | solution.py:157
  480.2 47.4 %fusion.9 = (bf16[1024,4096]{1,0:T(8,128)(2,1)}, f32[1024,4096]{1,0:T(8,128)}) fusion(f32[4096]{0:T(1024)S(1)} %bitcast.154, bf16[1024,4096]{1,0:T(8,128)(2,1)} %all-gather.10.cloned.1.call-done, bf16[1024,1024]{0,1:T(8,128)(2,1)S(1)} %add_convert_fusion.4.clone.4), kind=kOutput, calls=%fused_computation.27 | convolution fusion | flops 8866758656 | bytes 35667968 | tf_op jit(solution)/shard_map/dot_general | solution.py:167
  527.6 18.8 convert_reduce_fusion
  546.4 11.2 fusion.70
  597.3 907.0 %while.33 = (s32[]{:T(128)}, f32[2176,1024]{1,0:T(8,128)}, f32[2176,1024]{1,0:T(8,128)}, bf16[16,512,128]{1,2,0:T(8,128)(2,1)}, s32[16]{0:T(128)S(1)}, /*index=5...) while((s32[]{:T(128)}, f32[2176,1024]{1,0:T(8,128)}, ...), condition=%wide.region_12.13_spmd, body=%wide.region_10.12_spmd.sunk | while | flops 1107475456 | bytes 141559856 | solution.py:246
  645.8 6.3 dynamic_update_slice.44
  874.0 6.3 dynamic_update_slice.44
  987.9 6.3 dynamic_update_slice.44
  1547.8 10.1 fusion.41
  1558.6 16.6 fusion.60
  1575.3 16.4 fusion.72
  1592.4 16.2 add_convert_fusion.1
  1614.7 12.8 fusion.69
  1638.4 67.6 %all-reduce.17 = (f32[1024]{0:T(1024)S(1)}, f32[1024]{0:T(1024)S(1)}, f32[1024]{0:T(1024)S(1)}, f32[1024]{0:T(1024)S(1)}, f32[1024]{0:T(1024)S(1)}, /*index=5*/f...) all-reduce(f32[1024]{0:T(1024)S(1)} %get-tuple-element.431, ...), channel_id=2, replica_groups=mesh['fsdp'=32] {'fsdp'}, use_global_device_ids=true, to_apply=%region_16.17.clone | all-reduce | flops 12288 | bytes 98304
  1710.8 6.9 fusion.38
  1723.7 18.1 reduce-scatter.5.cloned.1.call-done
  1741.8 184.8 %reduce-scatter.9.cloned.1.call-done = f32[32,4096]{1,0:T(8,128)} async-done(((f32[1024,4096]{1,0:T(8,128)}), f32[32,4096]{1,0:T(8,128)}) %reduce-scatter.9.cloned.1.call-update) | async-done | bytes 524304 | tf_op jit(solution)/shard_map/reduce_scatter | solution.py:281
  1926.6 187.6 %reduce-scatter.11.cloned.1.call-done = f32[128,1024]{1,0:T(8,128)} async-done(((f32[4096,1024]{1,0:T(8,128)}), f32[128,1024]{1,0:T(8,128)}) %reduce-scatter.11.cloned.1.call-update) | async-done | bytes 524304 | tf_op jit(solution)/shard_map/reduce_scatter | solution.py:283
  (1014 shorter events, 1189.5 us)
Async XLA Ops:
  7.2 76.0 %all-gather.6.cloned.1.call-start = ((), (), s32[]{:S(2)}) async-start(), calls=%async_computation.4 | async-start | bytes 6488064 | tf_op jit(solution)/shard_map/all_gather | solution.py:82
  7.9 464.6 %all-gather.8.cloned.1.call-start = ((), (), s32[]{:S(2)}) async-start(), calls=%async_computation.5 | async-start | bytes 2162688 | tf_op jit(solution)/shard_map/all_gather | solution.py:85
  8.7 471.6 %all-gather.10.cloned.1.call-start = ((), (), s32[]{:S(2)}) async-start(), calls=%async_computation.6 | async-start | bytes 8650752 | tf_op jit(solution)/shard_map/all_gather | solution.py:89
  9.4 518.2 %all-gather.12.cloned.1.call-start = ((), (), s32[]{:S(2)}) async-start(), calls=%async_computation.7 | async-start | bytes 8650752 | tf_op jit(solution)/shard_map/all_gather | solution.py:91
  58.7 24.5 %copy-start.32 = (f32[1024]{0:T(1024)}, f32[1024]{0:T(1024)S(1)}, u32[]{:S(2)}) copy-start(f32[1024]{0:T(1024)S(1)} %convert_element_type.134) | copy-start | bytes 12292
  58.7 24.5 %copy-start.44 = (f32[1024]{0:T(1024)}, f32[1024]{0:T(1024)S(1)}, u32[]{:S(2)}) copy-start(f32[1024]{0:T(1024)S(1)} %convert_element_type.135) | copy-start | bytes 12292
  61.8 410.6 %copy-start.6 = (bf16[1024,1024]{0,1:T(8,128)(2,1)}, bf16[1024,1024]{0,1:T(8,128)(2,1)S(1)}, u32[]{:S(2)}) copy-start(bf16[1024,1024]{0,1:T(8,128)(2,1)S(1)} %copy.82) | copy-start | bytes 6291460
  62.2 31.3 %copy-start.30 = (f32[1024]{0:T(1024)}, f32[1024]{0:T(1024)S(1)}, u32[]{:S(2)}) copy-start(f32[1024]{0:T(1024)S(1)} %broadcast_multiply_fusion.5) | copy-start | bytes 12292
  62.9 30.7 %copy-start.34 = (f32[1024]{0:T(1024)}, f32[1024]{0:T(1024)S(1)}, u32[]{:S(2)}) copy-start(f32[1024]{0:T(1024)S(1)} %add_rsqrt_fusion.1) | copy-start | bytes 12292
  97.8 108.3 %collective-permute-start = (bf16[576,2048]{1,0:T(8,128)(2,1)}, bf16[576,2048]{1,0:T(8,128)(2,1)}, u32[]{:S(2)}, u32[]{:S(2)}) collective-permute-start(bf16[576,2048]{1,0:T(8,128)(2,1)} %get-tuple-element.500), channel_id=1, source_target_pairs={{0,1},{1,2},{2,3},{3,4},{4,5},{5,6},{6,7},{7,8},{8,9},{9,10},{10,1... | collective-permute-start | bytes 7077896 | tf_op jit(solution)/shard_map/ppermute | solution.py:20
  101.3 104.7 %collective-permute-start.1 = (bf16[576,2048]{1,0:T(8,128)(2,1)}, bf16[576,2048]{1,0:T(8,128)(2,1)}, u32[]{:S(2)}, u32[]{:S(2)}) collective-permute-start(bf16[576,2048]{1,0:T(8,128)(2,1)} %get-tuple-element.501), channel_id=1, source_target_pairs={{1,0},{2,1},{3,2},{4,3},{5,4},{6,5},{7,6},{8,7},{9,8},{10,9},{11,1... | collective-permute-start | bytes 7077896 | tf_op jit(solution)/shard_map/ppermute | solution.py:23
  102.7 91.4 %collective-permute-start.2 = (bf16[576]{0:T(1024)(128)(2,1)S(1)}, bf16[576]{0:T(1024)(128)(2,1)S(1)}, u32[]{:S(2)}, u32[]{:S(2)}) collective-permute-start(bf16[576]{0:T(1024)(128)(2,1)S(1)} %get-tuple-element.508), channel_id=1, source_target_pairs={{0,1},{1,2},{2,3},{3,4},{4,5},{5,6},{6,7},{7,8},{8,9},{9,10},{10,1... | collective-permute-start | bytes 3464 | tf_op jit(solution)/shard_map/ppermute | solution.py:20
  105.8 88.3 %collective-permute-start.3 = (bf16[576]{0:T(1024)(128)(2,1)S(1)}, bf16[576]{0:T(1024)(128)(2,1)S(1)}, u32[]{:S(2)}, u32[]{:S(2)}) collective-permute-start(bf16[576]{0:T(1024)(128)(2,1)S(1)} %get-tuple-element.507), channel_id=1, source_target_pairs={{1,0},{2,1},{3,2},{4,3},{5,4},{6,5},{7,6},{8,7},{9,8},{10,9},{11,1... | collective-permute-start | bytes 3464 | tf_op jit(solution)/shard_map/ppermute | solution.py:23
  107.1 1616.6 %reduce-scatter.7.cloned.1.call-start = ((), (), s32[]{:S(2)}) async-start(), calls=%async_computation.9 | async-start | bytes 4325376 | tf_op jit(solution)/shard_map/reduce_scatter | solution.py:277
  190.0 288.0 %copy-start.24 = (f32[1024]{0:T(1024)}, f32[1024]{0:T(1024)S(1)}, u32[]{:S(2)}) copy-start(f32[1024]{0:T(1024)S(1)} %convert_element_type.146) | copy-start | bytes 12292
  190.0 288.0 %copy-start.39 = (f32[1024]{0:T(1024)}, f32[1024]{0:T(1024)S(1)}, u32[]{:S(2)}) copy-start(f32[1024]{0:T(1024)S(1)} %convert_element_type.147) | copy-start | bytes 12292
  479.5 48.1 %copy-start.27 = (f32[1024]{0:T(1024)}, f32[1024]{0:T(1024)S(1)}, u32[]{:S(2)}) copy-start(f32[1024]{0:T(1024)S(1)} %add_rsqrt_fusion) | copy-start | bytes 12292
  527.6 18.8 copy-start.48
  579.0 1162.8 %reduce-scatter.5.cloned.1.call-start = ((), (), s32[]{:S(2)}) async-start(), calls=%async_computation.8 | async-start | bytes 12976128 | tf_op jit(solution)/shard_map/reduce_scatter | solution.py:274
  638.4 13.7 copy-start.1
  1513.2 24.8 %collective-permute-start.4 = (bf16[576,2048]{1,0:T(8,128)(2,1)}, bf16[576,2048]{1,0:T(8,128)(2,1)}, u32[]{:S(2)}, u32[]{:S(2)}) collective-permute-start(bf16[576,2048]{1,0:T(8,128)(2,1)} %pad_maximum_fusion.5), channel_id=1, source_target_pairs={{0,1},{1,2},{2,3},{3,4},{4,5},{5,6},{6,7},{7,8},{8,9},{9,10},{10,1... | collective-permute-start | bytes 7077896 | tf_op jit(solution)/shard_map/ppermute | solution.py:31
  1518.4 22.8 %collective-permute-start.5 = (bf16[576,2048]{1,0:T(8,128)(2,1)}, bf16[576,2048]{1,0:T(8,128)(2,1)}, u32[]{:S(2)}, u32[]{:S(2)}) collective-permute-start(bf16[576,2048]{1,0:T(8,128)(2,1)} %pad_maximum_fusion.6), channel_id=1, source_target_pairs={{1,0},{2,1},{3,2},{4,3},{5,4},{6,5},{7,6},{8,7},{9,8},{10,9},{11,1... | collective-permute-start | bytes 7077896 | tf_op jit(solution)/shard_map/ppermute | solution.py:31
  1557.9 368.7 %reduce-scatter.9.cloned.1.call-start = ((), (), s32[]{:S(2)}) async-start(), calls=%async_computation.10 | async-start | bytes 17301504 | tf_op jit(solution)/shard_map/reduce_scatter | solution.py:281
  1575.2 539.0 %reduce-scatter.11.cloned.1.call-start = ((), (), s32[]{:S(2)}) async-start(), calls=%async_computation.11 | async-start | bytes 17301504 | tf_op jit(solution)/shard_map/reduce_scatter | solution.py:283
  (133 other events, 904.3 us)
Sparse Core Ops, SparseCore 0:
  10.9 72.2 all-gather.5
  86.1 76.5 all-gather.7
  165.5 75.9 all-gather.9
  244.2 76.0 all-gather.11
  579.1 137.4 reduce-scatter.6
  1558.0 183.7 reduce-scatter.4
  1744.8 181.7 reduce-scatter.8
  1929.6 184.5 reduce-scatter.10
where the time goes:
time: 2140 us; the launch traced here: 2120 us
  local copies, waits for them, and re-layouts  615 us (29%)
  matrix products  550 us (26%)
  waiting for transfers between devices  413 us (19%)
  other arithmetic  212 us (10%)
  blocking collectives  193 us (9%)
  loops' own time  108 us (5%)
    reduce_scatter x1, waiting for transfers between devices, local(): lax.psum_scatter(grad_down, 'fsdp', scatter_dimension=0, tiled=True)  188 us
    reduce_scatter x1, waiting for transfers between devices, local(): lax.psum_scatter(grad_up, 'fsdp', scatter_dimension=0, tiled=True)  185 us
    dynamic_update_slice x32, local copies, waits for them, and re-layouts, back_piece(): lax.dynamic_update_slice(dvalue_ext, value_old + dvalue.reshape(window_ro...  135 us
    dot_general x32, matrix products, piece_inputs(): jnp.einsum('qhd,khd->hqk', query_block, key_block, preferred_element_type...  128 us
    unnamed x2, blocking collectives  110 us
    dynamic_update_slice x32, local copies, waits for them, and re-layouts, back_piece(): lax.dynamic_update_slice(dkey_ext, key_old + dkey.reshape(window_rows, pa...  97 us
    all_gather x1, blocking collectives, local(): lax.all_gather(up_bias, 'fsdp', axis=0, tiled=True)  82.9 us
    dynamic_slice x32, local copies, waits for them, and re-layouts, back_piece(): lax.dynamic_slice(dvalue_ext, (row_start, col_start), (window_rows, pair_...  74.9 us
  transfers between devices with their start and end apart: 14, of which 4 were waited for; matrix products, arithmetic and copies ran while one was open for 61% of the time, Pallas kernels for 0%

commit v1 on v0

v1 whole, which is shorter than its diff:
```python
import functools
import math

import jax
import jax.numpy as jnp
from jax import lax
from jax.experimental import pallas as pl
from jax.experimental.pallas import tpu as pltpu
from jax.sharding import PartitionSpec as P

HDIM = 64
IMG = 577
RIM = IMG - 1
WIN = 592
QB = 128
EPS = 1e-06
NEG = -1e30
AXIS = "fsdp"
BF = jnp.bfloat16
F32 = jnp.float32
NT = (((1,), (1,)), ((), ()))
TN = (((0,), (0,)), ((), ()))
NN = (((1,), (0,)), ((), ()))


def dot(a, b, dims=NN):
    return lax.dot_general(a, b, dims, preferred_element_type=F32)


def stacked(block):
    lane = lax.broadcasted_iota(jnp.int32, block.shape, 1)
    zero = jnp.zeros_like(block)
    return jnp.concatenate(
        [jnp.where(lane < HDIM, block, zero), jnp.where(lane >= HDIM, block, zero)], axis=0
    )


def unstacked(wide):
    return jnp.concatenate([wide[:HDIM, :QB], wide[HDIM:, QB:]], axis=0).T


def segments(meta, rows):
    n0, first, last = meta[0], meta[1], meta[2]
    limit = jnp.where(last == 1, RIM + rows, 2 * RIM + rows)
    start0 = jnp.where(first == 1, RIM, n0 - 1)
    start1 = RIM + n0
    start2 = start1 + IMG
    return (
        (start0, start1),
        (start1, jnp.minimum(start1 + IMG, limit)),
        (start2, jnp.minimum(start2 + IMG, limit)),
    )


def pick(seg, table):
    (a0, b0), (a1, b1), (a2, b2) = table
    start = jnp.where(seg == 0, a0, jnp.where(seg == 1, a1, a2))
    stop = jnp.where(seg == 0, b0, jnp.where(seg == 1, b1, b2))
    base = pl.multiple_of(start // 16 * 16, 16)
    return base, start - base, stop - base


def key_mask(low, high):
    row = lax.broadcasted_iota(jnp.int32, (WIN, 2 * QB), 0)
    return (row >= low) & (row < high)


def attend_kernel(meta, q_ref, k_ref, v_ref, out_ref, lse_ref):
    rows = q_ref.shape[0]
    n0 = meta[0]
    n1 = n0 + IMG
    table = segments(meta, rows)

    def one(queries, seg):
        base, low, high = pick(seg, table)
        keys = k_ref[pl.ds(base, WIN), :]
        values = v_ref[pl.ds(base, WIN), :]
        scores = jnp.where(key_mask(low, high), dot(keys, queries, NT), NEG)
        top = jnp.max(scores, axis=0, keepdims=True)
        terms = jnp.exp(scores - top)
        total = jnp.sum(terms, axis=0, keepdims=True)
        mixed = dot(values, terms.astype(BF), TN) / total
        return unstacked(mixed), top + jnp.log(total)

    @pl.loop(0, rows // QB)
    def _(blk):
        row0 = pl.multiple_of(blk * QB, QB)
        queries = stacked(q_ref[pl.ds(row0, QB), :]) * jnp.asarray(0.125, BF)
        seg_a = (row0 >= n0).astype(jnp.int32) + (row0 >= n1).astype(jnp.int32)
        end = row0 + QB - 1
        seg_b = (end >= n0).astype(jnp.int32) + (end >= n1).astype(jnp.int32)
        mixed, lse = one(queries, seg_a)
        out_ref[pl.ds(row0, QB), :] = mixed.astype(BF)
        lse_ref[0, pl.ds(blk, 1), :] = lse

        @pl.when(seg_b > seg_a)
        def _():
            split = jnp.where(seg_a == 0, n0, n1) - row0
            mixed_b, lse_b = one(queries, seg_b)
            here = lax.broadcasted_iota(jnp.int32, mixed.shape, 0) < split
            out_ref[pl.ds(row0, QB), :] = jnp.where(here, mixed, mixed_b).astype(BF)
            lane = lax.broadcasted_iota(jnp.int32, lse.shape, 1) % QB
            lse_ref[0, pl.ds(blk, 1), :] = jnp.where(lane < split, lse, lse_b)


def attend(meta, queries, key_value):
    rows, width = queries.shape
    pairs = width // (2 * HDIM)
    ext = key_value.shape[0]
    return pl.pallas_call(
        attend_kernel,
        grid_spec=pltpu.PrefetchScalarGridSpec(
            num_scalar_prefetch=1,
            grid=(pairs,),
            in_specs=[
                pl.BlockSpec((rows, 2 * HDIM), lambda p, m: (0, p)),
                pl.BlockSpec((ext, 2 * HDIM), lambda p, m: (0, p)),
                pl.BlockSpec((ext, 2 * HDIM), lambda p, m: (0, pairs + p)),
            ],
            out_specs=[
                pl.BlockSpec((rows, 2 * HDIM), lambda p, m: (0, p)),
                pl.BlockSpec((1, rows // QB, 2 * QB), lambda p, m: (p, 0, 0)),
            ],
        ),
        out_shape=[
            jax.ShapeDtypeStruct((rows, width), BF),
            jax.ShapeDtypeStruct((pairs, rows // QB, 2 * QB), F32),
        ],
        compiler_params=pltpu.CompilerParams(vmem_limit_bytes=48 * 2**20),
        name="attend",
    )(meta, queries, key_value, key_value)


def attend_back_kernel(meta, q_ref, k_ref, v_ref, up_ref, lse_ref, dq_ref, dk_ref, dv_ref):
    rows = q_ref.shape[0]
    n0 = meta[0]
    n1 = n0 + IMG
    table = segments(meta, rows)
    dk_ref[...] = jnp.zeros_like(dk_ref)
    dv_ref[...] = jnp.zeros_like(dv_ref)

    def one(queries, upstream, lse, seg):
        base, low, high = pick(seg, table)
        keys = k_ref[pl.ds(base, WIN), :]
        values = v_ref[pl.ds(base, WIN), :]
        scores = jnp.where(key_mask(low, high), dot(keys, queries, NT), NEG)
        probs = jnp.exp(scores - lse)
        dprobs = dot(values, upstream, NT)
        row_dot = jnp.sum(probs * dprobs, axis=0, keepdims=True)
        dscores = (probs * (dprobs - row_dot)).astype(BF)
        dv_ref[pl.ds(base, WIN), :] += dot(probs.astype(BF), upstream)
        dk_ref[pl.ds(base, WIN), :] += dot(dscores, queries)
        return unstacked(dot(keys, dscores, TN)) * 0.125

    @pl.loop(0, rows // QB)
    def _(blk):
        row0 = pl.multiple_of(blk * QB, QB)
        queries = stacked(q_ref[pl.ds(row0, QB), :]) * jnp.asarray(0.125, BF)
        upstream = stacked(up_ref[pl.ds(row0, QB), :])
        lse = lse_ref[0, pl.ds(blk, 1), :]
        seg_a = (row0 >= n0).astype(jnp.int32) + (row0 >= n1).astype(jnp.int32)
        end = row0 + QB - 1
        seg_b = (end >= n0).astype(jnp.int32) + (end >= n1).astype(jnp.int32)
        split = jnp.where(seg_b > seg_a, jnp.where(seg_a == 0, n0, n1) - row0, QB)
        lane = lax.broadcasted_iota(jnp.int32, lse.shape, 1) % QB
        dq = one(queries, upstream, jnp.where(lane < split, lse, -NEG), seg_a)
        dq_ref[pl.ds(row0, QB), :] = dq.astype(BF)

        @pl.when(seg_b > seg_a)
        def _():
            dq_b = one(queries, upstream, jnp.where(lane < split, -NEG, lse), seg_b)
            dq_ref[pl.ds(row0, QB), :] = (dq + dq_b).astype(BF)


def attend_back(meta, queries, key_value, upstream, lse):
    rows, width = queries.shape
    pairs = width // (2 * HDIM)
    ext = key_value.shape[0]
    own = pl.BlockSpec((rows, 2 * HDIM), lambda p, m: (0, p))
    wide = pl.BlockSpec((ext, 2 * HDIM), lambda p, m: (0, p))
    return pl.pallas_call(
        attend_back_kernel,
        grid_spec=pltpu.PrefetchScalarGridSpec(
            num_scalar_prefetch=1,
            grid=(pairs,),
            in_specs=[
                own,
                wide,
                pl.BlockSpec((ext, 2 * HDIM), lambda p, m: (0, pairs + p)),
                own,
                pl.BlockSpec((1, rows // QB, 2 * QB), lambda p, m: (p, 0, 0)),
            ],
            out_specs=[own, wide, wide],
        ),
        out_shape=[
            jax.ShapeDtypeStruct((rows, width), BF),
            jax.ShapeDtypeStruct((ext, width), F32),
            jax.ShapeDtypeStruct((ext, width), F32),
        ],
        compiler_params=pltpu.CompilerParams(vmem_limit_bytes=48 * 2**20),
        name="attend_back",
    )(meta, queries, key_value, key_value, upstream, lse)


def shifted(value, by):
    peers = lax.axis_size(AXIS)
    pairs = [(i, i + by) for i in range(peers) if 0 <= i + by < peers]
    return lax.ppermute(value, AXIS, pairs)


def gathered(value):
    return lax.all_gather(value, AXIS, axis=0, tiled=True)


def scattered(value):
    return lax.psum_scatter(value, AXIS, scatter_dimension=0, tiled=True)


def normalize(inputs, gain, shift):
    center = inputs - jnp.mean(inputs, axis=1, keepdims=True)
    inv_std = lax.rsqrt(jnp.mean(center * center, axis=1, keepdims=True) + EPS)
    scaled = center * inv_std
    return (scaled * gain + shift, scaled, inv_std)


def normalize_back(upstream, scaled, inv_std, gain):
    through = upstream * gain
    inner = (
        through
        - jnp.mean(through, axis=1, keepdims=True)
        - scaled * jnp.mean(through * scaled, axis=1, keepdims=True)
    )
    return (inv_std * inner, jnp.sum(upstream * scaled, axis=0), jnp.sum(upstream, axis=0))


def local(
    tokens,
    image_ids,
    cotangent,
    norm1_gain,
    norm1_shift,
    qkv_weight,
    query_bias,
    value_bias,
    out_weight,
    out_bias,
    norm2_gain,
    norm2_shift,
    up_weight,
    up_bias,
    down_weight,
    down_bias,
):
    rows, width = tokens.shape
    me = lax.axis_index(AXIS)
    peers = lax.axis_size(AXIS)
    meta = jnp.stack(
        [
            jnp.sum((image_ids == image_ids[0]).astype(jnp.int32)),
            (me == 0).astype(jnp.int32),
            (me == peers - 1).astype(jnp.int32),
        ]
    )
    ext = -(-(rows + 2 * RIM + 64) // 128) * 128
    vectors = gathered(
        jnp.concatenate(
            [norm1_gain, norm1_shift, query_bias, value_bias, out_bias, norm2_gain, norm2_shift,
             down_bias, up_bias]
        )[None]
    ).astype(F32)
    part = norm1_gain.shape[0]
    gain1, shift1, q_bias, v_bias, o_bias, gain2, shift2, d_bias = (
        vectors[:, i * part : (i + 1) * part].reshape(-1) for i in range(8)
    )
    u_bias = vectors[:, 8 * part :].reshape(-1)
    w_qkv, w_out, w_up, w_down = map(gathered, (qkv_weight, out_weight, up_weight, down_weight))

    low_rim = shifted(tokens[rows - RIM :], 1)
    high_rim = shifted(tokens[:RIM], -1)
    pad = jnp.zeros((ext - rows - 2 * RIM, width), BF)
    tokens_ext = jnp.concatenate([low_rim, tokens, high_rim, pad], axis=0).astype(F32)
    inputs = tokens.astype(F32)
    normed_ext = normalize(tokens_ext, gain1, shift1)[0].astype(BF)
    normed, scaled_one, inv_one = normalize(inputs, gain1, shift1)
    normed_low = normed.astype(BF)
    queries = (dot(normed_low, w_qkv[:, :width]) + q_bias).astype(BF)
    key_value = (
        dot(normed_ext, w_qkv[:, width:]) + jnp.concatenate([jnp.zeros_like(v_bias), v_bias])
    ).astype(BF)
    mixed_low, lse = attend(meta, queries, key_value)

    resid = inputs + dot(mixed_low, w_out) + o_bias
    normed_two, scaled_two, inv_two = normalize(resid, gain2, shift2)
    normed_two_low = normed_two.astype(BF)
    upward = dot(normed_two_low, w_up) + u_bias
    normal_cdf = 0.5 * (1.0 + lax.erf(upward * (1.0 / math.sqrt(2.0))))
    activated_low = (upward * normal_cdf).astype(BF)
    layer_out = (resid + dot(activated_low, w_down) + d_bias).astype(BF)

    upstream_out = cotangent.astype(F32)
    grad_down = dot(activated_low, cotangent, TN)
    grad_down_b = jnp.sum(upstream_out, axis=0)
    normal_pdf = jnp.exp(-0.5 * upward * upward) * (1.0 / math.sqrt(2.0 * math.pi))
    dupward_low = (dot(cotangent, w_down, NT) * (normal_cdf + upward * normal_pdf)).astype(BF)
    grad_up = dot(normed_two_low, dupward_low, TN)
    grad_up_b = jnp.sum(dupward_low.astype(F32), axis=0)
    dnormed_two = dot(dupward_low, w_up, NT)
    dresid_norm, grad_gain_two, grad_shift_two = normalize_back(
        dnormed_two, scaled_two, inv_two, gain2
    )
    dresid = upstream_out + dresid_norm
    dbranch_low = dresid.astype(BF)
    grad_out = dot(mixed_low, dbranch_low, TN)
    grad_out_b = jnp.sum(dbranch_low.astype(F32), axis=0)
    dmixed_low = dot(dbranch_low, w_out, NT).astype(BF)

    dquery_low, dkey_ext, dvalue_ext = attend_back(meta, queries, key_value, dmixed_low, lse)
    dkv_ext = jnp.concatenate([dkey_ext, dvalue_ext], axis=1)
    from_after = shifted(dkv_ext[:RIM].astype(BF), -1).astype(F32)
    from_before = shifted(dkv_ext[RIM + rows : 2 * RIM + rows].astype(BF), 1).astype(F32)
    own_grads = dkv_ext[RIM : RIM + rows]
    own_grads = own_grads.at[:RIM].add(from_before).at[rows - RIM :].add(from_after)
    dkv_low = own_grads.astype(BF)
    dproj_low = jnp.concatenate([dquery_low, dkv_low], axis=1)
    grad_qkv = dot(normed_low, dproj_low, TN)
    grad_query_b = jnp.sum(dquery_low.astype(F32), axis=0)
    grad_value_b = jnp.sum(dkv_low[:, width:].astype(F32), axis=0)
    dnormed = dot(dproj_low, w_qkv, NT)
    dinput_norm, grad_gain_one, grad_shift_one = normalize_back(
        dnormed, scaled_one, inv_one, gain1
    )
    grad_tokens = dresid + dinput_norm

    def small(value):
        return value.reshape(peers, -1)

    owned = scattered(
        jnp.concatenate(
            [
                small(v)
                for v in (
                    grad_gain_one, grad_shift_one, grad_query_b, grad_value_b, grad_out_b,
                    grad_gain_two, grad_shift_two, grad_down_b, grad_up_b,
                )
            ],
            axis=1,
        )
    )[0]
    g = [owned[i * part : (i + 1) * part] for i in range(8)] + [owned[8 * part :]]
    r_down, r_up, r_out, r_qkv = (
        scattered(v.astype(BF)).astype(F32) for v in (grad_down, grad_up, grad_out, grad_qkv)
    )
    return (
        layer_out, grad_tokens, g[0], g[1], r_qkv, g[2], g[3], r_out, g[4], g[5], g[6], r_up,
        g[8], r_down, g[7],
    )


def solution(mesh):
    row, vec = P(AXIS, None), P(AXIS)
    return jax.shard_map(
        local,
        mesh=mesh,
        in_specs=(
            row, vec, row, vec, vec, row, vec, vec, row, vec, vec, vec, row, vec, row, vec,
        ),
        out_specs=(
            row, row, vec, vec, row, vec, vec, row, vec, vec, vec, row, vec, row, vec,
        ),
        check_vma=False,
    )
```

time: 2140 us -> 1040 us (0.49)
  local copies, waits for them, and re-layouts: 615 us -> 67.1 us
  matrix products: 550 us -> 148 us
  other arithmetic: 212 us -> 51.6 us
  Pallas kernels: 0 us -> 128 us
  loops' own time: 108 us -> 0 us
  waiting for transfers between devices: 413 us -> 453 us
  blocking collectives: 193 us -> 158 us
    dot_general x124 -> x13, matrix products: 550 us -> 148 us  [dot(): return lax.dot_general(a, b, dims, preferred_element_type=F32)]
    dynamic_update_slice x96 -> x0, local copies, waits for them, and re-layouts: 254 us -> none  [the longest x32 135 us: back_piece(): lax.dynamic_update_slice(dvalue_ext, value_old + dvalue.reshape(window_ro...]
    dynamic_slice x256 -> x0, local copies, waits for them, and re-layouts: 222 us -> none  [the longest x32 74.9 us: back_piece(): lax.dynamic_slice(dvalue_ext, (row_start, col_start), (window_rows, pair_...]
    pallas_call x0 -> x2, Pallas kernels: none -> 128 us  [the longest x1 69.4 us: attend_back(): pl.pallas_call(attend_back_kernel, grid_spec=pltpu.PrefetchScalarGridSpec...]
    another operation x2 -> x0, loops' own time: 108 us -> none  [the longest x1 65.5 us: local(): lax.scan(back_piece, (zero_ext, zero_ext), jnp.arange(piece_count, dtype=...]
    all_gather x4, waiting for transfers between devices: 20.4 us -> 91.8 us  [gathered(): return lax.all_gather(value, AXIS, axis=0, tiled=True)]
    add x32 -> x0, other arithmetic: 40.7 us -> none  [the longest x16 39.3 us: back_piece(): value_old + dvalue.reshape(window_rows, pair_cols)]
    convert_element_type x28 -> x5, other arithmetic: 47.1 us -> 7.43 us  [the longest x4 6.77 us: local(): scattered(v.astype(BF)).astype(F32)]
  transfers between devices with their start and end apart: 14 -> 12, of which waited for: 4 -> 5; matrix products, arithmetic and copies ran while one was open for 61% -> 17% of each run, Pallas kernels for 0% -> 6%
where the time goes in v1:
time: 1040 us; the launch traced here: 1030 us
  waiting for transfers between devices  453 us (44%)
  blocking collectives  158 us (15%)
  matrix products  148 us (14%)
  Pallas kernels  128 us (12%)
  local copies, waits for them, and re-layouts  67.1 us (6%)
  other arithmetic  51.6 us (5%)
  between operations  15.3 us (1%)
    reduce_scatter x4, waiting for transfers between devices, scattered(): return lax.psum_scatter(value, AXIS, scatter_dimension=0, tiled=True)  358 us
    dot_general x13, matrix products, dot(): return lax.dot_general(a, b, dims, preferred_element_type=F32)  148 us
    all_gather x4, waiting for transfers between devices, gathered(): return lax.all_gather(value, AXIS, axis=0, tiled=True)  91.8 us
    unnamed x1, blocking collectives  89.2 us
    pallas_call x1, Pallas kernels, attend_back(): pl.pallas_call(attend_back_kernel, grid_spec=pltpu.PrefetchScalarGridSpec...  69.4 us
    all_gather x1, blocking collectives, gathered(): return lax.all_gather(value, AXIS, axis=0, tiled=True)  69.1 us
    pallas_call x1, Pallas kernels, attend(): pl.pallas_call(attend_kernel, grid_spec=pltpu.PrefetchScalarGridSpec(num_...  58.2 us
    unnamed x95, local copies, waits for them, and re-layouts  38 us
  transfers between devices with their start and end apart: 12, of which 5 were waited for; matrix products, arithmetic and copies ran while one was open for 17% of the time, Pallas kernels for 6%

profile of v1, /device:TPU:0, one launch (start us, length us, event | category | flops | bytes accessed | tf_op | source)
XLA Modules:
  0.0 1029.7 jit_solution(14081044687351128936)
XLA Ops:
  17.8 69.1 %all-gather.1 = bf16[32,1,384]{2,1,0:T(2,128)(2,1)S(1)} all-gather(bf16[1,1,384]{2,1,0:T(2,128)(2,1)S(1)} %reshape.193), channel_id=2, replica_groups=mesh['fsdp'=32] {'fsdp'}, dimensions={0}, use_global_device_ids=true | all-gather | bytes 25344 | tf_op jit(solution)/shard_map/all_gather | solution.py:212
  112.2 12.9 %add_convert_fusion.k_ref.v_ref = bf16[2304,2048]{1,0:T(8,128)(2,1)} fusion(f32[2048]{0:T(1024)S(1)} %concatenate.24, bf16[2304,1024]{1,0:T(8,128)(2,1)S(1)} %copy-done.13, f32[1024]{0:T(1024)S(1)} %add.151, f32[1024]{0:T(1024)S(1)} %mul.152, f32[2304]{0:T(1024)S(1)} %add_rsqrt_fusion, f32[2304]{0:T(1024)S(1)} %broadcast_multiply_fusion, ...), kind=kOutput, calls=%fused_computation.1 | convolution fusion | flops 9687269376 | bytes 18391040 | tf_op jit(solution)/shard_map/dot_general | solution.py:27
  125.1 58.2 %attend.1 = (bf16[1024,1024]{1,0:T(8,128)(2,1)S(1)}, f32[8,8,256]{2,1,0:T(8,128)S(1)}) custom-call(s32[3]{0:T(128)S(1)} %pad_add_fusion.meta, bf16[1024,1024]{1,0:T(8,128)(2,1)S(1)} %add_convert_fusion.3.q_ref, bf16[2304,2048]{1,0:T(8,128)(2,1)} %add_convert_fusion.k_ref.v_ref, bf16[2304,2048]{1,0:T(8,128)(2,1)} %add_convert_fusion.k_ref.v_ref), custom_call_target="tpu_custom_call" | custom-call | tf_op jit(solution)/shard_map/attend/pallas_call | solution.py:110
  184.7 5.7 fusion.50
  192.9 33.1 %all-gather.11.cloned.1.call-done = bf16[1024,4096]{1,0:T(8,128)(2,1)} async-done(((bf16[32,4096]{1,0:T(8,128)(2,1)}), bf16[1024,4096]{1,0:T(8,128)(2,1)}) %all-gather.11.cloned.1.call-update) | async-done | bytes 8388624 | tf_op jit(solution)/shard_map/all_gather | solution.py:212
  225.9 20.0 %multiply_convert_fusion = (bf16[1024,4096]{1,0:T(8,128)(2,1)}, f32[1024,4096]{1,0:T(8,128)}) fusion(f32[4096]{0:T(1024)S(1)} %slice_bitcast_fusion, bf16[1024,4096]{1,0:T(8,128)(2,1)} %all-gather.11.cloned.1.call-done, f32[1024,1024]{0,1:T(8,128)} %copy-done.7, f32[1024]{0:T(1024)S(1)} %add.168, f32[1024]{0:T(1024)S(1)} %mul.163, ...), kind=kOutput, calls=%fused_computation.9 | convolution fusion | flops 8620343296 | bytes 37781504 | tf_op jit(solution)/shard_map/dot_general | solution.py:27
  246.0 58.8 %all-gather.13.cloned.1.call-done = bf16[4096,1024]{1,0:T(8,128)(2,1)} async-done(((bf16[128,1024]{1,0:T(8,128)(2,1)}), bf16[4096,1024]{1,0:T(8,128)(2,1)}) %all-gather.13.cloned.1.call-update) | async-done | bytes 8388624 | tf_op jit(solution)/shard_map/all_gather | solution.py:212
  304.7 19.2 %convert_reduce_fusion = (f32[4096]{0:T(1024)}, bf16[1024,4096]{1,0:T(8,128)(2,1)S(1)}) fusion(f32[1024,4096]{1,0:T(8,128)} %get-tuple-element.113, f32[4096]{0:T(1024)S(1)} %slice_bitcast_fusion, bf16[1024,1024]{1,0:T(8,128)(2,1)} %param.22, bf16[4096,1024]{1,0:T(8,128)(2,1)} %all-gather.13.cloned.1.call-done), kind=kOutput, calls=%fused_computation.8 | convolution fusion | flops 8644456448 | bytes 35684352 | tf_op jit(solution)/shard_map/dot_general | solution.py:27
  323.9 11.1 %fusion.52 = (f32[1024]{0:T(1024)}, f32[1024,1024]{1,0:T(8,128)}) fusion(bf16[1024,4096]{1,0:T(8,128)(2,1)S(1)} %get-tuple-element.119, bf16[1024,4096]{1,0:T(8,128)(2,1)S(1)} %copy-done.40), kind=kOutput, calls=%fused_computation.105 | convolution fusion | flops 8590982144 | bytes 20975616 | tf_op jit(solution)/shard_map/dot_general | solution.py:27
  354.4 69.4 %attend_back.1 = (bf16[1024,1024]{1,0:T(8,128)(2,1)S(1)}, f32[2304,1024]{1,0:T(8,128)}, f32[2304,1024]{1,0:T(8,128)}) custom-call(s32[3]{0:T(128)S(1)} %pad_add_fusion.meta, bf16[1024,1024]{1,0:T(8,128)(2,1)S(1)} %add_convert_fusion.3.q_ref, bf16[2304,2048]{1,0:T(8,128)(2,1)} %add_convert_fusion.k_ref.v_ref, bf16[2304,2048]{1,0:T(8,128)(2,1)} %add_convert_fusion.k_ref.v_ref, ...), custom_call_target="tpu_custom_call" | custom-call | tf_op jit(solution)/shard_map/attend_back/pallas_call | solution.py:181
  423.8 10.0 constant_dynamic-update-slice_fusion.1
  433.8 5.4 constant_dynamic-update-slice_fusion
  439.3 7.5 convert.6
  471.9 9.2 convolution_convert_fusion.2
  481.1 14.9 %convolution_convert_fusion = bf16[4096,1024]{1,0:T(8,128)(2,1)} fusion(bf16[1024,4096]{1,0:T(8,128)(2,1)} %get-tuple-element.112, bf16[1024,1024]{1,0:T(8,128)(2,1)} %param.22), kind=kOutput, calls=%fused_computation.19 | convolution fusion | flops 8594128896 | bytes 18874368 | tf_op jit(solution)/shard_map/dot_general | solution.py:27
  496.7 15.4 %convolution_convert_fusion.1 = bf16[1024,4096]{1,0:T(8,128)(2,1)} fusion(bf16[1024,4096]{1,0:T(8,128)(2,1)} %copy-done.43, f32[1024,1024]{0,1:T(8,128)} %copy-done.7, f32[1024]{0:T(1024)S(1)} %copy-done.26, f32[1024]{0:T(1024)S(1)} %mul.163, f32[1024]{0:T(1024)S(1)} %add_rsqrt_fusion.1, f32[1024]{0:T(1024)S(1)} %broadcast_multiply_fusion.5), kind=kOutput, calls=%fused_computation.20 | convolution fusion | flops 8599371776 | bytes 20987904 | tf_op jit(solution)/shard_map/dot_general | solution.py:27
  513.0 15.4 %add_convert_fusion.1 = bf16[1024,1024]{0,1:T(8,128)(2,1)} fusion(f32[1024,1024]{0,1:T(8,128)} %copy-done.7, f32[1024]{0:T(1024)S(1)} %add.177, bf16[1024,4096]{1,0:T(8,128)(2,1)} %get-tuple-element.112, bf16[4096,1024]{1,0:T(8,128)(2,1)} %all-gather.13.cloned.1.call-done), kind=kOutput, calls=%fused_computation.58 | convolution fusion | flops 8593080320 | bytes 23072768 | tf_op jit(solution)/shard_map/dot_general | solution.py:27
  535.1 11.4 %fusion.51 = (f32[1024]{0:T(1024)S(1)}, f32[1024,1024]{1,0:T(8,128)}) fusion(bf16[1024,3072]{1,0:T(8,128)(2,1)} %all-gather.7.cloned.1.call-done, bf16[1024,2048]{1,0:T(8,128)(2,1)} %copy-done.15, bf16[1024,1024]{1,0:T(8,128)(2,1)S(1)} %copy-done.1), kind=kOutput, calls=%fused_computation.104 | convolution fusion | flops 6456081408 | bytes 16781312 | tf_op jit(solution)/shard_map/dot_general | solution.py:27
  546.6 5.6 copy.44
  556.0 5.5 fusion.30
  567.0 89.2 %all-reduce.1 = f32[32,384]{1,0:T(8,128)S(1)} all-reduce(f32[32,384]{1,0:T(8,128)S(1)} %concatenate.27), channel_id=3, replica_groups=mesh['fsdp'=32] {'fsdp'}, use_global_device_ids=true, to_apply=%region_20.0.clone | all-reduce | flops 12288 | bytes 98304
  659.0 64.3 %reduce-scatter.5.cloned.1.call-done = bf16[32,3072]{1,0:T(8,128)(2,1)} async-done(((bf16[1024,3072]{1,0:T(8,128)(2,1)}), bf16[32,3072]{1,0:T(8,128)(2,1)}) %reduce-scatter.5.cloned.1.call-update) | async-done | bytes 196624 | tf_op jit(solution)/shard_map/reduce_scatter | solution.py:216
  725.0 148.6 %reduce-scatter.11.cloned.1.call-done = bf16[128,1024]{1,0:T(8,128)(2,1)} async-done(((bf16[4096,1024]{1,0:T(8,128)(2,1)}), bf16[128,1024]{1,0:T(8,128)(2,1)}) %reduce-scatter.11.cloned.1.call-update) | async-done | bytes 262160 | tf_op jit(solution)/shard_map/reduce_scatter | solution.py:216
  875.3 145.2 %reduce-scatter.9.cloned.1.call-done = bf16[32,4096]{1,0:T(8,128)(2,1)} async-done(((bf16[1024,4096]{1,0:T(8,128)(2,1)}), bf16[32,4096]{1,0:T(8,128)(2,1)}) %reduce-scatter.9.cloned.1.call-update) | async-done | bytes 262160 | tf_op jit(solution)/shard_map/reduce_scatter | solution.py:216
  (182 shorter events, 109.4 us)
Async XLA Ops:
  7.2 10.4 %copy-start.38 = (bf16[32]{0:T(256)(128)(2,1)S(1)}, bf16[32]{0:T(256)(128)(2,1)}, u32[]{:S(2)}) copy-start(bf16[32]{0:T(256)(128)(2,1)} %param.35) | copy-start | bytes 196
  7.2 10.4 %copy-start.39 = (bf16[128]{0:T(256)(128)(2,1)S(1)}, bf16[128]{0:T(256)(128)(2,1)}, u32[]{:S(2)}) copy-start(bf16[128]{0:T(256)(128)(2,1)} %param.33) | copy-start | bytes 772
  7.2 10.4 %copy-start.37 = (bf16[32]{0:T(256)(128)(2,1)S(1)}, bf16[32]{0:T(256)(128)(2,1)}, u32[]{:S(2)}) copy-start(bf16[32]{0:T(256)(128)(2,1)} %param.31) | copy-start | bytes 196
  7.2 10.4 %copy-start.36 = (bf16[32]{0:T(256)(128)(2,1)S(1)}, bf16[32]{0:T(256)(128)(2,1)}, u32[]{:S(2)}) copy-start(bf16[32]{0:T(256)(128)(2,1)} %param.30) | copy-start | bytes 196
  7.2 10.4 %copy-start.35 = (bf16[32]{0:T(256)(128)(2,1)S(1)}, bf16[32]{0:T(256)(128)(2,1)}, u32[]{:S(2)}) copy-start(bf16[32]{0:T(256)(128)(2,1)} %param.29) | copy-start | bytes 196
  7.2 10.4 %copy-start.34 = (bf16[32]{0:T(256)(128)(2,1)S(1)}, bf16[32]{0:T(256)(128)(2,1)}, u32[]{:S(2)}) copy-start(bf16[32]{0:T(256)(128)(2,1)} %param.27) | copy-start | bytes 196
  7.3 99.4 %all-gather.7.cloned.1.call-start = ((), (), s32[]{:S(2)}) async-start(), calls=%async_computation.4 | async-start | bytes 6488064 | tf_op jit(solution)/shard_map/all_gather | solution.py:212
  8.0 176.6 %all-gather.9.cloned.1.call-start = ((), (), s32[]{:S(2)}) async-start(), calls=%async_computation.5 | async-start | bytes 2162688 | tf_op jit(solution)/shard_map/all_gather | solution.py:212
  8.8 217.2 %all-gather.11.cloned.1.call-start = ((), (), s32[]{:S(2)}) async-start(), calls=%async_computation.6 | async-start | bytes 8650752 | tf_op jit(solution)/shard_map/all_gather | solution.py:212
  9.5 295.2 %all-gather.13.cloned.1.call-start = ((), (), s32[]{:S(2)}) async-start(), calls=%async_computation.7 | async-start | bytes 8650752 | tf_op jit(solution)/shard_map/all_gather | solution.py:212
  10.1 647.4 %reduce-scatter.7.cloned.1.call-start = ((), (), s32[]{:S(2)}) async-start(), calls=%async_computation.9 | async-start | bytes 2162688 | tf_op jit(solution)/shard_map/reduce_scatter | solution.py:216
  13.4 84.8 %collective-permute-start = (bf16[576,1024]{1,0:T(8,128)(2,1)}, bf16[576,1024]{1,0:T(8,128)(2,1)S(1)}, u32[]{:S(2)}, u32[]{:S(2)}) collective-permute-start(bf16[576,1024]{1,0:T(8,128)(2,1)} %get-tuple-element.92), channel_id=1, source_target_pairs={{0,1},{1,2},{2,3},{3,4},{4,5},{5,6},{6,7},{7,8},{8,9},{9,10},{10,1... | collective-permute-start | bytes 3538952 | tf_op jit(solution)/shard_map/ppermute | solution.py:208
  15.8 82.4 %collective-permute-start.1 = (bf16[576,1024]{1,0:T(8,128)(2,1)}, bf16[576,1024]{1,0:T(8,128)(2,1)}, u32[]{:S(2)}, u32[]{:S(2)}) collective-permute-start(bf16[576,1024]{1,0:T(8,128)(2,1)} %get-tuple-element.93), channel_id=1, source_target_pairs={{1,0},{2,1},{3,2},{4,3},{5,4},{6,5},{7,6},{8,7},{9,8},{10,9},{11,1... | collective-permute-start | bytes 3538952 | tf_op jit(solution)/shard_map/ppermute | solution.py:208
  92.6 19.2 %copy-start.20 = (f32[1024]{0:T(1024)}, f32[1024]{0:T(1024)S(1)}, u32[]{:S(2)}) copy-start(f32[1024]{0:T(1024)S(1)} %mul.152) | copy-start | bytes 12292
  92.7 19.1 %copy-start.27 = (f32[1024]{0:T(1024)}, f32[1024]{0:T(1024)S(1)}, u32[]{:S(2)}) copy-start(f32[1024]{0:T(1024)S(1)} %add.151) | copy-start | bytes 12292
  92.8 133.2 %copy-start.25 = (f32[1024]{0:T(1024)}, f32[1024]{0:T(1024)S(1)}, u32[]{:S(2)}) copy-start(f32[1024]{0:T(1024)S(1)} %add.168) | copy-start | bytes 12292
  304.7 19.2 %copy-start.40 = (bf16[1024,4096]{1,0:T(8,128)(2,1)S(1)}, bf16[1024,4096]{1,0:T(8,128)(2,1)}, u32[]{:S(2)}) copy-start(bf16[1024,4096]{1,0:T(8,128)(2,1)} %all-gather.11.cloned.1.call-done) | copy-start | bytes 25165828
  323.9 11.1 %copy-start.43 = (bf16[1024,4096]{1,0:T(8,128)(2,1)}, bf16[1024,4096]{1,0:T(8,128)(2,1)S(1)}, u32[]{:S(2)}) copy-start(bf16[1024,4096]{1,0:T(8,128)(2,1)S(1)} %get-tuple-element.119) | copy-start | bytes 25165828
  350.7 102.8 %copy-start.14 = (f32[1024,1024]{0,1:T(8,128)}, f32[1024,1024]{0,1:T(8,128)S(1)}, u32[]{:S(2)}) copy-start(f32[1024,1024]{0,1:T(8,128)S(1)} %get-tuple-element.86) | copy-start | bytes 12582916
  448.6 12.9 %collective-permute-start.2 = (bf16[576,2048]{1,0:T(8,128)(2,1)}, bf16[576,2048]{1,0:T(8,128)(2,1)}, u32[]{:S(2)}, u32[]{:S(2)}) collective-permute-start(bf16[576,2048]{1,0:T(8,128)(2,1)} %get-tuple-element.90), channel_id=1, source_target_pairs={{0,1},{1,2},{2,3},{3,4},{4,5},{5,6},{6,7},{7,8},{8,9},{9,10},{10,1... | collective-permute-start | bytes 7077896 | tf_op jit(solution)/shard_map/ppermute | solution.py:208
  452.1 13.2 %collective-permute-start.3 = (bf16[576,2048]{1,0:T(8,128)(2,1)S(1)}, bf16[576,2048]{1,0:T(8,128)(2,1)}, u32[]{:S(2)}, u32[]{:S(2)}) collective-permute-start(bf16[576,2048]{1,0:T(8,128)(2,1)S(1)} %get-tuple-element.89), channel_id=1, source_target_pairs={{1,0},{2,1},{3,2},{4,3},{5,4},{6,5},{7,6},{8,7},{9,8},{10,9},{11,1... | collective-permute-start | bytes 7077896 | tf_op jit(solution)/shard_map/ppermute | solution.py:208
  457.2 266.0 %reduce-scatter.5.cloned.1.call-start = ((), (), s32[]{:S(2)}) async-start(), calls=%async_computation.8 | async-start | bytes 6488064 | tf_op jit(solution)/shard_map/reduce_scatter | solution.py:216
  481.1 392.4 %reduce-scatter.11.cloned.1.call-start = ((), (), s32[]{:S(2)}) async-start(), calls=%async_computation.11 | async-start | bytes 8650752 | tf_op jit(solution)/shard_map/reduce_scatter | solution.py:216
  496.1 524.5 %reduce-scatter.9.cloned.1.call-start = ((), (), s32[]{:S(2)}) async-start(), calls=%async_computation.10 | async-start | bytes 8650752 | tf_op jit(solution)/shard_map/reduce_scatter | solution.py:216
  (32 other events, 166.6 us)
Sparse Core Ops, SparseCore 0:
  11.0 77.3 all-gather.6
  91.2 55.1 all-gather.8
  149.3 76.5 all-gather.10
  228.7 76.0 all-gather.12
  457.3 148.8 reduce-scatter.6
  612.7 110.5 reduce-scatter.4
  725.5 147.9 reduce-scatter.10
  875.8 144.7 reduce-scatter.8

commit v2 on v1

v2 whole, which is shorter than its diff:
```python
import functools
import math

import jax
import jax.numpy as jnp
from jax import lax
from jax.experimental import pallas as pl
from jax.experimental.pallas import tpu as pltpu
from jax.sharding import PartitionSpec as P

HDIM = 64
IMG = 577
RIM = IMG - 1
WIN = 592
QB = 128
EPS = 1e-06
NEG = -1e30
AXIS = "fsdp"
BF = jnp.bfloat16
F32 = jnp.float32
NT = (((1,), (1,)), ((), ()))
TN = (((0,), (0,)), ((), ()))
NN = (((1,), (0,)), ((), ()))


def dot(a, b, dims=NN):
    return lax.dot_general(a, b, dims, preferred_element_type=F32)


def stacked(block):
    lane = lax.broadcasted_iota(jnp.int32, block.shape, 1)
    zero = jnp.zeros_like(block)
    return jnp.concatenate(
        [jnp.where(lane < HDIM, block, zero), jnp.where(lane >= HDIM, block, zero)], axis=0
    )


def unstacked(wide):
    return jnp.concatenate([wide[:HDIM, :QB], wide[HDIM:, QB:]], axis=0).T


def key_mask(low, high):
    row = lax.broadcasted_iota(jnp.int32, (WIN, 2 * QB), 0)
    return (row >= low) & (row < high)


def mesh_copy(src, dst, send_sem, recv_sem, to):
    return pltpu.make_async_remote_copy(
        src_ref=src,
        dst_ref=dst,
        send_sem=send_sem,
        recv_sem=recv_sem,
        device_id=(to,),
        device_id_type=pl.DeviceIdType.MESH,
    )


class Place:
    def __init__(self):
        me = lax.axis_index(AXIS)
        self.c, self.x, self.y, self.z = me % 2, me // 2 % 2, me // 4 % 2, me // 8
        self.sib = self.at(self.z, self.y, self.x, 1 - self.c)
        self.xp = self.at(self.z, self.y, 1 - self.x, self.c)
        self.yp = self.at(self.z, 1 - self.y, self.x, self.c)
        self.zp = [self.at((self.z + k) % 4, self.y, self.x, self.c) for k in (1, 2, 3)]
        self.partners = [self.sib, self.xp, self.yp, *self.zp]

    @staticmethod
    def at(z, y, x, c):
        return ((z * 2 + y) * 2 + x) * 2 + c


def greet(partners, before=None, after=None):
    barrier = pltpu.get_barrier_semaphore()

    def hello(to):
        pl.semaphore_signal(
            barrier, inc=1, device_id=(to,), device_id_type=pl.DeviceIdType.MESH
        )

    for to in partners:
        hello(to)
    if before is None:
        pl.semaphore_wait(barrier, len(partners))
        return
    me = lax.axis_index(AXIS)
    pl.when(before)(lambda: hello(me - 1))
    pl.when(after)(lambda: hello(me + 1))
    pl.semaphore_wait(
        barrier, len(partners) + before.astype(jnp.int32) + after.astype(jnp.int32)
    )


class Gather:
    def __init__(self, place, shard, full, cols, send, recv, own):
        self.shard, self.own = shard.at[:, cols], own
        p, rows = place, shard.shape[0]
        half = rows // 2

        def block(y, x, part=slice(None)):
            return full.at[:, y, x, p.c, part, cols]

        mine = full.at[p.z, p.y, p.x, p.c, :, cols]
        self.local = lambda: pltpu.make_async_copy(self.shard, mine, own)

        def copy(i, src, dst, to):
            return lambda: mesh_copy(src, dst, send.at[i], recv.at[i], to)

        same = lambda i, ref, to: copy(i, ref, ref, to)
        first, second = pl.ds(0, half), pl.ds(half, half)
        self.z = [copy(i, self.shard, mine, to) for i, to in enumerate(p.zp)]
        self.xy = [same(3, block(p.y, p.x), p.xp), same(4, block(p.y, p.x), p.yp)]
        self.far = [
            same(5, block(p.y, 1 - p.x, first), p.yp),
            same(6, block(1 - p.y, p.x, second), p.xp),
        ]
        self.pair = [
            same(7, block(p.y, p.x), p.sib),
            same(8, block(p.y, 1 - p.x), p.sib),
            same(9, block(1 - p.y, p.x), p.sib),
            same(10, block(1 - p.y, 1 - p.x), p.sib),
        ]

    def stage(self, number):
        if number == 0:
            self.local().start()
            for c in self.z:
                c().start()
        elif number == 1:
            self.local().wait()
            for c in self.z:
                c().wait()
            for c in (*self.xy, self.pair[0]):
                c().start()
        elif number == 2:
            for c in self.xy:
                c().wait()
            for c in (*self.far, self.pair[1], self.pair[2]):
                c().start()
        elif number == 3:
            for c in self.far:
                c().wait()
            self.pair[3]().start()
        else:
            for c in self.pair:
                c().wait()


GATHER_SEMS = 11


def run_stages(pieces, tick, last):
    for at in range(last + 1):
        steps = [
            (s, piece)
            for k, piece in enumerate(pieces)
            for s in (4, 3, 2, 1, 0)
            if k + s == at
        ]
        if steps:
            @pl.when(tick == at)
            def _():
                for s, piece in steps:
                    piece.stage(s)


class Scatter:
    def __init__(self, place, grad, held, from_pair, far, side, line, out, sems):
        self.p, self.out = place, out
        self.held, self.from_pair, self.far, self.side, self.line = held, from_pair, far, side, line
        p, rows = place, held.shape[3]
        self.half = rows // 2
        own, send, recv = sems
        first, second = pl.ds(0, self.half), pl.ds(self.half, self.half)

        def copy(i, src, dst, to):
            return lambda: mesh_copy(src, dst, send.at[i], recv.at[i], to)

        self.load = lambda: pltpu.make_async_copy(grad.at[:, :, :, p.c], held, own)
        self.to_pair = copy(0, grad.at[:, :, :, 1 - p.c], from_pair, p.sib)
        self.to_far = [
            copy(1, held.at[:, 1 - p.y, 1 - p.x, first], far.at[0], p.xp),
            copy(2, held.at[:, 1 - p.y, 1 - p.x, second], far.at[1], p.yp),
        ]
        self.to_side = [
            copy(3, held.at[:, p.y, 1 - p.x], side.at[0], p.xp),
            copy(4, held.at[:, 1 - p.y, p.x], side.at[1], p.yp),
        ]
        self.to_line = [
            copy(5 + k, held.at[(p.z + k + 1) % 4, p.y, p.x], line.at[k], to)
            for k, to in enumerate(p.zp)
        ]

    def stage(self, number):
        p, half = self.p, self.half
        held, far, side, line = self.held, self.far, self.side, self.line
        if number == 0:
            self.load().start()
            self.to_pair().start()
        elif number == 1:
            self.load().wait()
            self.to_pair().wait()

            @pl.loop(0, 4)
            def _(z):
                for y in range(2):
                    for x in range(2):
                        held[z, y, x] = (
                            held[z, y, x].astype(F32) + self.from_pair[z, y, x].astype(F32)
                        ).astype(held.dtype)

            for c in self.to_far:
                c().start()
        elif number == 2:
            for c in self.to_far:
                c().wait()

            @pl.loop(0, 4)
            def _(z):
                held[z, 1 - p.y, p.x, :half] = (
                    held[z, 1 - p.y, p.x, :half].astype(F32) + far[0, z].astype(F32)
                ).astype(held.dtype)
                held[z, p.y, 1 - p.x, half:] = (
                    held[z, p.y, 1 - p.x, half:].astype(F32) + far[1, z].astype(F32)
                ).astype(held.dtype)

            for c in self.to_side:
                c().start()
        elif number == 3:
            for c in self.to_side:
                c().wait()

            @pl.loop(0, 4)
            def _(z):
                held[z, p.y, p.x] = (
                    held[z, p.y, p.x].astype(F32)
                    + side[0, z].astype(F32)
                    + side[1, z].astype(F32)
                ).astype(held.dtype)

            for c in self.to_line:
                c().start()
        else:
            for c in self.to_line:
                c().wait()
            self.out[...] = (
                held[p.z, p.y, p.x].astype(F32)
                + line[0].astype(F32)
                + line[1].astype(F32)
                + line[2].astype(F32)
            )


SCATTER_SEMS = 8
UNIT = 1024


def scatter_scratch(rows, cols, dtype=BF):
    return [
        pltpu.VMEM((4, 2, 2, rows, cols), dtype),
        pltpu.VMEM((4, 2, 2, rows, cols), dtype),
        pltpu.VMEM((2, 4, rows // 2, cols), dtype),
        pltpu.VMEM((2, 4, rows, cols), dtype),
        pltpu.VMEM((3, rows, cols), dtype),
        pltpu.SemaphoreType.DMA,
        pltpu.SemaphoreType.DMA((SCATTER_SEMS,)),
        pltpu.SemaphoreType.DMA((SCATTER_SEMS,)),
    ]


def blocks(value):
    return value.reshape(4, 2, 2, 2, value.shape[0] // 32, value.shape[1])


def gather_kernel(wide, vec, wide_out, vec_out, send, recv, own):
    place = Place()
    greet(place.partners)
    pieces = [Gather(place, vec, vec_out, pl.ds(0, vec.shape[1]), send.at[0], recv.at[0], own.at[0])]
    for k in range(wide.shape[1] // UNIT):
        pieces.append(
            Gather(
                place, wide, wide_out, pl.ds(k * UNIT, UNIT), send.at[k + 1], recv.at[k + 1],
                own.at[k + 1],
            )
        )
    for at in range(len(pieces) + 4):
        for s in (4, 3, 2, 1, 0):
            if 0 <= at - s < len(pieces):
                pieces[at - s].stage(s)


def gather_blocks(wide, vec):
    count = wide.shape[1] // UNIT + 1
    out = [
        jax.ShapeDtypeStruct((4, 2, 2, 2, *v.shape), v.dtype) for v in (wide, vec)
    ]
    hbm = pl.BlockSpec(memory_space=pl.ANY)
    full, small = pl.pallas_call(
        gather_kernel,
        out_shape=out,
        in_specs=[hbm, hbm],
        out_specs=[hbm, hbm],
        scratch_shapes=[
            pltpu.SemaphoreType.DMA((count, GATHER_SEMS)),
            pltpu.SemaphoreType.DMA((count, GATHER_SEMS)),
            pltpu.SemaphoreType.DMA((count,)),
        ],
        compiler_params=pltpu.CompilerParams(collective_id=0, has_side_effects=True),
        name="gather_qkv",
    )(wide, vec)
    return full.reshape(-1, wide.shape[1]), small.reshape(32, -1)


def scatter_kernel(g_q, g_k, g_v, small, out, small_out, *scratch):
    place = Place()
    greet(place.partners)
    size = 8
    pieces = []
    for k, grad in enumerate((g_q, g_k, g_v, small)):
        bufs = scratch[k * size : (k + 1) * size]
        to = small_out if k == 3 else out.at[:, pl.ds(k * UNIT, UNIT)]
        pieces.append(Scatter(place, grad, *bufs[:5], to, bufs[5:]))
    for at in range(len(pieces) + 4):
        for s in (4, 3, 2, 1, 0):
            if 0 <= at - s < len(pieces):
                pieces[at - s].stage(s)


def scatter_blocks(grads, small):
    hbm = pl.BlockSpec(memory_space=pl.ANY)
    vmem = pl.BlockSpec(memory_space=pltpu.VMEM)
    rows = grads[0].shape[0] // 32
    small = blocks(small)
    return pl.pallas_call(
        scatter_kernel,
        out_shape=[
            jax.ShapeDtypeStruct((rows, 3 * UNIT), F32),
            jax.ShapeDtypeStruct(small.shape[4:], F32),
        ],
        in_specs=[hbm] * 4,
        out_specs=[vmem] * 2,
        scratch_shapes=scatter_scratch(rows, UNIT) * 3
        + scatter_scratch(*small.shape[4:], F32),
        compiler_params=pltpu.CompilerParams(
            collective_id=3, has_side_effects=True, vmem_limit_bytes=40 * 2**20
        ),
        name="scatter_qkv",
    )(*map(blocks, grads), small)


ITEMS = 10


class Images:
    def __init__(self, n0, rows, ext):
        self.n0, self.n1, self.rows, self.ext = n0, n0 + IMG, rows, ext
        me, peers = lax.axis_index(AXIS), lax.axis_size(AXIS)
        limit = jnp.where(me == peers - 1, RIM + rows, 2 * RIM + rows)
        start0 = jnp.where(me == 0, RIM, n0 - 1)
        start1 = RIM + n0
        start2 = start1 + IMG
        self.spans = (
            (start0, start1),
            (start1, jnp.minimum(start1 + IMG, limit)),
            (start2, jnp.minimum(start2 + IMG, limit)),
        )
        one = lambda flag: jnp.where(flag, 1, 0)
        self.b0, self.b1 = lax.div(n0, QB), lax.div(self.n1, QB)
        self.d0 = one(self.b0 * QB != n0)
        self.d1 = one((self.n1 < rows) & (self.b1 * QB != self.n1))
        self.third = self.n1 < rows
        self.end0 = lax.div(n0 - 1, QB)
        self.end1 = lax.div(self.n1 - 1, QB) + self.d0
        self.one = one

    def base(self, start):
        return jnp.minimum(lax.div(start, 16), (self.ext - WIN) // 16)

    def segment(self, item):
        return self.one(item > self.end0) + self.one(item > self.end1)

    def item(self, item):
        blk = (
            item
            - self.d0 * self.one(item > self.b0)
            - self.d1 * self.one(item > self.b1 + self.d0)
        )
        used = blk < self.rows // QB
        blk = jnp.minimum(blk, self.rows // QB - 1)
        seg = self.segment(item)
        choose = lambda i: jnp.where(
            seg == 0, self.spans[0][i], jnp.where(seg == 1, self.spans[1][i], self.spans[2][i])
        )
        start, stop = choose(0), choose(1)
        base = self.base(start) * 16
        row0 = blk * QB
        low = jnp.maximum(start - RIM - row0, 0)
        high = jnp.where(used, jnp.minimum(stop - RIM - row0, QB), 0)
        return blk, row0, base, start - base, stop - base, low, high

    def of_block(self, blk):
        at0 = self.d0 * self.one(blk == self.b0)
        at1 = self.d1 * self.one(blk == self.b1)
        first = blk + self.d0 * self.one(blk > self.b0) + self.d1 * self.one(blk > self.b1)
        split = jnp.where(at0 == 1, self.n0, jnp.where(at1 == 1, self.n1, self.rows)) - blk * QB
        return first, first + at0 + at1, split


def attend_body(n0_ref, q_ref, k_ref, v_ref, out_ref, lse_ref, parts, parts_lse):
    rows = q_ref.shape[0]
    images = Images(n0_ref[0], rows, k_ref.shape[0])

    @pl.loop(0, ITEMS)
    def _(item):
        _, row0, base, low, high, _, _ = images.item(item)
        queries = stacked(q_ref[pl.ds(row0, QB), :]) * jnp.asarray(0.125, BF)
        keys = k_ref[pl.ds(base, WIN), :]
        values = v_ref[pl.ds(base, WIN), :]
        scores = jnp.where(key_mask(low, high), dot(keys, queries, NT), NEG)
        top = jnp.max(scores, axis=0, keepdims=True)
        terms = jnp.exp(scores - top)
        total = jnp.sum(terms, axis=0, keepdims=True)
        mixed = dot(values, terms.astype(BF), TN) / total
        parts[item] = unstacked(mixed)
        parts_lse[item] = jnp.broadcast_to(top + jnp.log(total), parts_lse.shape[1:])

    for blk in range(rows // QB):
        first, last, split = images.of_block(blk)
        row = lax.broadcasted_iota(jnp.int32, (QB, 2 * HDIM), 0)
        out_ref[pl.ds(blk * QB, QB), :] = jnp.where(
            row < split, parts[first], parts[last]
        ).astype(BF)
        lane = lax.broadcasted_iota(jnp.int32, parts_lse.shape[1:], 1) % QB
        lse_ref[0, pl.ds(blk, 1), :] = jnp.where(
            lane < split, parts_lse[first], parts_lse[last]
        )[:1]


def attend_kernel(n0_ref, q_ref, k_ref, v_ref, out_ref, lse_ref, parts, parts_lse):
    attend_body(n0_ref, q_ref, k_ref, v_ref, out_ref, lse_ref, parts, parts_lse)


def attend_gather_kernel(
    n0_ref, q_ref, k_ref, v_ref, w_out, w_up, out_ref, lse_ref, full_out, full_up,
    parts, parts_lse, send, recv, own,
):
    tick = pl.program_id(0)
    place = Place()
    pl.when(tick == 0)(lambda: greet(place.partners))
    pieces = []
    for shard, full in ((w_out, full_out), (w_up, full_up)):
        for k in range(shard.shape[1] // UNIT):
            i = len(pieces)
            pieces.append(
                Gather(
                    place, shard, full, pl.ds(k * UNIT, UNIT), send.at[i], recv.at[i], own.at[i]
                )
            )
    run_stages(pieces, tick, 7)
    attend_body(n0_ref, q_ref, k_ref, v_ref, out_ref, lse_ref, parts, parts_lse)

    @pl.when(tick == 7)
    def _():
        pieces[-1].stage(4)


def attend(n0, queries, key_value, shards=None):
    rows, width = queries.shape
    pairs = width // (2 * HDIM)
    ext = key_value.shape[0]
    hbm = pl.BlockSpec(memory_space=pl.ANY)
    in_specs = [
        pl.BlockSpec(memory_space=pltpu.SMEM),
        pl.BlockSpec((rows, 2 * HDIM), lambda p: (0, p)),
        pl.BlockSpec((ext, 2 * HDIM), lambda p: (0, p)),
        pl.BlockSpec((ext, 2 * HDIM), lambda p: (0, pairs + p)),
    ]
    out_specs = [
        pl.BlockSpec((rows, 2 * HDIM), lambda p: (0, p)),
        pl.BlockSpec((1, rows // QB, 2 * QB), lambda p: (p, 0, 0)),
    ]
    out_shape = [
        jax.ShapeDtypeStruct((rows, width), BF),
        jax.ShapeDtypeStruct((pairs, rows // QB, 2 * QB), F32),
    ]
    scratch = [
        pltpu.VMEM((ITEMS, QB, 2 * HDIM), F32),
        pltpu.VMEM((ITEMS, 8, 2 * QB), F32),
    ]
    params = dict(vmem_limit_bytes=48 * 2**20)
    args = [n0, queries, key_value, key_value]
    kernel = attend_kernel
    if shards is not None:
        kernel = attend_gather_kernel
        in_specs += [hbm] * 2
        out_specs += [hbm] * 2
        out_shape += [jax.ShapeDtypeStruct((4, 2, 2, 2, *v.shape), BF) for v in shards]
        count = sum(v.shape[1] // UNIT for v in shards)
        scratch += [
            pltpu.SemaphoreType.DMA((count, GATHER_SEMS)),
            pltpu.SemaphoreType.DMA((count, GATHER_SEMS)),
            pltpu.SemaphoreType.DMA((count,)),
        ]
        params |= dict(collective_id=1, has_side_effects=True)
        args += shards
    return pl.pallas_call(
        kernel,
        grid=(pairs,),
        in_specs=in_specs,
        out_specs=out_specs,
        out_shape=out_shape,
        scratch_shapes=scratch,
        compiler_params=pltpu.CompilerParams(**params),
        name="attend",
    )(*args)


TILE = 64


def attend_back_body(
    pair, pairs, n0_ref, q_ref, k_ref, v_ref, up_ref, lse_ref, dq_ref, dk_ref, dv_ref,
    slots, parts, padded, outgoing, incoming, send, recv,
):
    rows = q_ref.shape[0]
    images = Images(n0_ref[0], rows, k_ref.shape[0])
    me, peers = lax.axis_index(AXIS), lax.axis_size(AXIS)
    wide = slice(TILE, TILE + WIN)

    def halo(p, way):
        return mesh_copy(
            outgoing.at[p, way], incoming.at[p, way], send.at[p, way], recv.at[p, way],
            me - 1 if way == 0 else me + 1,
        )

    @pl.when(pair == 0)
    def _():
        slots[0] = jnp.zeros(slots.shape[1:], F32)
        padded[...] = jnp.zeros(padded.shape, F32)

        @pl.when(me == 0)
        def _():
            incoming[:, 1] = jnp.zeros((pairs, WIN, 4 * HDIM), BF)

        @pl.when(me == peers - 1)
        def _():
            incoming[:, 0] = jnp.zeros((pairs, WIN, 4 * HDIM), BF)

    @pl.when(pair < pairs)
    def _():
        @pl.loop(0, ITEMS)
        def _(item):
            blk, row0, base, low, high, first, stop = images.item(item)
            queries = stacked(q_ref[pl.ds(row0, QB), :]) * jnp.asarray(0.125, BF)
            upstream = stacked(up_ref[pl.ds(row0, QB), :])
            lane = lax.broadcasted_iota(jnp.int32, (1, 2 * QB), 1) % QB
            here = (lane >= first) & (lane < stop)
            lse = jnp.where(here, lse_ref[0, pl.ds(blk, 1), :], -NEG)
            keys = k_ref[pl.ds(base, WIN), :]
            values = v_ref[pl.ds(base, WIN), :]
            scores = jnp.where(key_mask(low, high), dot(keys, queries, NT), NEG)
            probs = jnp.exp(scores - lse)
            dprobs = dot(values, upstream, NT)
            row_dot = jnp.sum(probs * dprobs, axis=0, keepdims=True)
            dscores = (probs * (dprobs - row_dot)).astype(BF)
            same = images.segment(item) == images.segment(item - 1)
            keep = (item > 0) & same
            old = jnp.where(keep, slots[item], jnp.zeros(slots.shape[1:], F32))
            slots[item + 1, :, : 2 * HDIM] = old[:, : 2 * HDIM] + dot(dscores, queries)
            slots[item + 1, :, 2 * HDIM :] = old[:, 2 * HDIM :] + dot(probs.astype(BF), upstream)
            parts[item] = unstacked(dot(keys, dscores, TN)) * 0.125

        for blk in range(rows // QB):
            first, last, split = images.of_block(blk)
            row = lax.broadcasted_iota(jnp.int32, (QB, 2 * HDIM), 0)
            dq_ref[pl.ds(blk * QB, QB), :] = jnp.where(
                row < split, parts[first], parts[last]
            ).astype(BF)

    @pl.when(pair > 0)
    def _():
        done = pair - 1

        @pl.when(me > 0)
        def _():
            halo(done, 0).wait_send()

        @pl.when(me < peers - 1)
        def _():
            halo(done, 0).wait_recv()
            halo(done, 1).wait_send()

        @pl.when(me > 0)
        def _():
            halo(done, 1).wait_recv()

        none = jnp.zeros((WIN, 4 * HDIM), F32)
        last = jnp.where(images.third, 2, 1)
        stop = jnp.where(images.third, images.spans[2][1], images.spans[1][1])
        cut = (stop > RIM + rows) & (me < peers - 1)
        after = jnp.where(cut, incoming[done, 0].astype(F32), none)
        before = jnp.where(images.spans[0][0] < RIM, incoming[done, 1].astype(F32), none)
        padded[0, wide] = padded[0, wide] + before
        padded[1, wide] = padded[1, wide] + jnp.where(last == 1, after, none)
        padded[2, wide] = padded[2, wide] + jnp.where(last == 2, after, none)
        bases = [images.base(span[0]) for span in images.spans]

        @pl.loop(0, rows // TILE)
        def _(tile):
            row = pl.multiple_of(tile * TILE, TILE)
            total = None
            for seg, base in enumerate(bases):
                off = jnp.maximum((RIM + TILE) // 16 + tile * (TILE // 16) - base, 0)
                off = jnp.minimum(off, (WIN + TILE) // 16) * 16
                term = padded[seg, pl.ds(off, TILE), :]
                total = term if total is None else total + term
            dk_ref[pl.ds(row, TILE), :] = total[:, : 2 * HDIM].astype(BF)
            dv_ref[pl.ds(row, TILE), :] = total[:, 2 * HDIM :].astype(BF)

    @pl.when(pair < pairs)
    def _():
        ends = (
            images.end0 + 1,
            jnp.minimum(images.end1, (rows - 1) // QB + images.d0) + 1,
            jnp.where(images.third, ITEMS, 0),
        )
        for seg, end in enumerate(ends):
            padded[seg, wide] = slots[end]
        outgoing[pair, 0] = padded[0, wide].astype(BF)
        outgoing[pair, 1] = jnp.where(images.third, padded[2, wide], padded[1, wide]).astype(BF)

        @pl.when(me > 0)
        def _():
            halo(pair, 0).start()

        @pl.when(me < peers - 1)
        def _():
            halo(pair, 1).start()


def attend_back_kernel(pairs, *refs):
    me, peers = lax.axis_index(AXIS), lax.axis_size(AXIS)
    pair = pl.program_id(0)
    pl.when(pair == 0)(lambda: greet([], me > 0, me < peers - 1))
    attend_back_body(pair, pairs, *refs)


def attend_back_scatter_kernel(pairs, *refs):
    base, (g_out, g_up), rest = refs[:6], refs[6:8], refs[8:]
    outs, (r_out, r_up), scratch = rest[:3], rest[3:5], rest[5:]
    mine, comm = scratch[:7], scratch[7:]
    me, peers = lax.axis_index(AXIS), lax.axis_size(AXIS)
    pair = pl.program_id(0)
    place = Place()
    pl.when(pair == 0)(lambda: greet(place.partners, me > 0, me < peers - 1))
    pieces = []
    for grad, out in ((g_out, r_out), (g_up, r_up)):
        for k in range(grad.shape[5] // UNIT):
            cols = pl.ds(k * UNIT, UNIT)
            bufs = comm[len(pieces) * 8 : len(pieces) * 8 + 8]
            pieces.append(
                Scatter(
                    place, grad.at[:, :, :, :, :, cols], *bufs[:5], out.at[:, cols], bufs[5:]
                )
            )
    run_stages(pieces, pair, pairs)
    attend_back_body(pair, pairs, *base, *outs, *mine)


def attend_back(n0, queries, key_value, upstream, lse, grads=None):
    rows, width = queries.shape
    pairs = width // (2 * HDIM)
    ext = key_value.shape[0]
    hbm, vmem = pl.BlockSpec(memory_space=pl.ANY), pl.BlockSpec(memory_space=pltpu.VMEM)
    here = lambda p: jnp.minimum(p, pairs - 1)
    own = pl.BlockSpec((rows, 2 * HDIM), lambda p: (0, here(p)))
    late = pl.BlockSpec((rows, 2 * HDIM), lambda p: (0, jnp.maximum(p - 1, 0)))
    in_specs = [
        pl.BlockSpec(memory_space=pltpu.SMEM),
        own,
        pl.BlockSpec((ext, 2 * HDIM), lambda p: (0, here(p))),
        pl.BlockSpec((ext, 2 * HDIM), lambda p: (0, pairs + here(p))),
        own,
        pl.BlockSpec((1, rows // QB, 2 * QB), lambda p: (here(p), 0, 0)),
    ]
    out_specs = [own, late, late]
    out_shape = [jax.ShapeDtypeStruct((rows, width), BF)] * 3
    scratch = [
        pltpu.VMEM((ITEMS + 1, WIN, 4 * HDIM), F32),
        pltpu.VMEM((ITEMS, QB, 2 * HDIM), F32),
        pltpu.VMEM((3, WIN + 2 * TILE, 4 * HDIM), F32),
        pltpu.VMEM((pairs, 2, WIN, 4 * HDIM), BF),
        pltpu.VMEM((pairs, 2, WIN, 4 * HDIM), BF),
        pltpu.SemaphoreType.DMA((pairs, 2)),
        pltpu.SemaphoreType.DMA((pairs, 2)),
    ]
    args = [n0, queries, key_value, key_value, upstream, lse]
    kernel, collective = attend_back_kernel, 4
    if grads is not None:
        kernel, collective = attend_back_scatter_kernel, 2
        args += map(blocks, grads)
        in_specs += [hbm] * 2
        out_specs += [vmem] * 2
        out_shape += [jax.ShapeDtypeStruct((v.shape[0] // 32, v.shape[1]), F32) for v in grads]
        for v in grads:
            scratch += scatter_scratch(v.shape[0] // 32, UNIT) * (v.shape[1] // UNIT)
    return pl.pallas_call(
        functools.partial(kernel, pairs),
        grid=(pairs + 1,),
        in_specs=in_specs,
        out_specs=out_specs,
        out_shape=out_shape,
        scratch_shapes=scratch,
        compiler_params=pltpu.CompilerParams(
            vmem_limit_bytes=58 * 2**20, collective_id=collective, has_side_effects=True
        ),
        name="attend_back",
    )(*args)


def shifted(value, by):
    peers = lax.axis_size(AXIS)
    pairs = [(i, i + by) for i in range(peers) if 0 <= i + by < peers]
    return lax.ppermute(value, AXIS, pairs)


def gathered(value):
    return lax.all_gather(value, AXIS, axis=0, tiled=True)


def scattered(value):
    return lax.psum_scatter(value, AXIS, scatter_dimension=0, tiled=True)


def normalize(inputs, gain, shift):
    center = inputs - jnp.mean(inputs, axis=1, keepdims=True)
    inv_std = lax.rsqrt(jnp.mean(center * center, axis=1, keepdims=True) + EPS)
    scaled = center * inv_std
    return (scaled * gain + shift, scaled, inv_std)


def normalize_back(upstream, scaled, inv_std, gain):
    through = upstream * gain
    inner = (
        through
        - jnp.mean(through, axis=1, keepdims=True)
        - scaled * jnp.mean(through * scaled, axis=1, keepdims=True)
    )
    return (inv_std * inner, jnp.sum(upstream * scaled, axis=0), jnp.sum(upstream, axis=0))


def local(
    tokens,
    image_ids,
    cotangent,
    norm1_gain,
    norm1_shift,
    qkv_weight,
    query_bias,
    value_bias,
    out_weight,
    out_bias,
    norm2_gain,
    norm2_shift,
    up_weight,
    up_bias,
    down_weight,
    down_bias,
):
    rows, width = tokens.shape
    me = lax.axis_index(AXIS)
    peers = lax.axis_size(AXIS)
    n0 = jnp.sum((image_ids == image_ids[0]).astype(jnp.int32)).reshape(1)
    ext = -(-(rows + 2 * RIM + 64) // 128) * 128
    packed = jnp.concatenate(
        [norm1_gain, norm1_shift, query_bias, value_bias, out_bias, norm2_gain, norm2_shift,
         down_bias, up_bias]
    )
    block_plan = peers == 32
    if block_plan:
        count = packed.shape[0]
        packed = jnp.pad(packed, (0, 32 * 128 - count)).reshape(32, 128)
        w_qkv, vectors = gather_blocks(qkv_weight, packed)
        vectors = vectors[:, :count].astype(F32)
    else:
        w_qkv, vectors = gathered(qkv_weight), gathered(packed[None]).astype(F32)
        w_out, w_up = gathered(out_weight), gathered(up_weight)
    w_down = gathered(down_weight)
    part = norm1_gain.shape[0]
    gain1, shift1, q_bias, v_bias, o_bias, gain2, shift2, d_bias = (
        vectors[:, i * part : (i + 1) * part].reshape(-1) for i in range(8)
    )
    u_bias = vectors[:, 8 * part :].reshape(-1)

    low_rim = shifted(tokens[rows - RIM :], 1)
    high_rim = shifted(tokens[:RIM], -1)
    pad = jnp.zeros((ext - rows - 2 * RIM, width), BF)
    tokens_ext = jnp.concatenate([low_rim, tokens, high_rim, pad], axis=0).astype(F32)
    inputs = tokens.astype(F32)
    normed_ext = normalize(tokens_ext, gain1, shift1)[0].astype(BF)
    normed, scaled_one, inv_one = normalize(inputs, gain1, shift1)
    normed_low = normed.astype(BF)
    queries = (dot(normed_low, w_qkv[:, :width]) + q_bias).astype(BF)
    key_value = (
        dot(normed_ext, w_qkv[:, width:]) + jnp.concatenate([jnp.zeros_like(v_bias), v_bias])
    ).astype(BF)
    if block_plan:
        mixed_low, lse, w_out, w_up = attend(
            n0, queries, key_value, (out_weight, up_weight)
        )
        w_out, w_up = w_out.reshape(width, -1), w_up.reshape(width, -1)
    else:
        mixed_low, lse = attend(n0, queries, key_value)

    resid = inputs + dot(mixed_low, w_out) + o_bias
    normed_two, scaled_two, inv_two = normalize(resid, gain2, shift2)
    normed_two_low = normed_two.astype(BF)
    upward = dot(normed_two_low, w_up) + u_bias
    normal_cdf = 0.5 * (1.0 + lax.erf(upward * (1.0 / math.sqrt(2.0))))
    activated_low = (upward * normal_cdf).astype(BF)
    layer_out = (resid + dot(activated_low, w_down) + d_bias).astype(BF)

    upstream_out = cotangent.astype(F32)
    grad_down = dot(activated_low, cotangent, TN)
    grad_down_b = jnp.sum(upstream_out, axis=0)
    normal_pdf = jnp.exp(-0.5 * upward * upward) * (1.0 / math.sqrt(2.0 * math.pi))
    dupward_low = (dot(cotangent, w_down, NT) * (normal_cdf + upward * normal_pdf)).astype(BF)
    grad_up = dot(normed_two_low, dupward_low, TN)
    grad_up_b = jnp.sum(dupward_low.astype(F32), axis=0)
    dnormed_two = dot(dupward_low, w_up, NT)
    dresid_norm, grad_gain_two, grad_shift_two = normalize_back(
        dnormed_two, scaled_two, inv_two, gain2
    )
    dresid = upstream_out + dresid_norm
    dbranch_low = dresid.astype(BF)
    grad_out = dot(mixed_low, dbranch_low, TN)
    grad_out_b = jnp.sum(dbranch_low.astype(F32), axis=0)
    dmixed_low = dot(dbranch_low, w_out, NT).astype(BF)

    grad_out, grad_up = grad_out.astype(BF), grad_up.astype(BF)
    r_down = scattered(grad_down.astype(BF)).astype(F32)
    if block_plan:
        dquery, dkey, dvalue, r_out, r_up = attend_back(
            n0, queries, key_value, dmixed_low, lse, (grad_out, grad_up)
        )
    else:
        dquery, dkey, dvalue = attend_back(n0, queries, key_value, dmixed_low, lse)
        r_out, r_up = (scattered(v).astype(F32) for v in (grad_out, grad_up))
    dproj = (dquery, dkey, dvalue)
    grad_qkv = [dot(normed_low, v, TN).astype(BF) for v in dproj]
    grad_query_b = jnp.sum(dquery.astype(F32), axis=0)
    grad_value_b = jnp.sum(dvalue.astype(F32), axis=0)
    dnormed = sum(
        dot(v, w_qkv[:, i * width : (i + 1) * width], NT) for i, v in enumerate(dproj)
    )
    dinput_norm, grad_gain_one, grad_shift_one = normalize_back(
        dnormed, scaled_one, inv_one, gain1
    )
    grad_tokens = dresid + dinput_norm

    def small(value):
        return value.reshape(peers, -1)

    smalls = jnp.concatenate(
        [
            small(v)
            for v in (
                grad_gain_one, grad_shift_one, grad_query_b, grad_value_b, grad_out_b,
                grad_gain_two, grad_shift_two, grad_down_b, grad_up_b,
            )
        ],
        axis=1,
    )
    if block_plan:
        count = smalls.shape[1]
        smalls = jnp.pad(smalls, ((0, 0), (0, 16 * 128 - count))).reshape(peers * 16, 128)
        r_qkv, owned = scatter_blocks(grad_qkv, smalls)
        owned = owned.reshape(-1)[:count]
    else:
        owned = scattered(smalls)[0]
        r_qkv = jnp.concatenate([scattered(v) for v in grad_qkv], axis=1).astype(F32)
    g = [owned[i * part : (i + 1) * part] for i in range(8)] + [owned[8 * part :]]
    return (
        layer_out, grad_tokens, g[0], g[1], r_qkv, g[2], g[3], r_out, g[4], g[5], g[6], r_up,
        g[8], r_down, g[7],
    )


def solution(mesh):
    row, vec = P(AXIS, None), P(AXIS)
    return jax.shard_map(
        local,
        mesh=mesh,
        in_specs=(
            row, vec, row, vec, vec, row, vec, vec, row, vec, vec, vec, row, vec, row, vec,
        ),
        out_specs=(
            row, row, vec, vec, row, vec, vec, row, vec, vec, vec, row, vec, row, vec,
        ),
        check_vma=False,
    )
```

time: 1040 us -> 594 us (0.57)
  waiting for transfers between devices: 453 us -> 0.73 us
  Pallas kernels: 128 us -> 353 us
  blocking collectives: 158 us -> 0 us
  local copies, waits for them, and re-layouts: 67.1 us -> 32.7 us
  other arithmetic: 51.6 us -> 26.5 us
    reduce_scatter x4 -> x1, waiting for transfers between devices: 358 us -> 0.01 us  [scattered(): return lax.psum_scatter(value, AXIS, scatter_dimension=0, tiled=True)]
    pallas_call x2 -> x4, Pallas kernels: 128 us -> 353 us  [the longest x1 145 us: attend_back(): pl.pallas_call(functools.partial(kernel, pairs), grid=(pairs + 1,), in_sp...]
    all_gather x4 -> x1, waiting for transfers between devices: 91.8 us -> 0.02 us  [gathered(): return lax.all_gather(value, AXIS, axis=0, tiled=True)]
    unnamed x1 -> x0, blocking collectives: 89.2 us -> none
    all_gather x1 -> x0, blocking collectives: 69.1 us -> none  [gathered(): return lax.all_gather(value, AXIS, axis=0, tiled=True)]
    unnamed x95 -> x94, local copies, waits for them, and re-layouts: 38 us -> 19.6 us
    dot_general x13 -> x17, matrix products: 148 us -> 153 us  [dot(): return lax.dot_general(a, b, dims, preferred_element_type=F32)]
  transfers between devices with their start and end apart: 12 -> 4, of which waited for: 5 -> 0; matrix products, arithmetic and copies ran while one was open for 17% -> 35% of each run, Pallas kernels for 6% -> 60%
where the time goes in v2:
time: 594 us; the launch traced here: 585 us
  Pallas kernels  353 us (59%)
  matrix products  153 us (26%)
  local copies, waits for them, and re-layouts  32.7 us (6%)
  other arithmetic  26.5 us (4%)
  between operations  15.5 us (3%)
    dot_general x17, matrix products, dot(): return lax.dot_general(a, b, dims, preferred_element_type=F32)  153 us
    pallas_call x1, Pallas kernels, attend_back(): pl.pallas_call(functools.partial(kernel, pairs), grid=(pairs + 1,), in_sp...  145 us
    pallas_call x1, Pallas kernels, gather_blocks(): pl.pallas_call(gather_kernel, out_shape=out, in_specs=[hbm, hbm], out_spe...  79.6 us
    pallas_call x1, Pallas kernels, attend(): pl.pallas_call(kernel, grid=(pairs,), in_specs=in_specs, out_specs=out_sp...  77.5 us
    pallas_call x1, Pallas kernels, scatter_blocks(): pl.pallas_call(scatter_kernel, out_shape=[jax.ShapeDtypeStruct((rows, 3 *...  50.9 us
    unnamed x94, local copies, waits for them, and re-layouts  19.6 us
  transfers between devices with their start and end apart: 4, of which 0 were waited for; matrix products, arithmetic and copies ran while one was open for 35% of the time, Pallas kernels for 60%

profile of v2, /device:TPU:0, one launch (start us, length us, event | category | flops | bytes accessed | tf_op | source)
XLA Modules:
  0.0 585.5 jit_solution(1432171342637239337)
XLA Ops:
  18.8 79.6 %gather_qkv.1 = (bf16[4,2,2,2,32,3072]{5,4,3,2,1,0:T(8,128)(2,1)}, bf16[4,2,2,2,32,128]{5,4,3,2,1,0:T(8,128)(2,1)}) custom-call(bf16[32,3072]{1,0:T(8,128)(2,1)} %wide.1, bf16[32,128]{1,0:T(8,128)(2,1)} %pad_bitcast_fusion.1.vec), custom_call_target="tpu_custom_call" | custom-call | tf_op jit(solution)/shard_map/gather_qkv/pallas_call | solution.py:298
  103.0 4.0 copy.33
  107.6 5.7 add_convert_fusion.3.q_ref.refs_1_
  113.4 4.4 convert_reduce_fusion.1
  119.3 15.1 %add_convert_fusion.k_ref.v_ref.refs_2_.refs_3_ = bf16[2304,2048]{1,0:T(8,128)(2,1)} fusion(f32[2048]{0:T(1024)S(1)} %concatenate.14, bf16[2304,1024]{1,0:T(8,128)(2,1)S(1)} %get-tuple-element.66, f32[1024]{0:T(1024)S(1)} %add.139, f32[1024]{0:T(1024)S(1)} %mul.152, f32[2304]{0:T(1024)S(1)} %add_rsqrt_fusion, f32[2304]{0:T(1024)S(1)} %broadcast_multiply_fusion, ...), kind=kOutput, calls=%fused_computation.1 | convolution fusion | flops 9687269376 | bytes 18384896 | tf_op jit(solution)/shard_map/dot_general | solution.py:27
  134.4 77.5 %attend.1 = (bf16[1024,1024]{1,0:T(8,128)(2,1)S(1)}, f32[8,8,256]{2,1,0:T(8,128)S(1)}, bf16[4,2,2,2,32,1024]{5,4,3,2,1,0:T(8,128)(2,1)S(1)}, bf16[4,2,2,2,32,4096]{5,4,3,2,1,0:T(8,128)(2,1)}) custom-call(s32[1]{0:T(128)} %bitcast.1.n0_ref.refs_0_, bf16[1024,1024]{1,0:T(8,128)(2,1)} %add_convert_fusion.3.q_ref.refs_1_, ...), custom_call_target="tpu_custom_call" | custom-call | tf_op jit(solution)/shard_map/attend/pallas_call | solution.py:506
  215.1 19.7 %multiply_convert_fusion = (bf16[1024,4096]{1,0:T(8,128)(2,1)}, f32[1024,4096]{1,0:T(8,128)}) fusion(f32[4096]{0:T(1024)S(1)} %slice_bitcast_fusion, bf16[1024,4096]{1,0:T(8,128)(2,1)} %bitcast.59, f32[1024,1024]{0,1:T(8,128)S(1)} %get-tuple-element.87, f32[1024]{0:T(1024)S(1)} %add.156, f32[1024]{0:T(1024)S(1)} %mul.163, f32[1024]{0:T(1024)S(1)} %add_rsqrt_fusion.1, ...), kind=kOutput, calls=%fused_computation.9 | convolution fusion | flops 8620343296 | bytes 37781504 | tf_op jit(solution)/shard_map/dot_general | solution.py:27
  234.8 15.0 %convolution_convert_fusion = bf16[4096,1024]{1,0:T(8,128)(2,1)} fusion(bf16[1024,4096]{1,0:T(8,128)(2,1)} %get-tuple-element.93, bf16[1024,1024]{1,0:T(8,128)(2,1)S(1)} %copy-done.15), kind=kOutput, calls=%fused_computation.19 | convolution fusion | flops 8594128896 | bytes 18874368 | tf_op jit(solution)/shard_map/dot_general | solution.py:27
  249.9 18.1 %convert_reduce_fusion = (f32[4096]{0:T(1024)S(1)}, bf16[1024,4096]{1,0:T(8,128)(2,1)S(1)}) fusion(f32[1024,4096]{1,0:T(8,128)} %get-tuple-element.94, f32[4096]{0:T(1024)S(1)} %slice_bitcast_fusion, bf16[1024,1024]{1,0:T(8,128)(2,1)} %param.18, bf16[4096,1024]{1,0:T(8,128)(2,1)} %all-gather.2.cloned.1.call-done), kind=kOutput, calls=%fused_computation.8 | convolution fusion | flops 8644456448 | bytes 35684352 | tf_op jit(solution)/shard_map/dot_general | solution.py:27
  268.0 15.6 %fusion.50 = (f32[1024]{0:T(1024)S(1)}, f32[1024,1024]{1,0:T(8,128)}) fusion(bf16[1024,4096]{1,0:T(8,128)(2,1)S(1)} %get-tuple-element.92, bf16[1024,4096]{1,0:T(8,128)(2,1)} %bitcast.60), kind=kOutput, calls=%fused_computation.96 | convolution fusion | flops 8590982144 | bytes 20975616 | tf_op jit(solution)/shard_map/dot_general | solution.py:27
  283.6 5.5 copy.34
  289.1 4.7 multiply_reduce_fusion
  295.1 4.2 convert_reduce_fusion.4
  299.4 3.8 convolution_convert_fusion.5
  303.1 3.7 convolution_convert_fusion.6.refs_4_
  306.8 15.0 %convolution_convert_fusion.1 = bf16[1024,4096]{1,0:T(8,128)(2,1)} fusion(bf16[1024,4096]{1,0:T(8,128)(2,1)} %copy-done.41, f32[1024,1024]{0,1:T(8,128)S(1)} %copy-done.6, f32[1024]{0:T(1024)S(1)} %add.156, f32[1024]{0:T(1024)S(1)} %mul.163, f32[1024]{0:T(1024)S(1)} %add_rsqrt_fusion.1, f32[1024]{0:T(1024)S(1)} %broadcast_multiply_fusion.5), kind=kOutput, calls=%fused_computation.20 | convolution fusion | flops 8599371776 | bytes 20987904 | tf_op jit(solution)/shard_map/dot_general | solution.py:27
  321.8 144.7 %attend_back.1 = (bf16[1024,1024]{1,0:T(8,128)(2,1)}, bf16[1024,1024]{1,0:T(8,128)(2,1)}, bf16[1024,1024]{1,0:T(8,128)(2,1)}, f32[32,1024]{1,0:T(8,128)}, f32[32,4096]{1,0:T(8,128)}) custom-call(s32[1]{0:T(128)} %bitcast.1.n0_ref.refs_0_, bf16[1024,1024]{1,0:T(8,128)(2,1)} %add_convert_fusion.3.q_ref.refs_1_, ...), custom_call_target="tpu_custom_call" | custom-call | tf_op jit(solution)/shard_map/attend_back/pallas_call | solution.py:707
  466.6 4.7 fusion.35
  471.4 4.1 fusion.33
  475.6 7.0 %fusion.29 = (f32[1024]{0:T(1024)S(1)}, f32[1024]{0:T(1024)S(1)}, f32[1024]{0:T(1024)S(1)}, f32[1024]{0:T(1024)S(1)}, f32[1024,1024]{0,1:T(8,128)}) fusion(bf16[1024,1024]{0,1:T(8,128)(2,1)S(1)} %copy-done.10, f32[1024]{0:T(1024)S(1)} %copy-done.27, f32[1024]{0:T(1024)S(1)} %copy-done.23, f32[1024]{0:T(1024)S(1)} %copy-done.25, ...), kind=kOutput, calls=%fused_computation.43 | convolution fusion | flops 2160062464 | bytes 18903040 | tf_op jit(solution)/shard_map/dot_general | solution.py:27
  487.2 4.1 convolution_convert_fusion.3
  496.5 50.9 %scatter_qkv.1 = (f32[32,3072]{1,0:T(8,128)S(1)}, f32[16,128]{1,0:T(8,128)S(1)}) custom-call(bf16[4,2,2,2,32,1024]{5,4,3,2,1,0:T(8,128)(2,1)S(1)} %bitcast.50, bf16[4,2,2,2,32,1024]{5,4,3,2,1,0:T(8,128)(2,1)S(1)} %bitcast.48, bf16[4,2,2,2,32,1024]{5,4,3,2,1,0:T(8,128)(2,1)S(1)} %bitcast.49, f32[4,2,2,2,16,128]{5,4,3,2,1,0:T(8,128)S(1)} %bitcast.51), custom_call_target="tpu_custom_call" | custom-call | tf_op jit(solution)/shard_map/scatter_qkv/pallas_call | solution.py:334
  550.8 5.3 copy.40
  556.1 14.4 %add_convert_fusion.1 = bf16[1024,1024]{0,1:T(8,128)(2,1)S(1)} fusion(f32[1024,1024]{0,1:T(8,128)} %copy-done.5, f32[1024]{0:T(1024)S(1)} %copy-done.28, bf16[1024,4096]{1,0:T(8,128)(2,1)} %get-tuple-element.93, bf16[4096,1024]{1,0:T(8,128)(2,1)} %all-gather.2.cloned.1.call-done), kind=kOutput, calls=%fused_computation.53 | convolution fusion | flops 8593080320 | bytes 23072768 | tf_op jit(solution)/shard_map/dot_general | solution.py:27
  (153 shorter events, 43.0 us)
Async XLA Ops:
  7.2 242.7 %all-gather.2.cloned.1.call-start = ((), (), s32[]{:S(2)}) async-start(), calls=%async_computation.1 | async-start | bytes 8650752 | tf_op jit(solution)/shard_map/all_gather | solution.py:728
  7.9 10.0 %copy-start.32 = (bf16[32]{0:T(256)(128)(2,1)S(1)}, bf16[32]{0:T(256)(128)(2,1)}, u32[]{:S(2)}) copy-start(bf16[32]{0:T(256)(128)(2,1)} %param.19) | copy-start | bytes 196
  7.9 10.0 %copy-start.33 = (bf16[32]{0:T(256)(128)(2,1)S(1)}, bf16[32]{0:T(256)(128)(2,1)}, u32[]{:S(2)}) copy-start(bf16[32]{0:T(256)(128)(2,1)} %param.20) | copy-start | bytes 196
  7.9 10.0 %copy-start.34 = (bf16[32]{0:T(256)(128)(2,1)S(1)}, bf16[32]{0:T(256)(128)(2,1)}, u32[]{:S(2)}) copy-start(bf16[32]{0:T(256)(128)(2,1)} %param.22) | copy-start | bytes 196
  7.9 10.0 %copy-start.35 = (bf16[32]{0:T(256)(128)(2,1)S(1)}, bf16[32]{0:T(256)(128)(2,1)}, u32[]{:S(2)}) copy-start(bf16[32]{0:T(256)(128)(2,1)} %param.23) | copy-start | bytes 196
  8.0 10.0 %copy-start.36 = (bf16[32]{0:T(256)(128)(2,1)S(1)}, bf16[32]{0:T(256)(128)(2,1)}, u32[]{:S(2)}) copy-start(bf16[32]{0:T(256)(128)(2,1)} %param.25) | copy-start | bytes 196
  8.0 10.0 %copy-start.37 = (bf16[32]{0:T(256)(128)(2,1)S(1)}, bf16[32]{0:T(256)(128)(2,1)}, u32[]{:S(2)}) copy-start(bf16[32]{0:T(256)(128)(2,1)} %param.26) | copy-start | bytes 196
  8.0 10.0 %copy-start.38 = (bf16[32]{0:T(256)(128)(2,1)S(1)}, bf16[32]{0:T(256)(128)(2,1)}, u32[]{:S(2)}) copy-start(bf16[32]{0:T(256)(128)(2,1)} %param.27) | copy-start | bytes 196
  8.0 91.5 %copy-start.31 = (s32[1024]{0:T(1024)S(1)}, s32[1024]{0:T(1024)}, u32[]{:S(2)}) copy-start(s32[1024]{0:T(1024)} %param.17) | copy-start | bytes 12292
  8.0 566.2 %reduce-scatter.2.cloned.1.call-start = ((), (), s32[]{:S(2)}) async-start(), calls=%async_computation.2 | async-start | bytes 8650752 | tf_op jit(solution)/shard_map/reduce_scatter | solution.py:732
  11.3 102.1 %collective-permute-start = (bf16[576,1024]{1,0:T(8,128)(2,1)}, bf16[576,1024]{1,0:T(8,128)(2,1)S(1)}, u32[]{:S(2)}, u32[]{:S(2)}) collective-permute-start(bf16[576,1024]{1,0:T(8,128)(2,1)} %get-tuple-element.68), channel_id=1, source_target_pairs={{0,1},{1,2},{2,3},{3,4},{4,5},{5,6},{6,7},{7,8},{8,9},{9,10},{10,1... | collective-permute-start | bytes 3538952 | tf_op jit(solution)/shard_map/ppermute | solution.py:724
  13.7 99.7 %collective-permute-start.1 = (bf16[576,1024]{1,0:T(8,128)(2,1)}, bf16[576,1024]{1,0:T(8,128)(2,1)}, u32[]{:S(2)}, u32[]{:S(2)}) collective-permute-start(bf16[576,1024]{1,0:T(8,128)(2,1)} %get-tuple-element.69), channel_id=1, source_target_pairs={{1,0},{2,1},{3,2},{4,3},{5,4},{6,5},{7,6},{8,7},{9,8},{10,9},{11,1... | collective-permute-start | bytes 3538952 | tf_op jit(solution)/shard_map/ppermute | solution.py:724
  18.0 89.6 %copy-start.8 = (bf16[1024,1024]{0,1:T(8,128)(2,1)}, bf16[1024,1024]{0,1:T(8,128)(2,1)S(1)}, u32[]{:S(2)}) copy-start(bf16[1024,1024]{0,1:T(8,128)(2,1)S(1)} %copy.31) | copy-start | bytes 6291460
  100.4 12.9 %copy-start.22 = (f32[1024]{0:T(1024)}, f32[1024]{0:T(1024)S(1)}, u32[]{:S(2)}) copy-start(f32[1024]{0:T(1024)S(1)} %broadcast_multiply_fusion.6) | copy-start | bytes 12292
  102.5 16.8 %copy-start.24 = (f32[1024]{0:T(1024)}, f32[1024]{0:T(1024)S(1)}, u32[]{:S(2)}) copy-start(f32[1024]{0:T(1024)S(1)} %mul.152) | copy-start | bytes 12292
  102.6 16.7 %copy-start.29 = (f32[1024]{0:T(1024)}, f32[1024]{0:T(1024)S(1)}, u32[]{:S(2)}) copy-start(f32[1024]{0:T(1024)S(1)} %add.139) | copy-start | bytes 12292
  119.3 15.1 %copy-start = (bf16[32,4096]{1,0:T(8,128)(2,1)S(1)}, bf16[32,4096]{1,0:T(8,128)(2,1)}, u32[]{:S(2)}) copy-start(bf16[32,4096]{1,0:T(8,128)(2,1)} %w_up.1) | copy-start | bytes 786436
  119.3 15.1 %copy-start.1 = (bf16[32,1024]{1,0:T(8,128)(2,1)S(1)}, bf16[32,1024]{1,0:T(8,128)(2,1)}, u32[]{:S(2)}) copy-start(bf16[32,1024]{1,0:T(8,128)(2,1)} %w_out.1) | copy-start | bytes 196612
  134.4 77.5 %copy-start.9 = (bf16[1024,1024]{0,1:T(8,128)(2,1)S(1)}, bf16[1024,1024]{0,1:T(8,128)(2,1)}, u32[]{:S(2)}) copy-start(bf16[1024,1024]{0,1:T(8,128)(2,1)} %copy-done.8) | copy-start | bytes 6291460
  214.6 20.2 %copy-start.5 = (f32[1024,1024]{0,1:T(8,128)}, f32[1024,1024]{0,1:T(8,128)S(1)}, u32[]{:S(2)}) copy-start(f32[1024,1024]{0,1:T(8,128)S(1)} %get-tuple-element.87) | copy-start | bytes 12582916
  215.1 19.7 %copy-start.15 = (bf16[1024,1024]{1,0:T(8,128)(2,1)S(1)}, bf16[1024,1024]{1,0:T(8,128)(2,1)}, u32[]{:S(2)}) copy-start(bf16[1024,1024]{1,0:T(8,128)(2,1)} %param.18) | copy-start | bytes 6291460
  268.0 15.7 %copy-start.41 = (bf16[1024,4096]{1,0:T(8,128)(2,1)}, bf16[1024,4096]{1,0:T(8,128)(2,1)S(1)}, u32[]{:S(2)}) copy-start(bf16[1024,4096]{1,0:T(8,128)(2,1)S(1)} %get-tuple-element.92) | copy-start | bytes 25165828
  494.1 53.3 %copy-start.14 = (f32[1024,1024]{0,1:T(8,128)S(1)}, f32[1024,1024]{0,1:T(8,128)}, u32[]{:S(2)}) copy-start(f32[1024,1024]{0,1:T(8,128)} %get-tuple-element.88) | copy-start | bytes 12582916
  496.5 51.0 %copy-start.13 = (f32[1024,1024]{0,1:T(8,128)S(1)}, f32[1024,1024]{0,1:T(8,128)}, u32[]{:S(2)}) copy-start(f32[1024,1024]{0,1:T(8,128)} %copy-done.12) | copy-start | bytes 12582916
  (22 other events, 111.2 us)
Sparse Core Ops, SparseCore 0:
  10.9 100.4 all-gather.1
  250.0 159.8 reduce-scatter.1

commit v3 on v2

--- a/solution.py
+++ b/solution.py
@@ -149,19 +149,21 @@
 GATHER_SEMS = 11
 
 
-def run_stages(pieces, tick, last):
-    for at in range(last + 1):
-        steps = [
-            (s, piece)
+def run_stages(pieces, step, steps):
+    for at in sorted(set(steps)):
+        todo = [
+            (q, piece)
+            for tick, when in enumerate(steps)
+            if when == at
             for k, piece in enumerate(pieces)
-            for s in (4, 3, 2, 1, 0)
-            if k + s == at
+            for q in (4, 3, 2, 1, 0)
+            if k + q == tick
         ]
-        if steps:
-            @pl.when(tick == at)
-            def _():
-                for s, piece in steps:
-                    piece.stage(s)
+
+        @pl.when(step == at)
+        def _():
+            for q, piece in todo:
+                piece.stage(q)
 
 
 class Scatter:
@@ -456,7 +458,7 @@
                     place, shard, full, pl.ds(k * UNIT, UNIT), send.at[i], recv.at[i], own.at[i]
                 )
             )
-    run_stages(pieces, tick, 7)
+    run_stages(pieces, tick, range(8))
     attend_body(n0_ref, q_ref, k_ref, v_ref, out_ref, lse_ref, parts, parts_lse)
 
     @pl.when(tick == 7)
@@ -663,7 +665,7 @@
                     place, grad.at[:, :, :, :, :, cols], *bufs[:5], out.at[:, cols], bufs[5:]
                 )
             )
-    run_stages(pieces, pair, pairs)
+    run_stages(pieces, pair, range(9))
     attend_back_body(pair, pairs, *base, *outs, *mine)
 
 
@@ -715,6 +717,273 @@
             vmem_limit_bytes=58 * 2**20, collective_id=collective, has_side_effects=True
         ),
         name="attend_back",
+    )(*args)
+
+
+ROW_TILE = 256
+FF_TILE = 512
+ROOT_HALF = 1.0 / math.sqrt(2.0)
+PDF_SCALE = 1.0 / math.sqrt(2.0 * math.pi)
+
+
+def row_stats(value):
+    mean = jnp.mean(value, axis=1, keepdims=True)
+    center = value - mean
+    inv_std = lax.rsqrt(jnp.mean(center * center, axis=1, keepdims=True) + EPS)
+    return center * inv_std, inv_std
+
+
+def mlp_up_body(
+    step, row_steps, mixed, tokens, w_out, vecs, w_up, up_bias, cot, resid, normed, act, slope,
+    g_down, held,
+):
+    @pl.when(step < row_steps)
+    def _():
+        value = tokens[...].astype(F32) + dot(mixed[...], w_out[...]) + vecs[0:1]
+        resid[...] = value
+        low = (row_stats(value)[0] * vecs[1:2] + vecs[2:3]).astype(BF)
+        normed[...] = low
+        held[pl.ds(step * ROW_TILE, ROW_TILE), :] = low
+
+    @pl.when(step >= row_steps)
+    def _():
+        rows = held.shape[0]
+
+        for row in range(0, rows, ROW_TILE):
+            part = pl.ds(row, ROW_TILE)
+            upward = dot(held[part, :], w_up[...]) + up_bias[...]
+            cdf = 0.5 * (1.0 + lax.erf(upward * ROOT_HALF))
+            pdf = jnp.exp(-0.5 * upward * upward) * PDF_SCALE
+            act[part, :] = (upward * cdf).astype(BF)
+            slope[part, :] = (cdf + upward * pdf).astype(BF)
+        g_down[...] = dot(act[...], cot[...], TN).astype(BF)
+
+
+def mlp_up_kernel(row_steps, *refs):
+    mlp_up_body(pl.program_id(0), row_steps, *refs)
+
+
+def mlp_up_gather_kernel(row_steps, *refs):
+    ins, shard, outs, full = refs[:7], refs[7], refs[8:13], refs[13]
+    held, send, recv, own = refs[14:]
+    step = pl.program_id(0)
+    place = Place()
+    pl.when(step == 0)(lambda: greet(place.partners))
+    cols = shard.shape[1] // 4
+    pieces = [
+        Gather(place, shard, full, pl.ds(k * cols, cols), send.at[k], recv.at[k], own.at[k])
+        for k in range(4)
+    ]
+    run_stages(pieces, step, (0, 2, 4, 5, 7, 9, 11))
+    mlp_up_body(step, row_steps, *ins, *outs, held)
+
+    @pl.when(step == pl.num_programs(0) - 1)
+    def _():
+        pieces[3].stage(4)
+
+
+def mlp_up(mixed, tokens, w_out, vecs, w_up, up_bias, cot, shard=None):
+    rows, width = tokens.shape
+    hidden = w_up.shape[1]
+    row_steps, ff_steps = rows // ROW_TILE, hidden // FF_TILE
+    at_row = lambda s: (jnp.minimum(s, row_steps - 1), 0)
+    at_col = lambda s: (0, jnp.maximum(s - row_steps, 0))
+    at_ff = lambda s: (jnp.maximum(s - row_steps, 0), 0)
+    const = lambda s: (0, 0)
+    hbm = pl.BlockSpec(memory_space=pl.ANY)
+    tall = pl.BlockSpec((rows, FF_TILE), at_col)
+    in_specs = [
+        pl.BlockSpec((ROW_TILE, width), at_row),
+        pl.BlockSpec((ROW_TILE, width), at_row),
+        pl.BlockSpec((width, width), const),
+        pl.BlockSpec((8, width), const),
+        pl.BlockSpec((width, FF_TILE), at_col),
+        pl.BlockSpec((1, FF_TILE), at_col),
+        pl.BlockSpec((rows, width), const),
+    ]
+    out_specs = [
+        pl.BlockSpec((ROW_TILE, width), at_row),
+        pl.BlockSpec((ROW_TILE, width), at_row),
+        tall,
+        tall,
+        pl.BlockSpec((FF_TILE, width), at_ff),
+    ]
+    out_shape = [
+        jax.ShapeDtypeStruct((rows, width), F32),
+        jax.ShapeDtypeStruct((rows, width), BF),
+        jax.ShapeDtypeStruct((rows, hidden), BF),
+        jax.ShapeDtypeStruct((rows, hidden), BF),
+        jax.ShapeDtypeStruct((hidden, width), BF),
+    ]
+    scratch = [pltpu.VMEM((rows, width), BF)]
+    params = dict(vmem_limit_bytes=58 * 2**20)
+    args = [mixed, tokens, w_out, vecs, w_up, up_bias, cot]
+    kernel = mlp_up_kernel
+    if shard is not None:
+        kernel = mlp_up_gather_kernel
+        in_specs += [hbm]
+        out_specs += [hbm]
+        out_shape += [jax.ShapeDtypeStruct((4, 2, 2, 2, *shard.shape), BF)]
+        scratch += [
+            pltpu.SemaphoreType.DMA((4, GATHER_SEMS)),
+            pltpu.SemaphoreType.DMA((4, GATHER_SEMS)),
+            pltpu.SemaphoreType.DMA((4,)),
+        ]
+        params |= dict(collective_id=5, has_side_effects=True)
+        args += [shard]
+    return pl.pallas_call(
+        functools.partial(kernel, row_steps),
+        grid=(row_steps + ff_steps,),
+        in_specs=in_specs,
+        out_specs=out_specs,
+        out_shape=out_shape,
+        scratch_shapes=scratch,
+        compiler_params=pltpu.CompilerParams(**params),
+        name="mlp_up",
+    )(*args)
+
+
+def mlp_back_body(
+    step, ff_steps, act, slope, w_up, w_down, cot, normed, resid, mixed, w_out, vecs,
+    g_up, up_sums, layer_out, dresid, dmixed, g_out, sums, total, dnormed, branches, dup,
+):
+    rows, width = cot.shape
+
+    @pl.when(step == 0)
+    def _():
+        total[...] = jnp.zeros(total.shape, F32)
+        dnormed[...] = jnp.zeros(dnormed.shape, F32)
+        sums[...] = jnp.zeros(sums.shape, F32)
+
+    @pl.when(step < ff_steps)
+    def _():
+        count = jnp.zeros(up_sums.shape, F32)
+        for row in range(0, rows, ROW_TILE):
+            part = pl.ds(row, ROW_TILE)
+            total[part, :] += dot(act[part, :], w_down[...])
+            dact = dot(cot[part, :], w_down[...], NT)
+            low = (dact * slope[part, :].astype(F32)).astype(BF)
+            dup[part, :] = low
+            count += jnp.sum(low.astype(F32), axis=0, keepdims=True)
+            dnormed[part, :] += dot(low, w_up[...], NT)
+        up_sums[...] = count
+        g_up[...] = dot(normed[...], dup[...], TN).astype(BF)
+
+    @pl.when(step >= ff_steps)
+    def _():
+        part = pl.ds((step - ff_steps) * ROW_TILE, ROW_TILE)
+        value = resid[...]
+        scaled, inv_std = row_stats(value)
+        upstream = dnormed[part, :]
+        above = cot[part, :].astype(F32)
+        through = upstream * vecs[1:2]
+        inner = (
+            through
+            - jnp.mean(through, axis=1, keepdims=True)
+            - scaled * jnp.mean(through * scaled, axis=1, keepdims=True)
+        )
+        grad = above + inv_std * inner
+        dresid[...] = grad
+        low = grad.astype(BF)
+        branches[part, :] = low
+        dmixed[...] = dot(low, w_out[...], NT).astype(BF)
+        layer_out[...] = (value + total[part, :] + vecs[3:4]).astype(BF)
+        sums[0:1] += jnp.sum(low.astype(F32), axis=0, keepdims=True)
+        sums[1:2] += jnp.sum(upstream * scaled, axis=0, keepdims=True)
+        sums[2:3] += jnp.sum(upstream, axis=0, keepdims=True)
+        sums[3:4] += jnp.sum(above, axis=0, keepdims=True)
+
+    @pl.when(step == pl.num_programs(0) - 1)
+    def _():
+        g_out[...] = dot(mixed[...], branches[...], TN).astype(BF)
+
+
+def mlp_back_kernel(ff_steps, *refs):
+    mlp_back_body(pl.program_id(0), ff_steps, *refs)
+
+
+def mlp_back_scatter_kernel(ff_steps, *refs):
+    ins, grad, outs, reduced, scratch, comm = (
+        refs[:10], refs[10], refs[11:18], refs[18], refs[19:23], refs[23:],
+    )
+    step = pl.program_id(0)
+    place = Place()
+    pl.when(step == 0)(lambda: greet(place.partners))
+    cols = reduced.shape[1] // 4
+    pieces = []
+    for k in range(4):
+        here = pl.ds(k * cols, cols)
+        bufs = comm[k * 8 : k * 8 + 8]
+        pieces.append(
+            Scatter(
+                place, grad.at[:, :, :, :, :, here], *bufs[:5], reduced.at[:, here], bufs[5:]
+            )
+        )
+    run_stages(pieces, step, (0, 1, 2, 4, 5, 7, 9))
+    mlp_back_body(step, ff_steps, *ins, *outs, *scratch)
+
+    @pl.when(step == pl.num_programs(0) - 1)
+    def _():
+        pieces[3].stage(4)
+
+
+def mlp_back(act, slope, w_up, w_down, cot, normed, resid, mixed, w_out, vecs, grad=None):
+    rows, width = cot.shape
+    hidden = w_up.shape[1]
+    row_steps, ff_steps = rows // ROW_TILE, hidden // FF_TILE
+    at_row = lambda s: (jnp.maximum(s - ff_steps, 0), 0)
+    at_col = lambda s: (0, jnp.minimum(s, ff_steps - 1))
+    at_ff = lambda s: (jnp.minimum(s, ff_steps - 1), 0)
+    const = lambda s: (0, 0)
+    hbm, vmem = pl.BlockSpec(memory_space=pl.ANY), pl.BlockSpec(memory_space=pltpu.VMEM)
+    once = lambda *shape: pl.BlockSpec(shape, const, pipeline_mode=pl.Buffered(1))
+    tall = pl.BlockSpec((rows, FF_TILE), at_col)
+    tile = pl.BlockSpec((ROW_TILE, width), at_row)
+    in_specs = [
+        tall, tall, pl.BlockSpec((width, FF_TILE), at_col), pl.BlockSpec((FF_TILE, width), at_ff),
+        once(rows, width), once(rows, width), tile, once(rows, width), once(width, width),
+        once(8, width),
+    ]
+    out_specs = [
+        pl.BlockSpec((width, FF_TILE), at_col), pl.BlockSpec((1, FF_TILE), at_col), tile, tile,
+        tile, once(width, width), once(8, width),
+    ]
+    out_shape = [
+        jax.ShapeDtypeStruct((width, hidden), BF),
+        jax.ShapeDtypeStruct((1, hidden), F32),
+        jax.ShapeDtypeStruct((rows, width), BF),
+        jax.ShapeDtypeStruct((rows, width), F32),
+        jax.ShapeDtypeStruct((rows, width), BF),
+        jax.ShapeDtypeStruct((width, width), BF),
+        jax.ShapeDtypeStruct((8, width), F32),
+    ]
+    scratch = [
+        pltpu.VMEM((rows, width), F32),
+        pltpu.VMEM((rows, width), F32),
+        pltpu.VMEM((rows, width), BF),
+        pltpu.VMEM((rows, FF_TILE), BF),
+    ]
+    params = dict(vmem_limit_bytes=60 * 2**20)
+    args = [act, slope, w_up, w_down, cot, normed, resid, mixed, w_out, vecs]
+    kernel = mlp_back_kernel
+    if grad is not None:
+        kernel = mlp_back_scatter_kernel
+        part = grad.shape[0] // 32
+        in_specs += [hbm]
+        out_specs += [vmem]
+        out_shape += [jax.ShapeDtypeStruct((part, width), F32)]
+        scratch += scatter_scratch(part, width // 4) * 4
+        params |= dict(collective_id=6, has_side_effects=True)
+        args += [blocks(grad)]
+    return pl.pallas_call(
+        functools.partial(kernel, ff_steps),
+        grid=(row_steps + ff_steps,),
+        in_specs=in_specs,
+        out_specs=out_specs,
+        out_shape=out_shape,
+        scratch_shapes=scratch,
+        compiler_params=pltpu.CompilerParams(**params),
+        name="mlp_back",
     )(*args)
 
 
@@ -784,8 +1053,7 @@
         vectors = vectors[:, :count].astype(F32)
     else:
         w_qkv, vectors = gathered(qkv_weight), gathered(packed[None]).astype(F32)
-        w_out, w_up = gathered(out_weight), gathered(up_weight)
-    w_down = gathered(down_weight)
+        w_out, w_up, w_down = map(gathered, (out_weight, up_weight, down_weight))
     part = norm1_gain.shape[0]
     gain1, shift1, q_bias, v_bias, o_bias, gain2, shift2, d_bias = (
         vectors[:, i * part : (i + 1) * part].reshape(-1) for i in range(8)
@@ -812,33 +1080,24 @@
     else:
         mixed_low, lse = attend(n0, queries, key_value)
 
-    resid = inputs + dot(mixed_low, w_out) + o_bias
-    normed_two, scaled_two, inv_two = normalize(resid, gain2, shift2)
-    normed_two_low = normed_two.astype(BF)
-    upward = dot(normed_two_low, w_up) + u_bias
-    normal_cdf = 0.5 * (1.0 + lax.erf(upward * (1.0 / math.sqrt(2.0))))
-    activated_low = (upward * normal_cdf).astype(BF)
-    layer_out = (resid + dot(activated_low, w_down) + d_bias).astype(BF)
-
-    upstream_out = cotangent.astype(F32)
-    grad_down = dot(activated_low, cotangent, TN)
-    grad_down_b = jnp.sum(upstream_out, axis=0)
-    normal_pdf = jnp.exp(-0.5 * upward * upward) * (1.0 / math.sqrt(2.0 * math.pi))
-    dupward_low = (dot(cotangent, w_down, NT) * (normal_cdf + upward * normal_pdf)).astype(BF)
-    grad_up = dot(normed_two_low, dupward_low, TN)
-    grad_up_b = jnp.sum(dupward_low.astype(F32), axis=0)
-    dnormed_two = dot(dupward_low, w_up, NT)
-    dresid_norm, grad_gain_two, grad_shift_two = normalize_back(
-        dnormed_two, scaled_two, inv_two, gain2
-    )
-    dresid = upstream_out + dresid_norm
-    dbranch_low = dresid.astype(BF)
-    grad_out = dot(mixed_low, dbranch_low, TN)
-    grad_out_b = jnp.sum(dbranch_low.astype(F32), axis=0)
-    dmixed_low = dot(dbranch_low, w_out, NT).astype(BF)
-
-    grad_out, grad_up = grad_out.astype(BF), grad_up.astype(BF)
-    r_down = scattered(grad_down.astype(BF)).astype(F32)
+    vecs = jnp.stack([o_bias, gain2, shift2, d_bias] + [jnp.zeros_like(d_bias)] * 4)
+    args = (mixed_low, tokens, w_out, vecs, w_up, u_bias[None], cotangent)
+    if block_plan:
+        resid, normed_two, act, slope, grad_down, w_down = mlp_up(*args, down_weight)
+        w_down = w_down.reshape(-1, width)
+    else:
+        resid, normed_two, act, slope, grad_down = mlp_up(*args)
+    args = (act, slope, w_up, w_down, cotangent, normed_two, resid, mixed_low, w_out, vecs)
+    if block_plan:
+        grad_up, up_sums, layer_out, dresid, dmixed_low, grad_out, sums, r_down = mlp_back(
+            *args, grad_down
+        )
+    else:
+        grad_up, up_sums, layer_out, dresid, dmixed_low, grad_out, sums = mlp_back(*args)
+        r_down = scattered(grad_down).astype(F32)
+    grad_out_b, grad_gain_two, grad_shift_two, grad_down_b = sums[:4]
+    grad_up_b = up_sums[0]
+
     if block_plan:
         dquery, dkey, dvalue, r_out, r_up = attend_back(
             n0, queries, key_value, dmixed_low, lse, (grad_out, grad_up)

time: 594 us -> 535 us (0.901)
  matrix products: 153 us -> 54.2 us
  Pallas kernels: 353 us -> 438 us
  between operations: 15.5 us -> 1.34 us
  other arithmetic: 26.5 us -> 13.7 us
  local copies, waits for them, and re-layouts: 32.7 us -> 20.3 us
    pallas_call x0 -> x2, Pallas kernels: none -> 133 us  [the longest x1 75.2 us: mlp_back(): pl.pallas_call(functools.partial(kernel, ff_steps), grid=(row_steps + ff_...]
    dot_general x17 -> x8, matrix products: 153 us -> 54.2 us  [dot(): return lax.dot_general(a, b, dims, preferred_element_type=F32)]
    pallas_call x1, Pallas kernels: 145 us -> 111 us  [attend_back(): pl.pallas_call(functools.partial(kernel, pairs), grid=(pairs + 1,), in_sp...]
    pallas_call x1, Pallas kernels: 79.6 us -> 61.9 us  [gather_blocks(): pl.pallas_call(gather_kernel, out_shape=out, in_specs=[hbm, hbm], out_spe...]
    reduce_sum x3 -> x0, other arithmetic: 10.8 us -> none  [the longest x1 4.65 us: normalize_back(): jnp.sum(upstream * scaled, axis=0)]
    unnamed x94 -> x72, local copies, waits for them, and re-layouts: 19.6 us -> 12 us
  transfers between devices with their start and end apart: 4 -> 2, of which waited for: 0 -> 0; matrix products, arithmetic and copies ran while one was open for 35% -> 2% of each run, Pallas kernels for 60% -> 12%
where the time goes in v3:
time: 535 us; the launch traced here: 531 us
  Pallas kernels  438 us (82%)
  matrix products  54.2 us (10%)
  local copies, waits for them, and re-layouts  20.3 us (4%)
  other arithmetic  13.7 us (3%)
    pallas_call x1, Pallas kernels, attend_back(): pl.pallas_call(functools.partial(kernel, pairs), grid=(pairs + 1,), in_sp...  111 us
    pallas_call x1, Pallas kernels, attend(): pl.pallas_call(kernel, grid=(pairs,), in_specs=in_specs, out_specs=out_sp...  78.8 us
    pallas_call x1, Pallas kernels, mlp_back(): pl.pallas_call(functools.partial(kernel, ff_steps), grid=(row_steps + ff_...  75.2 us
    pallas_call x1, Pallas kernels, gather_blocks(): pl.pallas_call(gather_kernel, out_shape=out, in_specs=[hbm, hbm], out_spe...  61.9 us
    pallas_call x1, Pallas kernels, mlp_up(): pl.pallas_call(functools.partial(kernel, row_steps), grid=(row_steps + ff...  57.3 us
    dot_general x8, matrix products, dot(): return lax.dot_general(a, b, dims, preferred_element_type=F32)  54.2 us
    pallas_call x1, Pallas kernels, scatter_blocks(): pl.pallas_call(scatter_kernel, out_shape=[jax.ShapeDtypeStruct((rows, 3 *...  53 us
    unnamed x72, local copies, waits for them, and re-layouts  12 us
  transfers between devices with their start and end apart: 2, of which 0 were waited for; matrix products, arithmetic and copies ran while one was open for 2% of the time, Pallas kernels for 12%

profile of v3, /device:TPU:0, one launch (start us, length us, event | category | flops | bytes accessed | tf_op | source)
XLA Modules:
  0.0 530.9 jit_solution(5218639021443565659)
XLA Ops:
  0.8 3.4 fusion.36
  4.1 2.4 collective-permute-start
  9.0 61.9 %gather_qkv.1 = (bf16[4,2,2,2,32,3072]{5,4,3,2,1,0:T(8,128)(2,1)}, bf16[4,2,2,2,32,128]{5,4,3,2,1,0:T(8,128)(2,1)}) custom-call(bf16[32,3072]{1,0:T(8,128)(2,1)} %wide.1, bf16[32,128]{1,0:T(8,128)(2,1)} %pad_bitcast_fusion.1.vec), custom_call_target="tpu_custom_call" | custom-call | tf_op jit(solution)/shard_map/gather_qkv/pallas_call | solution.py:300
  76.5 5.7 %add_convert_fusion.1.q_ref.refs_1_ = bf16[1024,1024]{1,0:T(8,128)(2,1)} fusion(f32[1024]{0:T(1024)S(1)} %add.78, bf16[1024,3072]{1,0:T(8,128)(2,1)} %bitcast.51, bf16[1024,1024]{1,0:T(8,128)(2,1)S(1)} %copy-done.7, f32[1024]{0:T(1024)S(1)} %add.75, f32[1024]{0:T(1024)S(1)} %mul.69, f32[1024]{0:T(1024)S(1)} %add_rsqrt_fusion.1, ...), kind=kOutput, calls=%fused_computation.34 | convolution fusion | flops 2155872256 | bytes 6311936 | tf_op jit(solution)/shard_map/dot_general | solution.py:27
  82.2 4.6 convert_reduce_fusion
  86.8 1.4 fusion.2
  88.3 13.0 %add_convert_fusion.k_ref.v_ref.refs_2_.refs_3_ = bf16[2304,2048]{1,0:T(8,128)(2,1)} fusion(f32[2048]{0:T(1024)S(1)} %concatenate.14, bf16[2304,1024]{1,0:T(8,128)(2,1)S(1)} %get-tuple-element.78, f32[1024]{0:T(1024)S(1)} %add.75, f32[1024]{0:T(1024)S(1)} %mul.69, f32[2304]{0:T(1024)S(1)} %add_rsqrt_fusion, f32[2304]{0:T(1024)S(1)} %broadcast_multiply_fusion, ...), kind=kOutput, calls=%fused_computation | convolution fusion | flops 9687269376 | bytes 18391040 | tf_op jit(solution)/shard_map/dot_general | solution.py:27
  101.3 78.8 %attend.1 = (bf16[1024,1024]{1,0:T(8,128)(2,1)S(1)}, f32[8,8,256]{2,1,0:T(8,128)S(1)}, bf16[4,2,2,2,32,1024]{5,4,3,2,1,0:T(8,128)(2,1)S(1)}, bf16[4,2,2,2,32,4096]{5,4,3,2,1,0:T(8,128)(2,1)}) custom-call(s32[1]{0:T(128)} %bitcast.1.n0_ref.refs_0_, bf16[1024,1024]{1,0:T(8,128)(2,1)} %add_convert_fusion.1.q_ref.refs_1_, ...), custom_call_target="tpu_custom_call" | custom-call | tf_op jit(solution)/shard_map/attend/pallas_call | solution.py:508
  180.1 1.3 copy-done
  181.4 1.3 copy-done.1
  183.4 57.3 %mlp_up.1 = (f32[1024,1024]{1,0:T(8,128)}, bf16[1024,1024]{1,0:T(8,128)(2,1)}, bf16[1024,4096]{1,0:T(8,128)(2,1)}, bf16[1024,4096]{1,0:T(8,128)(2,1)}, bf16[4096...) custom-call(bf16[1024,1024]{1,0:T(8,128)(2,1)} %copy-done, bf16[1024,1024]{1,0:T(8,128)(2,1)} %refs_1_.1, ...), custom_call_target="tpu_custom_call" | custom-call | tf_op jit(solution)/shard_map/mlp_up/pallas_call | solution.py:834
  240.7 75.2 %mlp_back.1 = (bf16[1024,4096]{1,0:T(8,128)(2,1)}, f32[1,4096]{1,0:T(1,128)}, bf16[1024,1024]{1,0:T(8,128)(2,1)}, f32[1024,1024]{1,0:T(8,128)}, bf16[1024,1024]{...) custom-call(bf16[1024,4096]{1,0:T(8,128)(2,1)} %get-tuple-element.47.refs_0_, ...), custom_call_target="tpu_custom_call" | custom-call | tf_op jit(solution)/shard_map/mlp_back/pallas_call | solution.py:978
  315.9 111.4 %attend_back.1 = (bf16[1024,1024]{1,0:T(8,128)(2,1)}, bf16[1024,1024]{1,0:T(8,128)(2,1)}, bf16[1024,1024]{1,0:T(8,128)(2,1)}, f32[32,1024]{1,0:T(8,128)}, f32[32,4096]{1,0:T(8,128)}) custom-call(s32[1]{0:T(128)} %bitcast.1.n0_ref.refs_0_, bf16[1024,1024]{1,0:T(8,128)(2,1)} %add_convert_fusion.1.q_ref.refs_1_, ...), custom_call_target="tpu_custom_call" | custom-call | tf_op jit(solution)/shard_map/attend_back/pallas_call | solution.py:709
  427.4 4.4 convolution_convert_fusion.1
  431.8 6.1 %fusion.28 = f32[1024,1024]{1,0:T(8,128)} fusion(bf16[1024,1024]{1,0:T(8,128)(2,1)S(1)} %copy-done.29, bf16[1024,3072]{1,0:T(8,128)(2,1)} %bitcast.52), kind=kOutput, calls=%fused_computation.38 | convolution fusion | flops 2147483648 | bytes 8388608 | tf_op jit(solution)/shard_map/dot_general | solution.py:27
  437.9 4.1 convolution_convert_fusion.2
  442.9 4.2 convolution_convert_fusion
  447.1 6.2 %fusion.26 = f32[1024,1024]{1,0:T(8,128)} fusion(bf16[1024,1024]{1,0:T(8,128)(2,1)S(1)} %copy-done.13, bf16[1024,3072]{1,0:T(8,128)(2,1)} %bitcast.53), kind=kOutput, calls=%fused_computation.36 | convolution fusion | flops 2147483648 | bytes 8388608 | tf_op jit(solution)/shard_map/dot_general | solution.py:27
  453.7 10.4 %fusion.23 = (f32[1024]{0:T(1024)S(1)}, f32[1024]{0:T(1024)S(1)}, f32[1024]{0:T(1024)S(1)}, f32[1024]{0:T(1024)S(1)}, f32[1024,1024]{1,0:T(8,128)}) fusion(bf16[1024,1024]{1,0:T(8,128)(2,1)} %refs_1_.1, f32[1024]{0:T(1024)S(1)} %add_rsqrt_fusion.1, f32[1024]{0:T(1024)S(1)} %broadcast_multiply_fusion.3, f32[1024]{0:T(1024)S(1)} %mul.69, ...), kind=kOutput, calls=%fused_computation.28 | convolution fusion | flops 2160062464 | bytes 18903040 | tf_op jit(solution)/shard_map/dot_general | solution.py:27
  464.5 1.6 copy-done.2
  466.1 1.6 copy-done.3
  467.7 53.0 %scatter_qkv.1 = (f32[32,3072]{1,0:T(8,128)S(1)}, f32[16,128]{1,0:T(8,128)S(1)}) custom-call(bf16[4,2,2,2,32,1024]{5,4,3,2,1,0:T(8,128)(2,1)S(1)} %bitcast.38, bf16[4,2,2,2,32,1024]{5,4,3,2,1,0:T(8,128)(2,1)S(1)} %bitcast.37, bf16[4,2,2,2,32,1024]{5,4,3,2,1,0:T(8,128)(2,1)S(1)} %bitcast.39, f32[4,2,2,2,16,128]{5,4,3,2,1,0:T(8,128)S(1)} %bitcast.40), custom_call_target="tpu_custom_call" | custom-call | tf_op jit(solution)/shard_map/scatter_qkv/pallas_call | solution.py:336
  521.9 4.5 fusion.22
  526.4 1.3 copy.40
  (112 shorter events, 14.3 us)
Async XLA Ops:
  0.6 7.2 %copy-start.7 = (bf16[1024,1024]{1,0:T(8,128)(2,1)S(1)}, bf16[1024,1024]{1,0:T(8,128)(2,1)}, u32[]{:S(2)}) copy-start(bf16[1024,1024]{1,0:T(8,128)(2,1)} %refs_1_.1) | copy-start | bytes 6291460
  0.7 7.5 %copy-start.27 = (bf16[32]{0:T(256)(128)(2,1)S(1)}, bf16[32]{0:T(256)(128)(2,1)}, u32[]{:S(2)}) copy-start(bf16[32]{0:T(256)(128)(2,1)} %param.31) | copy-start | bytes 196
  0.7 7.5 %copy-start.28 = (bf16[128]{0:T(256)(128)(2,1)S(1)}, bf16[128]{0:T(256)(128)(2,1)}, u32[]{:S(2)}) copy-start(bf16[128]{0:T(256)(128)(2,1)} %param.29) | copy-start | bytes 772
  0.7 7.5 %copy-start.26 = (bf16[32]{0:T(256)(128)(2,1)S(1)}, bf16[32]{0:T(256)(128)(2,1)}, u32[]{:S(2)}) copy-start(bf16[32]{0:T(256)(128)(2,1)} %param.27) | copy-start | bytes 196
  0.7 7.5 %copy-start.25 = (bf16[32]{0:T(256)(128)(2,1)S(1)}, bf16[32]{0:T(256)(128)(2,1)}, u32[]{:S(2)}) copy-start(bf16[32]{0:T(256)(128)(2,1)} %param.26) | copy-start | bytes 196
  0.7 7.5 %copy-start.24 = (bf16[32]{0:T(256)(128)(2,1)S(1)}, bf16[32]{0:T(256)(128)(2,1)}, u32[]{:S(2)}) copy-start(bf16[32]{0:T(256)(128)(2,1)} %param.25) | copy-start | bytes 196
  0.7 7.5 %copy-start.23 = (bf16[32]{0:T(256)(128)(2,1)S(1)}, bf16[32]{0:T(256)(128)(2,1)}, u32[]{:S(2)}) copy-start(bf16[32]{0:T(256)(128)(2,1)} %param.23) | copy-start | bytes 196
  0.7 7.5 %copy-start.22 = (bf16[32]{0:T(256)(128)(2,1)S(1)}, bf16[32]{0:T(256)(128)(2,1)}, u32[]{:S(2)}) copy-start(bf16[32]{0:T(256)(128)(2,1)} %param.22) | copy-start | bytes 196
  0.7 7.5 %copy-start.21 = (bf16[32]{0:T(256)(128)(2,1)S(1)}, bf16[32]{0:T(256)(128)(2,1)}, u32[]{:S(2)}) copy-start(bf16[32]{0:T(256)(128)(2,1)} %param.20) | copy-start | bytes 196
  0.7 7.5 %copy-start.20 = (bf16[32]{0:T(256)(128)(2,1)S(1)}, bf16[32]{0:T(256)(128)(2,1)}, u32[]{:S(2)}) copy-start(bf16[32]{0:T(256)(128)(2,1)} %param.19) | copy-start | bytes 196
  0.8 71.9 %copy-start.19 = (s32[1024]{0:T(1024)S(1)}, s32[1024]{0:T(1024)}, u32[]{:S(2)}) copy-start(s32[1024]{0:T(1024)} %param.17) | copy-start | bytes 12292
  4.1 78.1 %collective-permute-start = (bf16[576,1024]{1,0:T(8,128)(2,1)}, bf16[576,1024]{1,0:T(8,128)(2,1)S(1)}, u32[]{:S(2)}, u32[]{:S(2)}) collective-permute-start(bf16[576,1024]{1,0:T(8,128)(2,1)} %get-tuple-element.79), channel_id=1, source_target_pairs={{0,1},{1,2},{2,3},{3,4},{4,5},{5,6},{6,7},{7,8},{8,9},{9,10},{10,1... | collective-permute-start | bytes 3538952 | tf_op jit(solution)/shard_map/ppermute | solution.py:993
  6.5 75.7 %collective-permute-start.1 = (bf16[576,1024]{1,0:T(8,128)(2,1)}, bf16[576,1024]{1,0:T(8,128)(2,1)}, u32[]{:S(2)}, u32[]{:S(2)}) collective-permute-start(bf16[576,1024]{1,0:T(8,128)(2,1)} %get-tuple-element.80), channel_id=1, source_target_pairs={{1,0},{2,1},{3,2},{4,3},{5,4},{6,5},{7,6},{8,7},{9,8},{10,9},{11,1... | collective-permute-start | bytes 3538952 | tf_op jit(solution)/shard_map/ppermute | solution.py:993
  75.8 12.5 %slice-start = ((s8[6291456]{0:T(1024)(128)(4,1)}), s8[4194304]{0:T(1024)(128)(4,1)S(1)}, s32[]{:S(2)}) async-start(s8[6291456]{0:T(1024)(128)(4,1)} %bitcast.55), calls=%async_computation | async-start | bytes 8388608
  76.5 11.8 %slice-start.1 = ((s8[6291456]{0:T(1024)(128)(4,1)}), s8[2097152]{0:T(1024)(128)(4,1)S(1)}, s32[]{:S(2)}) async-start(s8[6291456]{0:T(1024)(128)(4,1)} %bitcast.55), calls=%async_computation.1 | async-start | bytes 4194304
  88.3 13.1 %copy-start.4 = (bf16[32,4096]{1,0:T(8,128)(2,1)S(1)}, bf16[32,4096]{1,0:T(8,128)(2,1)}, u32[]{:S(2)}) copy-start(bf16[32,4096]{1,0:T(8,128)(2,1)} %w_up.1) | copy-start | bytes 786436
  88.3 13.0 %copy-start.5 = (bf16[32,1024]{1,0:T(8,128)(2,1)S(1)}, bf16[32,1024]{1,0:T(8,128)(2,1)}, u32[]{:S(2)}) copy-start(bf16[32,1024]{1,0:T(8,128)(2,1)} %w_out.1) | copy-start | bytes 196612
  315.9 111.4 %copy-start.8 = (bf16[1024,1024]{1,0:T(8,128)(2,1)S(1)}, bf16[1024,1024]{1,0:T(8,128)(2,1)}, u32[]{:S(2)}) copy-start(bf16[1024,1024]{1,0:T(8,128)(2,1)} %refs_1_.1) | copy-start | bytes 6291460
  431.8 6.1 %copy-start.12 = (bf16[1024,1024]{1,0:T(8,128)(2,1)S(1)}, bf16[1024,1024]{1,0:T(8,128)(2,1)}, u32[]{:S(2)}) copy-start(bf16[1024,1024]{1,0:T(8,128)(2,1)} %get-tuple-element.59) | copy-start | bytes 6291460
  447.0 6.3 %copy-start.18 = (f32[8,1024]{1,0:T(8,128)S(1)}, f32[8,1024]{1,0:T(8,128)}, u32[]{:S(2)}) copy-start(f32[8,1024]{1,0:T(8,128)} %get-tuple-element.62) | copy-start | bytes 98308
  453.7 10.6 %copy-start.17 = (f32[1,4096]{1,0:T(1,128)S(1)}, f32[1,4096]{1,0:T(1,128)}, u32[]{:S(2)}) copy-start(f32[1,4096]{1,0:T(1,128)} %get-tuple-element.63) | copy-start | bytes 49156
  467.7 54.2 %copy-start.9 = (bf16[1024,1024]{1,0:T(8,128)(2,1)S(1)}, bf16[1024,1024]{1,0:T(8,128)(2,1)}, u32[]{:S(2)}) copy-start(bf16[1024,1024]{1,0:T(8,128)(2,1)} %refs_1_.1) | copy-start | bytes 6291460
  467.7 54.2 %copy-start.10 = (f32[1024,1024]{1,0:T(8,128)S(1)}, f32[1024,1024]{1,0:T(8,128)}, u32[]{:S(2)}) copy-start(f32[1024,1024]{1,0:T(8,128)} %get-tuple-element.54) | copy-start | bytes 12582916
  521.9 4.5 copy-start.11
  (10 other events, 23.4 us)

commit v4 on v3

--- a/solution.py
+++ b/solution.py
@@ -40,8 +40,9 @@
 
 
 def key_mask(low, high):
-    row = lax.broadcasted_iota(jnp.int32, (WIN, 2 * QB), 0)
-    return (row >= low) & (row < high)
+    row = lax.broadcasted_iota(jnp.int32, (WIN, QB), 0)
+    bias = jnp.where((row >= low) & (row < high), 0.0, NEG)
+    return jnp.concatenate([bias, bias], axis=1)
 
 
 def mesh_copy(src, dst, send_sem, recv_sem, to):
@@ -313,44 +314,9 @@
     return full.reshape(-1, wide.shape[1]), small.reshape(32, -1)
 
 
-def scatter_kernel(g_q, g_k, g_v, small, out, small_out, *scratch):
-    place = Place()
-    greet(place.partners)
-    size = 8
-    pieces = []
-    for k, grad in enumerate((g_q, g_k, g_v, small)):
-        bufs = scratch[k * size : (k + 1) * size]
-        to = small_out if k == 3 else out.at[:, pl.ds(k * UNIT, UNIT)]
-        pieces.append(Scatter(place, grad, *bufs[:5], to, bufs[5:]))
-    for at in range(len(pieces) + 4):
-        for s in (4, 3, 2, 1, 0):
-            if 0 <= at - s < len(pieces):
-                pieces[at - s].stage(s)
-
-
-def scatter_blocks(grads, small):
-    hbm = pl.BlockSpec(memory_space=pl.ANY)
-    vmem = pl.BlockSpec(memory_space=pltpu.VMEM)
-    rows = grads[0].shape[0] // 32
-    small = blocks(small)
-    return pl.pallas_call(
-        scatter_kernel,
-        out_shape=[
-            jax.ShapeDtypeStruct((rows, 3 * UNIT), F32),
-            jax.ShapeDtypeStruct(small.shape[4:], F32),
-        ],
-        in_specs=[hbm] * 4,
-        out_specs=[vmem] * 2,
-        scratch_shapes=scatter_scratch(rows, UNIT) * 3
-        + scatter_scratch(*small.shape[4:], F32),
-        compiler_params=pltpu.CompilerParams(
-            collective_id=3, has_side_effects=True, vmem_limit_bytes=40 * 2**20
-        ),
-        name="scatter_qkv",
-    )(*map(blocks, grads), small)
-
-
 ITEMS = 10
+BACK_GROUP = 2
+GROUP = 5
 
 
 class Images:
@@ -412,19 +378,30 @@
     rows = q_ref.shape[0]
     images = Images(n0_ref[0], rows, k_ref.shape[0])
 
-    @pl.loop(0, ITEMS)
-    def _(item):
+    def scores_of(item):
         _, row0, base, low, high, _, _ = images.item(item)
         queries = stacked(q_ref[pl.ds(row0, QB), :]) * jnp.asarray(0.125, BF)
-        keys = k_ref[pl.ds(base, WIN), :]
-        values = v_ref[pl.ds(base, WIN), :]
-        scores = jnp.where(key_mask(low, high), dot(keys, queries, NT), NEG)
+        scores = dot(k_ref[pl.ds(base, WIN), :], queries, NT)
+        return scores + key_mask(low, high), base
+
+    def softmax_of(scores):
         top = jnp.max(scores, axis=0, keepdims=True)
         terms = jnp.exp(scores - top)
         total = jnp.sum(terms, axis=0, keepdims=True)
-        mixed = dot(values, terms.astype(BF), TN) / total
-        parts[item] = unstacked(mixed)
-        parts_lse[item] = jnp.broadcast_to(top + jnp.log(total), parts_lse.shape[1:])
+        return terms.astype(BF), top, total
+
+    @pl.loop(0, ITEMS // GROUP)
+    def _(step):
+        items = [step * GROUP + g for g in range(GROUP)]
+        scored = [scores_of(item) for item in items]
+        soft = [softmax_of(scores) for scores, _ in scored]
+        mixed = [
+            dot(v_ref[pl.ds(base, WIN), :], terms, TN) / total
+            for (_, base), (terms, _, total) in zip(scored, soft)
+        ]
+        for item, value, (_, top, total) in zip(items, mixed, soft):
+            parts[item] = unstacked(value)
+            parts_lse[item] = jnp.broadcast_to(top + jnp.log(total), parts_lse.shape[1:])
 
     for blk in range(rows // QB):
         first, last, split = images.of_block(blk)
@@ -517,144 +494,76 @@
     )(*args)
 
 
-TILE = 64
-
-
 def attend_back_body(
-    pair, pairs, n0_ref, q_ref, k_ref, v_ref, up_ref, lse_ref, dq_ref, dk_ref, dv_ref,
-    slots, parts, padded, outgoing, incoming, send, recv,
+    pair, n0_ref, q_ref, k_ref, v_ref, up_ref, lse_ref, dq_ref, dk_ref, dv_ref, slots, parts
 ):
     rows = q_ref.shape[0]
     images = Images(n0_ref[0], rows, k_ref.shape[0])
-    me, peers = lax.axis_index(AXIS), lax.axis_size(AXIS)
-    wide = slice(TILE, TILE + WIN)
-
-    def halo(p, way):
-        return mesh_copy(
-            outgoing.at[p, way], incoming.at[p, way], send.at[p, way], recv.at[p, way],
-            me - 1 if way == 0 else me + 1,
-        )
-
-    @pl.when(pair == 0)
-    def _():
-        slots[0] = jnp.zeros(slots.shape[1:], F32)
-        padded[...] = jnp.zeros(padded.shape, F32)
-
-        @pl.when(me == 0)
-        def _():
-            incoming[:, 1] = jnp.zeros((pairs, WIN, 4 * HDIM), BF)
-
-        @pl.when(me == peers - 1)
-        def _():
-            incoming[:, 0] = jnp.zeros((pairs, WIN, 4 * HDIM), BF)
-
-    @pl.when(pair < pairs)
-    def _():
-        @pl.loop(0, ITEMS)
-        def _(item):
-            blk, row0, base, low, high, first, stop = images.item(item)
-            queries = stacked(q_ref[pl.ds(row0, QB), :]) * jnp.asarray(0.125, BF)
-            upstream = stacked(up_ref[pl.ds(row0, QB), :])
-            lane = lax.broadcasted_iota(jnp.int32, (1, 2 * QB), 1) % QB
-            here = (lane >= first) & (lane < stop)
-            lse = jnp.where(here, lse_ref[0, pl.ds(blk, 1), :], -NEG)
-            keys = k_ref[pl.ds(base, WIN), :]
-            values = v_ref[pl.ds(base, WIN), :]
-            scores = jnp.where(key_mask(low, high), dot(keys, queries, NT), NEG)
-            probs = jnp.exp(scores - lse)
-            dprobs = dot(values, upstream, NT)
-            row_dot = jnp.sum(probs * dprobs, axis=0, keepdims=True)
-            dscores = (probs * (dprobs - row_dot)).astype(BF)
-            same = images.segment(item) == images.segment(item - 1)
-            keep = (item > 0) & same
-            old = jnp.where(keep, slots[item], jnp.zeros(slots.shape[1:], F32))
-            slots[item + 1, :, : 2 * HDIM] = old[:, : 2 * HDIM] + dot(dscores, queries)
-            slots[item + 1, :, 2 * HDIM :] = old[:, 2 * HDIM :] + dot(probs.astype(BF), upstream)
-            parts[item] = unstacked(dot(keys, dscores, TN)) * 0.125
-
-        for blk in range(rows // QB):
-            first, last, split = images.of_block(blk)
-            row = lax.broadcasted_iota(jnp.int32, (QB, 2 * HDIM), 0)
-            dq_ref[pl.ds(blk * QB, QB), :] = jnp.where(
-                row < split, parts[first], parts[last]
-            ).astype(BF)
-
-    @pl.when(pair > 0)
-    def _():
-        done = pair - 1
-
-        @pl.when(me > 0)
-        def _():
-            halo(done, 0).wait_send()
-
-        @pl.when(me < peers - 1)
-        def _():
-            halo(done, 0).wait_recv()
-            halo(done, 1).wait_send()
-
-        @pl.when(me > 0)
-        def _():
-            halo(done, 1).wait_recv()
-
-        none = jnp.zeros((WIN, 4 * HDIM), F32)
-        last = jnp.where(images.third, 2, 1)
-        stop = jnp.where(images.third, images.spans[2][1], images.spans[1][1])
-        cut = (stop > RIM + rows) & (me < peers - 1)
-        after = jnp.where(cut, incoming[done, 0].astype(F32), none)
-        before = jnp.where(images.spans[0][0] < RIM, incoming[done, 1].astype(F32), none)
-        padded[0, wide] = padded[0, wide] + before
-        padded[1, wide] = padded[1, wide] + jnp.where(last == 1, after, none)
-        padded[2, wide] = padded[2, wide] + jnp.where(last == 2, after, none)
-        bases = [images.base(span[0]) for span in images.spans]
-
-        @pl.loop(0, rows // TILE)
-        def _(tile):
-            row = pl.multiple_of(tile * TILE, TILE)
-            total = None
-            for seg, base in enumerate(bases):
-                off = jnp.maximum((RIM + TILE) // 16 + tile * (TILE // 16) - base, 0)
-                off = jnp.minimum(off, (WIN + TILE) // 16) * 16
-                term = padded[seg, pl.ds(off, TILE), :]
-                total = term if total is None else total + term
-            dk_ref[pl.ds(row, TILE), :] = total[:, : 2 * HDIM].astype(BF)
-            dv_ref[pl.ds(row, TILE), :] = total[:, 2 * HDIM :].astype(BF)
-
-    @pl.when(pair < pairs)
-    def _():
-        ends = (
-            images.end0 + 1,
-            jnp.minimum(images.end1, (rows - 1) // QB + images.d0) + 1,
-            jnp.where(images.third, ITEMS, 0),
-        )
-        for seg, end in enumerate(ends):
-            padded[seg, wide] = slots[end]
-        outgoing[pair, 0] = padded[0, wide].astype(BF)
-        outgoing[pair, 1] = jnp.where(images.third, padded[2, wide], padded[1, wide]).astype(BF)
-
-        @pl.when(me > 0)
-        def _():
-            halo(pair, 0).start()
-
-        @pl.when(me < peers - 1)
-        def _():
-            halo(pair, 1).start()
-
-
-def attend_back_kernel(pairs, *refs):
-    me, peers = lax.axis_index(AXIS), lax.axis_size(AXIS)
-    pair = pl.program_id(0)
-    pl.when(pair == 0)(lambda: greet([], me > 0, me < peers - 1))
-    attend_back_body(pair, pairs, *refs)
-
-
-def attend_back_scatter_kernel(pairs, *refs):
+    pl.when(pair == 0)(lambda: slots.__setitem__(0, jnp.zeros(slots.shape[1:], F32)))
+    lane = lax.broadcasted_iota(jnp.int32, (1, 2 * QB), 1) % QB
+
+    def begin(item):
+        blk, row0, base, low, high, first, stop = images.item(item)
+        queries = stacked(q_ref[pl.ds(row0, QB), :]) * jnp.asarray(0.125, BF)
+        upstream = stacked(up_ref[pl.ds(row0, QB), :])
+        here = (lane >= first) & (lane < stop)
+        lse = jnp.where(here, lse_ref[0, pl.ds(blk, 1), :], -NEG)
+        scores = dot(k_ref[pl.ds(base, WIN), :], queries, NT)
+        dprobs = dot(v_ref[pl.ds(base, WIN), :], upstream, NT)
+        return base, queries, upstream, scores + key_mask(low, high), lse, dprobs
+
+    def middle(scores, lse, dprobs):
+        probs = jnp.exp(scores - lse)
+        row_dot = jnp.sum(probs * dprobs, axis=0, keepdims=True)
+        return probs.astype(BF), (probs * (dprobs - row_dot)).astype(BF)
+
+    def finish(item, base, queries, upstream, probs, dscores):
+        keep = (item > 0) & (images.segment(item) == images.segment(item - 1))
+        old = jnp.where(keep, slots[item], jnp.zeros(slots.shape[1:], F32))
+        slots[item + 1, :, : 2 * HDIM] = old[:, : 2 * HDIM] + dot(dscores, queries)
+        slots[item + 1, :, 2 * HDIM :] = old[:, 2 * HDIM :] + dot(probs, upstream)
+        parts[item] = unstacked(dot(k_ref[pl.ds(base, WIN), :], dscores, TN)) * 0.125
+
+    @pl.loop(0, ITEMS // BACK_GROUP)
+    def _(step):
+        items = [step * BACK_GROUP + g for g in range(BACK_GROUP)]
+        begun = [begin(items[0])]
+        done = []
+        for g in range(BACK_GROUP + 1):
+            if g + 1 < BACK_GROUP:
+                begun.append(begin(items[g + 1]))
+            if g < BACK_GROUP:
+                done.append(middle(*begun[g][3:]))
+            if g > 0:
+                finish(items[g - 1], *begun[g - 1][:3], *done[g - 1])
+
+    for blk in range(rows // QB):
+        first, last, split = images.of_block(blk)
+        row = lax.broadcasted_iota(jnp.int32, (QB, 2 * HDIM), 0)
+        dq_ref[pl.ds(blk * QB, QB), :] = jnp.where(
+            row < split, parts[first], parts[last]
+        ).astype(BF)
+    ends = (
+        images.end0 + 1,
+        jnp.minimum(images.end1, (rows - 1) // QB + images.d0) + 1,
+        jnp.where(images.third, ITEMS, 0),
+    )
+    for seg, end in enumerate(ends):
+        dk_ref[seg] = slots[end, :, : 2 * HDIM].astype(BF)
+        dv_ref[seg] = slots[end, :, 2 * HDIM :].astype(BF)
+
+
+def attend_back_kernel(*refs):
+    attend_back_body(pl.program_id(0), *refs)
+
+
+def attend_back_scatter_kernel(*refs):
     base, (g_out, g_up), rest = refs[:6], refs[6:8], refs[8:]
     outs, (r_out, r_up), scratch = rest[:3], rest[3:5], rest[5:]
-    mine, comm = scratch[:7], scratch[7:]
-    me, peers = lax.axis_index(AXIS), lax.axis_size(AXIS)
+    mine, comm = scratch[:2], scratch[2:]
     pair = pl.program_id(0)
     place = Place()
-    pl.when(pair == 0)(lambda: greet(place.partners, me > 0, me < peers - 1))
+    pl.when(pair == 0)(lambda: greet(place.partners))
     pieces = []
     for grad, out in ((g_out, r_out), (g_up, r_up)):
         for k in range(grad.shape[5] // UNIT):
@@ -665,8 +574,12 @@
                     place, grad.at[:, :, :, :, :, cols], *bufs[:5], out.at[:, cols], bufs[5:]
                 )
             )
-    run_stages(pieces, pair, range(9))
-    attend_back_body(pair, pairs, *base, *outs, *mine)
+    run_stages(pieces, pair, range(8))
+    attend_back_body(pair, *base, *outs, *mine)
+
+    @pl.when(pair == pl.num_programs(0) - 1)
+    def _():
+        pieces[-1].stage(4)
 
 
 def attend_back(n0, queries, key_value, upstream, lse, grads=None):
@@ -674,32 +587,28 @@
     pairs = width // (2 * HDIM)
     ext = key_value.shape[0]
     hbm, vmem = pl.BlockSpec(memory_space=pl.ANY), pl.BlockSpec(memory_space=pltpu.VMEM)
-    here = lambda p: jnp.minimum(p, pairs - 1)
-    own = pl.BlockSpec((rows, 2 * HDIM), lambda p: (0, here(p)))
-    late = pl.BlockSpec((rows, 2 * HDIM), lambda p: (0, jnp.maximum(p - 1, 0)))
+    own = pl.BlockSpec((rows, 2 * HDIM), lambda p: (0, p))
+    windows = pl.BlockSpec((3, WIN, 2 * HDIM), lambda p: (0, 0, p))
     in_specs = [
         pl.BlockSpec(memory_space=pltpu.SMEM),
         own,
-        pl.BlockSpec((ext, 2 * HDIM), lambda p: (0, here(p))),
-        pl.BlockSpec((ext, 2 * HDIM), lambda p: (0, pairs + here(p))),
+        pl.BlockSpec((ext, 2 * HDIM), lambda p: (0, p)),
+        pl.BlockSpec((ext, 2 * HDIM), lambda p: (0, pairs + p)),
         own,
-        pl.BlockSpec((1, rows // QB, 2 * QB), lambda p: (here(p), 0, 0)),
-    ]
-    out_specs = [own, late, late]
-    out_shape = [jax.ShapeDtypeStruct((rows, width), BF)] * 3
+        pl.BlockSpec((1, rows // QB, 2 * QB), lambda p: (p, 0, 0)),
+    ]
+    out_specs = [own, windows, windows]
+    out_shape = [jax.ShapeDtypeStruct((rows, width), BF)]
+    out_shape += [jax.ShapeDtypeStruct((3, WIN, width), BF)] * 2
     scratch = [
         pltpu.VMEM((ITEMS + 1, WIN, 4 * HDIM), F32),
         pltpu.VMEM((ITEMS, QB, 2 * HDIM), F32),
-        pltpu.VMEM((3, WIN + 2 * TILE, 4 * HDIM), F32),
-        pltpu.VMEM((pairs, 2, WIN, 4 * HDIM), BF),
-        pltpu.VMEM((pairs, 2, WIN, 4 * HDIM), BF),
-        pltpu.SemaphoreType.DMA((pairs, 2)),
-        pltpu.SemaphoreType.DMA((pairs, 2)),
     ]
     args = [n0, queries, key_value, key_value, upstream, lse]
-    kernel, collective = attend_back_kernel, 4
+    kernel, params = attend_back_kernel, dict(vmem_limit_bytes=58 * 2**20)
     if grads is not None:
-        kernel, collective = attend_back_scatter_kernel, 2
+        kernel = attend_back_scatter_kernel
+        params |= dict(collective_id=2, has_side_effects=True)
         args += map(blocks, grads)
         in_specs += [hbm] * 2
         out_specs += [vmem] * 2
@@ -707,15 +616,13 @@
         for v in grads:
             scratch += scatter_scratch(v.shape[0] // 32, UNIT) * (v.shape[1] // UNIT)
     return pl.pallas_call(
-        functools.partial(kernel, pairs),
-        grid=(pairs + 1,),
+        kernel,
+        grid=(pairs,),
         in_specs=in_specs,
         out_specs=out_specs,
         out_shape=out_shape,
         scratch_shapes=scratch,
-        compiler_params=pltpu.CompilerParams(
-            vmem_limit_bytes=58 * 2**20, collective_id=collective, has_side_effects=True
-        ),
+        compiler_params=pltpu.CompilerParams(**params),
         name="attend_back",
     )(*args)
 
@@ -987,6 +894,258 @@
     )(*args)
 
 
+TILE = 64
+
+
+class Total:
+    def __init__(self, place, value, arrived, send, recv):
+        p = place
+        near = p.z + 1 - 2 * (p.z % 2)
+        self.to = [p.sib, p.xp, p.yp, p.at(near, p.y, p.x, p.c), p.zp[1]]
+        self.value, self.arrived, self.send, self.recv = value, arrived, send, recv
+
+    def run(self):
+        for i, to in enumerate(self.to):
+            copy = mesh_copy(
+                self.value.at[i], self.arrived.at[i], self.send.at[i], self.recv.at[i], to
+            )
+            copy.start()
+            copy.wait()
+            self.value[i + 1] = self.value[i] + self.arrived[i]
+
+
+def last_body(
+    step, n0_ref, normed, dq, dk, dv, w_qkv, tokens, dresid, vecs, sums, up_sums, out, grads,
+    padded, outgoing, incoming, send, recv, vector_out,
+):
+    rows = dq.shape[0]
+    ext, width = normed.shape
+    images = Images(n0_ref[0], rows, ext)
+    bases = [images.base(span[0]) for span in images.spans]
+    me, peers = lax.axis_index(AXIS), lax.axis_size(AXIS)
+    wide = slice(TILE, TILE + WIN)
+
+    def halo(way):
+        return mesh_copy(
+            outgoing.at[way], incoming.at[way], send.at[way], recv.at[way],
+            me - 1 if way == 0 else me + 1,
+        )
+
+    def column_sums(value):
+        return jnp.sum(value.astype(F32), axis=0, keepdims=True)
+
+    @pl.when(step == 0)
+    def _():
+        vector_out[...] = jnp.zeros(vector_out.shape, F32)
+        vector_out[4:8] = sums[0:4]
+        for k in range(up_sums.shape[1] // width):
+            vector_out[8 + k : 9 + k] = up_sums[:, k * width : (k + 1) * width]
+        vector_out[2:3] = column_sums(dq[...])
+        padded[...] = jnp.zeros(padded.shape, F32)
+
+        @pl.when(me == 0)
+        def _():
+            incoming[1] = jnp.zeros(incoming.shape[1:], BF)
+
+        @pl.when(me == peers - 1)
+        def _():
+            incoming[0] = jnp.zeros(incoming.shape[1:], BF)
+
+        for col in range(0, width, ROW_TILE):
+            cols = pl.ds(col, ROW_TILE)
+            grads[0, cols, :] = dot(normed[pl.ds(RIM, rows), cols], dq[...], TN).astype(BF)
+
+    for which, part in ((1, dk), (2, dv)):
+        @pl.when(step == which)
+        def _():
+            for col in range(0, width, ROW_TILE):
+                cols = pl.ds(col, ROW_TILE)
+                total = None
+                for seg, base in enumerate(bases):
+                    term = dot(normed[pl.ds(base * 16, WIN), cols], part[seg], TN)
+                    total = term if total is None else total + term
+                grads[which, cols, :] = total.astype(BF)
+            if which == 2:
+                vector_out[3:4] = (
+                    column_sums(dv[0]) + column_sums(dv[1]) + column_sums(dv[2])
+                )
+
+    @pl.when(step == 3)
+    def _():
+        for seg in range(3):
+            padded[seg, wide] = dot(dk[seg], w_qkv[...], NT)
+
+    @pl.when(step == 4)
+    def _():
+        for seg in (0, 2, 1):
+            padded[seg, wide] += dot(dv[seg], w_qkv[...], NT)
+        outgoing[0] = padded[0, wide].astype(BF)
+        outgoing[1] = jnp.where(images.third, padded[2, wide], padded[1, wide]).astype(BF)
+        pl.when(me > 0)(lambda: halo(0).start())
+        pl.when(me < peers - 1)(lambda: halo(1).start())
+
+    @pl.when(step == 5)
+    def _():
+        @pl.when(me > 0)
+        def _():
+            halo(0).wait_send()
+            halo(1).wait_recv()
+
+        @pl.when(me < peers - 1)
+        def _():
+            halo(1).wait_send()
+            halo(0).wait_recv()
+
+        none = jnp.zeros((WIN, width), F32)
+        stop = jnp.where(images.third, images.spans[2][1], images.spans[1][1])
+        cut = (stop > RIM + rows) & (me < peers - 1)
+        after = jnp.where(cut, incoming[0].astype(F32), none)
+        padded[0, wide] += jnp.where(images.spans[0][0] < RIM, incoming[1].astype(F32), none)
+        padded[1, wide] += jnp.where(images.third, none, after)
+        padded[2, wide] += jnp.where(images.third, after, none)
+
+    @pl.when(step >= 5)
+    def _():
+        first = (step - 5) * ROW_TILE
+        upstream = dot(dq[pl.ds(first, ROW_TILE), :], w_qkv[...], NT)
+        places = []
+        for k in range(ROW_TILE // TILE):
+            total = upstream[k * TILE : (k + 1) * TILE]
+            for seg, base in enumerate(bases):
+                off = jnp.maximum(
+                    (RIM + TILE) // 16 + (step - 5) * (ROW_TILE // 16) + k * (TILE // 16) - base, 0
+                )
+                off = jnp.minimum(off, (WIN + TILE) // 16) * 16
+                total = total + padded[seg, pl.ds(off, TILE), :]
+            places.append(total)
+        upstream = jnp.concatenate(places, axis=0)
+        scaled, inv_std = row_stats(tokens[...].astype(F32))
+        through = upstream * vecs[0:1]
+        inner = (
+            through
+            - jnp.mean(through, axis=1, keepdims=True)
+            - scaled * jnp.mean(through * scaled, axis=1, keepdims=True)
+        )
+        out[...] = dresid[...] + inv_std * inner
+        vector_out[0:1] += jnp.sum(upstream * scaled, axis=0, keepdims=True)
+        vector_out[1:2] += jnp.sum(upstream, axis=0, keepdims=True)
+
+
+LAST_STEPS = 9
+
+
+def last_kernel(*refs):
+    step = pl.program_id(0)
+    me, peers = lax.axis_index(AXIS), lax.axis_size(AXIS)
+    ins, (out, vector_out, grads_out), scratch = refs[:11], refs[11:14], refs[14:]
+    grads, padded, outgoing, incoming, send, recv = scratch
+    pl.when(step == 0)(lambda: greet([], me > 0, me < peers - 1))
+    last_body(step, *ins, out, grads, padded, outgoing, incoming, send, recv, vector_out)
+
+    @pl.when(step == LAST_STEPS - 1)
+    def _():
+        grads_out[...] = grads[...]
+
+
+def last_scatter_kernel(*refs):
+    step = pl.program_id(0)
+    me, peers = lax.axis_index(AXIS), lax.axis_size(AXIS)
+    ins, (out, vector_out, reduced), scratch = refs[:11], refs[11:14], refs[14:]
+    grads, padded, outgoing, incoming, send, recv = scratch[:6]
+    vectors, arrived, vec_send, vec_recv = scratch[6:10]
+    comm = scratch[10:]
+    place = Place()
+    pl.when(step == 0)(lambda: greet(place.partners, me > 0, me < peers - 1))
+    pieces = [
+        Scatter(
+            place, grads.at[k], *comm[k * 8 : k * 8 + 5], reduced.at[:, pl.ds(k * UNIT, UNIT)],
+            comm[k * 8 + 5 : k * 8 + 8],
+        )
+        for k in range(3)
+    ]
+    run_stages(pieces, step, (1, 2, 3, 4, 5, 6))
+    last_body(
+        step, *ins, out, Flat(grads), padded, outgoing, incoming, send, recv, vectors.at[0]
+    )
+
+    @pl.when(step == LAST_STEPS - 1)
+    def _():
+        pieces[2].stage(4)
+        Total(place, vectors, arrived, vec_send, vec_recv).run()
+        vector_out[...] = vectors[5]
+
+
+class Flat:
+    def __init__(self, ref):
+        self.ref = ref
+
+    def __setitem__(self, index, value):
+        k, rows, _ = index
+        part = self.ref.shape[5]
+        count = rows.size // part
+        first = rows.start // part
+        for i in range(0, count, 8):
+            block = value[i * part : (i + 8) * part].reshape(2, 2, 2, part, value.shape[1])
+            self.ref[k, (first + i) // 8] = block
+
+
+def last(n0, normed, dq, dk, dv, w_qkv, tokens, dresid, vecs, sums, up_sums, plan):
+    rows, width = dq.shape
+    ext = normed.shape[0]
+    peers = lax.axis_size(AXIS)
+    const = lambda s: (0, 0)
+    once = lambda *shape: pl.BlockSpec(
+        shape, lambda s: (0,) * len(shape), pipeline_mode=pl.Buffered(1)
+    )
+    tile = pl.BlockSpec((ROW_TILE, width), lambda s: (jnp.maximum(s - 5, 0), 0))
+    third = lambda s: (0, jnp.where(s <= 3, 1, jnp.where(s == 4, 2, 0)))
+    vmem = pl.BlockSpec(memory_space=pltpu.VMEM)
+    in_specs = [
+        pl.BlockSpec(memory_space=pltpu.SMEM),
+        once(ext, width), once(rows, width), once(3, WIN, width), once(3, WIN, width),
+        pl.BlockSpec((width, width), third), tile, tile, once(8, width), once(8, width),
+        once(*up_sums.shape),
+    ]
+    vector_rows = 16
+    shared = [
+        pltpu.VMEM((3, WIN + 2 * TILE, width), F32),
+        pltpu.VMEM((2, WIN, width), BF),
+        pltpu.VMEM((2, WIN, width), BF),
+        pltpu.SemaphoreType.DMA((2,)),
+        pltpu.SemaphoreType.DMA((2,)),
+    ]
+    if plan:
+        part = width // peers
+        kernel, collective = last_scatter_kernel, 3
+        scratch = [pltpu.VMEM((3, 4, 2, 2, 2, part, width), BF)] + shared + [
+            pltpu.VMEM((6, vector_rows, width), F32),
+            pltpu.VMEM((5, vector_rows, width), F32),
+            pltpu.SemaphoreType.DMA((5,)),
+            pltpu.SemaphoreType.DMA((5,)),
+        ] + scatter_scratch(part, UNIT) * 3
+        third_out = jax.ShapeDtypeStruct((part, 3 * width), F32)
+    else:
+        kernel, collective = last_kernel, 4
+        scratch = [pltpu.VMEM((3, width, width), BF)] + shared
+        third_out = jax.ShapeDtypeStruct((3, width, width), BF)
+    return pl.pallas_call(
+        kernel,
+        grid=(LAST_STEPS,),
+        in_specs=in_specs,
+        out_specs=[tile, once(vector_rows, width), once(*third_out.shape)],
+        out_shape=[
+            jax.ShapeDtypeStruct((rows, width), F32),
+            jax.ShapeDtypeStruct((vector_rows, width), F32),
+            third_out,
+        ],
+        scratch_shapes=scratch,
+        compiler_params=pltpu.CompilerParams(
+            vmem_limit_bytes=61 * 2**20, collective_id=collective, has_side_effects=True
+        ),
+        name="last",
+    )(n0, normed, dq, dk, dv, w_qkv, tokens, dresid, vecs, sums, up_sums)
+
+
 def shifted(value, by):
     peers = lax.axis_size(AXIS)
     pairs = [(i, i + by) for i in range(peers) if 0 <= i + by < peers]
@@ -1006,16 +1165,6 @@
     inv_std = lax.rsqrt(jnp.mean(center * center, axis=1, keepdims=True) + EPS)
     scaled = center * inv_std
     return (scaled * gain + shift, scaled, inv_std)
-
-
-def normalize_back(upstream, scaled, inv_std, gain):
-    through = upstream * gain
-    inner = (
-        through
-        - jnp.mean(through, axis=1, keepdims=True)
-        - scaled * jnp.mean(through * scaled, axis=1, keepdims=True)
-    )
-    return (inv_std * inner, jnp.sum(upstream * scaled, axis=0), jnp.sum(upstream, axis=0))
 
 
 def local(
@@ -1064,10 +1213,8 @@
     high_rim = shifted(tokens[:RIM], -1)
     pad = jnp.zeros((ext - rows - 2 * RIM, width), BF)
     tokens_ext = jnp.concatenate([low_rim, tokens, high_rim, pad], axis=0).astype(F32)
-    inputs = tokens.astype(F32)
     normed_ext = normalize(tokens_ext, gain1, shift1)[0].astype(BF)
-    normed, scaled_one, inv_one = normalize(inputs, gain1, shift1)
-    normed_low = normed.astype(BF)
+    normed_low = normed_ext[RIM : RIM + rows]
     queries = (dot(normed_low, w_qkv[:, :width]) + q_bias).astype(BF)
     key_value = (
         dot(normed_ext, w_qkv[:, width:]) + jnp.concatenate([jnp.zeros_like(v_bias), v_bias])
@@ -1095,9 +1242,6 @@
     else:
         grad_up, up_sums, layer_out, dresid, dmixed_low, grad_out, sums = mlp_back(*args)
         r_down = scattered(grad_down).astype(F32)
-    grad_out_b, grad_gain_two, grad_shift_two, grad_down_b = sums[:4]
-    grad_up_b = up_sums[0]
-
     if block_plan:
         dquery, dkey, dvalue, r_out, r_up = attend_back(
             n0, queries, key_value, dmixed_low, lse, (grad_out, grad_up)
@@ -1105,40 +1249,18 @@
     else:
         dquery, dkey, dvalue = attend_back(n0, queries, key_value, dmixed_low, lse)
         r_out, r_up = (scattered(v).astype(F32) for v in (grad_out, grad_up))
-    dproj = (dquery, dkey, dvalue)
-    grad_qkv = [dot(normed_low, v, TN).astype(BF) for v in dproj]
-    grad_query_b = jnp.sum(dquery.astype(F32), axis=0)
-    grad_value_b = jnp.sum(dvalue.astype(F32), axis=0)
-    dnormed = sum(
-        dot(v, w_qkv[:, i * width : (i + 1) * width], NT) for i, v in enumerate(dproj)
+    vecs = jnp.concatenate([gain1[None], jnp.zeros((7, width), F32)])
+    grad_tokens, totals, r_qkv = last(
+        n0, normed_ext, dquery, dkey, dvalue, w_qkv, tokens, dresid, vecs, sums, up_sums,
+        block_plan,
     )
-    dinput_norm, grad_gain_one, grad_shift_one = normalize_back(
-        dnormed, scaled_one, inv_one, gain1
-    )
-    grad_tokens = dresid + dinput_norm
-
-    def small(value):
-        return value.reshape(peers, -1)
-
-    smalls = jnp.concatenate(
-        [
-            small(v)
-            for v in (
-                grad_gain_one, grad_shift_one, grad_query_b, grad_value_b, grad_out_b,
-                grad_gain_two, grad_shift_two, grad_down_b, grad_up_b,
-            )
-        ],
-        axis=1,
-    )
-    if block_plan:
-        count = smalls.shape[1]
-        smalls = jnp.pad(smalls, ((0, 0), (0, 16 * 128 - count))).reshape(peers * 16, 128)
-        r_qkv, owned = scatter_blocks(grad_qkv, smalls)
-        owned = owned.reshape(-1)[:count]
-    else:
-        owned = scattered(smalls)[0]
-        r_qkv = jnp.concatenate([scattered(v) for v in grad_qkv], axis=1).astype(F32)
-    g = [owned[i * part : (i + 1) * part] for i in range(8)] + [owned[8 * part :]]
+    if not block_plan:
+        totals = lax.psum(totals, AXIS)
+        r_qkv = jnp.concatenate([scattered(v) for v in r_qkv], axis=1).astype(F32)
+    owned = lax.dynamic_slice_in_dim(totals[:8], me * part, part, 1)
+    size = u_bias.shape[0] // peers
+    up_own = lax.dynamic_slice_in_dim(totals[8 : 8 + u_bias.shape[0] // width].reshape(-1), me * size, size)
+    g = [owned[i] for i in range(8)] + [up_own]
     return (
         layer_out, grad_tokens, g[0], g[1], r_qkv, g[2], g[3], r_out, g[4], g[5], g[6], r_up,
         g[8], r_down, g[7],

time: 535 us -> 496 us (0.927)
  matrix products: 54.2 us -> 15.8 us
    dot_general x8 -> x2, matrix products: 54.2 us -> 15.8 us  [dot(): return lax.dot_general(a, b, dims, preferred_element_type=F32)]
    pallas_call x2, Pallas kernels: 164 us -> 181 us  [the longest x1 113 us: last(): pl.pallas_call(kernel, grid=(LAST_STEPS,), in_specs=in_specs, out_specs=[...]
    pallas_call x1, Pallas kernels: 78.8 us -> 68.3 us  [attend(): pl.pallas_call(kernel, grid=(pairs,), in_specs=in_specs, out_specs=out_sp...]
    unnamed x72 -> x59, local copies, waits for them, and re-layouts: 12 us -> 11.7 us
  transfers between devices with their start and end apart: 2 -> 2, of which waited for: 0 -> 0; matrix products, arithmetic and copies ran while one was open for 2% -> 1% of each run, Pallas kernels for 12% -> 13%
where the time goes in v4:
time: 496 us; the launch traced here: 493 us
  Pallas kernels  440 us (89%)
  local copies, waits for them, and re-layouts  21.1 us (4%)
  matrix products  15.8 us (3%)
  other arithmetic  10.1 us (2%)
    pallas_call x1, Pallas kernels, last(): pl.pallas_call(kernel, grid=(LAST_STEPS,), in_specs=in_specs, out_specs=[...  113 us
    pallas_call x1, Pallas kernels, mlp_back(): pl.pallas_call(functools.partial(kernel, ff_steps), grid=(row_steps + ff_...  71.7 us
    pallas_call x1, Pallas kernels, attend(): pl.pallas_call(kernel, grid=(pairs,), in_specs=in_specs, out_specs=out_sp...  68.3 us
    pallas_call x1, Pallas kernels, attend_back(): pl.pallas_call(kernel, grid=(pairs,), in_specs=in_specs, out_specs=out_sp...  68.2 us
    pallas_call x1, Pallas kernels, gather_blocks(): pl.pallas_call(gather_kernel, out_shape=out, in_specs=[hbm, hbm], out_spe...  61.7 us
    pallas_call x1, Pallas kernels, mlp_up(): pl.pallas_call(functools.partial(kernel, row_steps), grid=(row_steps + ff...  57.2 us
    dot_general x2, matrix products, dot(): return lax.dot_general(a, b, dims, preferred_element_type=F32)  15.8 us
    unnamed x59, local copies, waits for them, and re-layouts  11.7 us
  transfers between devices with their start and end apart: 2, of which 0 were waited for; matrix products, arithmetic and copies ran while one was open for 1% of the time, Pallas kernels for 13%

profile of v4, /device:TPU:0, one launch (start us, length us, event | category | flops | bytes accessed | tf_op | source)
XLA Modules:
  0.0 493.1 jit_solution(13816681555205060279)
XLA Ops:
  0.8 3.4 fusion.14
  4.1 3.4 collective-permute-start
  7.5 1.3 collective-permute-start.1
  9.6 61.7 %gather_qkv.1 = (bf16[4,2,2,2,32,3072]{5,4,3,2,1,0:T(8,128)(2,1)}, bf16[4,2,2,2,32,128]{5,4,3,2,1,0:T(8,128)(2,1)}) custom-call(bf16[32,3072]{1,0:T(8,128)(2,1)} %wide.1, bf16[32,128]{1,0:T(8,128)(2,1)} %pad_bitcast_fusion.vec), custom_call_target="tpu_custom_call" | custom-call | tf_op jit(solution)/shard_map/gather_qkv/pallas_call | solution.py:301
  71.3 1.1 copy.35
  75.5 1.3 convert_reduce_fusion.1
  76.8 5.4 %convert_reduce_fusion = (f32[2304]{0:T(1024)S(1)}, bf16[2304,1024]{1,0:T(8,128)(2,1)S(1)}) fusion(bf16[2304]{0:T(1024)(128)(2,1)S(1)} %pad.10.clone, bf16[576,1024]{1,0:T(8,128)(2,1)} %collective-permute-done.1, bf16[1024,1024]{1,0:T(8,128)(2,1)S(1)} %copy-done.5, bf16[576,1024]{1,0:T(8,128)(2,1)} %collective-permute-done), kind=kLoop, calls=%fused_computation.2 | loop fusion | flops 23590656 | bytes 9188864 | tf_op jit(solution)/shard_map/reduce_sum | solution.py:1164
  82.2 1.4 fusion.2
  83.6 2.1 fusion.5.refs_1_
  85.8 12.1 %add_convert_fusion.k_ref.v_ref.refs_2_.refs_3_ = bf16[2304,2048]{1,0:T(8,128)(2,1)} fusion(bf16[2304,1024]{1,0:T(8,128)(2,1)S(1)} %fusion.5.refs_1_, f32[2048]{0:T(1024)S(1)} %concatenate.14, bf16[1024,3072]{1,0:T(8,128)(2,1)S(1)} %bitcast.49), kind=kOutput, calls=%fused_computation | convolution fusion | flops 9673113600 | bytes 18358272 | tf_op jit(solution)/shard_map/dot_general | solution.py:27
  97.9 3.7 add_convert_fusion.1.q_ref.refs_1_
  101.6 68.3 %attend.1 = (bf16[1024,1024]{1,0:T(8,128)(2,1)S(1)}, f32[8,8,256]{2,1,0:T(8,128)S(1)}, bf16[4,2,2,2,32,1024]{5,4,3,2,1,0:T(8,128)(2,1)S(1)}, bf16[4,2,2,2,32,4096]{5,4,3,2,1,0:T(8,128)(2,1)}) custom-call(s32[1]{0:T(128)} %bitcast.1.n0_ref.refs_0_, bf16[1024,1024]{1,0:T(8,128)(2,1)} %add_convert_fusion.1.q_ref.refs_1_, ...), custom_call_target="tpu_custom_call" | custom-call | tf_op jit(solution)/shard_map/attend/pallas_call | solution.py:485
  169.9 1.3 copy-done
  171.3 1.3 copy-done.1
  173.2 57.2 %mlp_up.1 = (f32[1024,1024]{1,0:T(8,128)}, bf16[1024,1024]{1,0:T(8,128)(2,1)}, bf16[1024,4096]{1,0:T(8,128)(2,1)}, bf16[1024,4096]{1,0:T(8,128)(2,1)}, bf16[4096...) custom-call(bf16[1024,1024]{1,0:T(8,128)(2,1)} %copy-done, bf16[1024,1024]{1,0:T(8,128)(2,1)} %refs_6_.3, ...), custom_call_target="tpu_custom_call" | custom-call | tf_op jit(solution)/shard_map/mlp_up/pallas_call | solution.py:741
  230.4 71.7 %mlp_back.1 = (bf16[1024,4096]{1,0:T(8,128)(2,1)}, f32[1,4096]{1,0:T(1,128)}, bf16[1024,1024]{1,0:T(8,128)(2,1)}, f32[1024,1024]{1,0:T(8,128)}, bf16[1024,1024]{...) custom-call(bf16[1024,4096]{1,0:T(8,128)(2,1)} %get-tuple-element.48.refs_0_, ...), custom_call_target="tpu_custom_call" | custom-call | tf_op jit(solution)/shard_map/mlp_back/pallas_call | solution.py:885
  302.1 68.2 %attend_back.1 = (bf16[1024,1024]{1,0:T(8,128)(2,1)}, bf16[3,592,1024]{2,1,0:T(8,128)(2,1)}, bf16[3,592,1024]{2,1,0:T(8,128)(2,1)}, f32[32,1024]{1,0:T(8,128)}, f32[32,4096]{1,0:T(8,128)}) custom-call(s32[1]{0:T(128)} %bitcast.1.n0_ref.refs_0_, bf16[1024,1024]{1,0:T(8,128)(2,1)} %add_convert_fusion.1.q_ref.refs_1_, ...), custom_call_target="tpu_custom_call" | custom-call | tf_op jit(solution)/shard_map/attend_back/pallas_call | solution.py:618
  370.4 113.0 %last.1 = (f32[1024,1024]{1,0:T(8,128)}, f32[16,1024]{1,0:T(8,128)}, f32[32,3072]{1,0:T(8,128)}) custom-call(s32[1]{0:T(128)} %bitcast.1.n0_ref.refs_0_, bf16[2304,1024]{1,0:T(8,128)(2,1)} %copy-done.6, bf16[1024,1024]{1,0:T(8,128)(2,1)} %get-tuple-element.59.refs_2_, bf16[3,592,1024]{2,1,0:T(8,128)(2,1)} %get-tuple-element.60.refs_3_, ...), custom_call_target="tpu_custom_call" | custom-call | tf_op jit(solution)/shard_map/last/pallas_call | solution.py:1131
  483.4 0.9 slice.94
  484.3 1.0 slice_bitcast_fusion
  486.5 1.3 copy.43
  487.9 2.0 copy.44
  491.3 0.8 copy.47
  492.1 0.8 copy.48
  (80 shorter events, 7.3 us)
Async XLA Ops:
  0.6 76.2 %copy-start.5 = (bf16[1024,1024]{1,0:T(8,128)(2,1)S(1)}, bf16[1024,1024]{1,0:T(8,128)(2,1)}, u32[]{:S(2)}) copy-start(bf16[1024,1024]{1,0:T(8,128)(2,1)} %refs_6_.3) | copy-start | bytes 6291460
  0.7 8.1 %copy-start.14 = (bf16[32]{0:T(256)(128)(2,1)S(1)}, bf16[32]{0:T(256)(128)(2,1)}, u32[]{:S(2)}) copy-start(bf16[32]{0:T(256)(128)(2,1)} %param.19) | copy-start | bytes 196
  0.7 8.1 %copy-start.15 = (bf16[32]{0:T(256)(128)(2,1)S(1)}, bf16[32]{0:T(256)(128)(2,1)}, u32[]{:S(2)}) copy-start(bf16[32]{0:T(256)(128)(2,1)} %param.20) | copy-start | bytes 196
  0.7 8.1 %copy-start.16 = (bf16[32]{0:T(256)(128)(2,1)S(1)}, bf16[32]{0:T(256)(128)(2,1)}, u32[]{:S(2)}) copy-start(bf16[32]{0:T(256)(128)(2,1)} %param.22) | copy-start | bytes 196
  0.7 8.1 %copy-start.17 = (bf16[32]{0:T(256)(128)(2,1)S(1)}, bf16[32]{0:T(256)(128)(2,1)}, u32[]{:S(2)}) copy-start(bf16[32]{0:T(256)(128)(2,1)} %param.23) | copy-start | bytes 196
  0.7 8.1 %copy-start.18 = (bf16[32]{0:T(256)(128)(2,1)S(1)}, bf16[32]{0:T(256)(128)(2,1)}, u32[]{:S(2)}) copy-start(bf16[32]{0:T(256)(128)(2,1)} %param.25) | copy-start | bytes 196
  0.7 8.1 %copy-start.19 = (bf16[32]{0:T(256)(128)(2,1)S(1)}, bf16[32]{0:T(256)(128)(2,1)}, u32[]{:S(2)}) copy-start(bf16[32]{0:T(256)(128)(2,1)} %param.26) | copy-start | bytes 196
  0.7 8.1 %copy-start.20 = (bf16[32]{0:T(256)(128)(2,1)S(1)}, bf16[32]{0:T(256)(128)(2,1)}, u32[]{:S(2)}) copy-start(bf16[32]{0:T(256)(128)(2,1)} %param.27) | copy-start | bytes 196
  0.7 8.1 %copy-start.22 = (bf16[128]{0:T(256)(128)(2,1)S(1)}, bf16[128]{0:T(256)(128)(2,1)}, u32[]{:S(2)}) copy-start(bf16[128]{0:T(256)(128)(2,1)} %param.29) | copy-start | bytes 772
  0.7 8.1 %copy-start.21 = (bf16[32]{0:T(256)(128)(2,1)S(1)}, bf16[32]{0:T(256)(128)(2,1)}, u32[]{:S(2)}) copy-start(bf16[32]{0:T(256)(128)(2,1)} %param.31) | copy-start | bytes 196
  0.8 72.6 %copy-start.13 = (s32[1024]{0:T(1024)S(1)}, s32[1024]{0:T(1024)}, u32[]{:S(2)}) copy-start(s32[1024]{0:T(1024)} %param.17) | copy-start | bytes 12292
  4.1 72.7 %collective-permute-start = (bf16[576,1024]{1,0:T(8,128)(2,1)}, bf16[576,1024]{1,0:T(8,128)(2,1)}, u32[]{:S(2)}, u32[]{:S(2)}) collective-permute-start(bf16[576,1024]{1,0:T(8,128)(2,1)} %get-tuple-element.73), channel_id=1, source_target_pairs={{0,1},{1,2},{2,3},{3,4},{4,5},{5,6},{6,7},{7,8},{8,9},{9,10},{10,1... | collective-permute-start | bytes 3538952 | tf_op jit(solution)/shard_map/ppermute | solution.py:1152
  7.5 69.3 %collective-permute-start.1 = (bf16[576,1024]{1,0:T(8,128)(2,1)}, bf16[576,1024]{1,0:T(8,128)(2,1)}, u32[]{:S(2)}, u32[]{:S(2)}) collective-permute-start(bf16[576,1024]{1,0:T(8,128)(2,1)} %get-tuple-element.74), channel_id=1, source_target_pairs={{1,0},{2,1},{3,2},{4,3},{5,4},{6,5},{7,6},{8,7},{9,8},{10,9},{11,1... | collective-permute-start | bytes 3538952 | tf_op jit(solution)/shard_map/ppermute | solution.py:1152
  82.2 3.5 slice-start
  83.6 2.1 slice-start.1
  85.7 12.2 %copy-start.6 = (bf16[2304,1024]{1,0:T(8,128)(2,1)}, bf16[2304,1024]{1,0:T(8,128)(2,1)S(1)}, u32[]{:S(2)}) copy-start(bf16[2304,1024]{1,0:T(8,128)(2,1)S(1)} %fusion.5.refs_1_) | copy-start | bytes 14155780
  97.9 3.7 copy-start.2
  97.9 3.7 copy-start.3
  370.4 116.1 %copy-start.8 = (bf16[1024,1024]{1,0:T(8,128)(2,1)S(1)}, bf16[1024,1024]{1,0:T(8,128)(2,1)}, u32[]{:S(2)}) copy-start(bf16[1024,1024]{1,0:T(8,128)(2,1)} %get-tuple-element.106) | copy-start | bytes 6291460
  483.4 4.4 copy-start.7
  487.8 2.0 copy-start.11
  487.8 2.8 copy-start.12
  487.8 3.4 copy-start.10
  487.8 4.2 copy-start.9
  (3 other events, 3.3 us)
